TPU v7x, 32 devices: a whole 2x2x4 slice. The times are simulated.
32 devices in a mesh: req: 8 (over y, x, core), head: 4 (over z).
Axes of the slice: x: 2, y: 2, z: 4, core: 2. Of those that a mesh axis runs over, the one named last changes fastest.
Arguments:
- tokens: bfloat16 [16384, 2048], P(('req', 'head')), may hold values from -6 to 6
- input_gain: float32 [2048], replicated, may hold values from 0.1 to 1.9
- w_query: bfloat16 [2048, 2048], replicated, may hold values from -0.125 to 0.125
- w_keyval: bfloat16 [2048, 1024], replicated, may hold values from -0.125 to 0.125
- query_gain: float32 [256], replicated, may hold values from 0.1 to 1.9
- key_gain: float32 [256], replicated, may hold values from 0.1 to 1.9
- w_output: bfloat16 [2048, 2048], P('req'), may hold values from -0.125 to 0.125
- laurel_left: bfloat16 [2048, 64], replicated, may hold values from -0.125 to 0.125
- laurel_right: bfloat16 [64, 2048], replicated, may hold values from -0.75 to 0.75
- laurel_gain: float32 [2048], replicated, may hold values from 0.1 to 1.9
- post_gain: float32 [2048], replicated, may hold values from 0.1 to 1.9
- cache_pool: bfloat16 [512, 64, 1024], P('req'), may hold values from -200 to 200, as said below
- page_table: int32 [32, 16], replicated, may hold values from 0 to 63, as said below
- cached_len: int32 [32], replicated, may hold values from 0 to 1024, as said below
- slot_of: int32 [32], replicated, may hold values from 0 to 31, as said below
Outputs:
- mixed: bfloat16 [16384, 2048], P(('req', 'head'))
Inputs may be any that keep to these rules, and one draw needn't show every extreme that they name: slot_of is a permutation of the 32 requests onto slots. Request i's pages lie in group i // 4. In each group exactly one request is served by the group before it and exactly one by the group after it (group indices cyclic over 8); all others are served by their own group. `page_table`: page p of request i holds its cached positions p*64 to (p+1)*64 - 1; the rows of the 4 requests of one group together name each of that group's 64 pages once. `cached_len`: at least one request that changes group has exactly 1024 cached positions, and some request has none. `cache_pool`: stored keys (already normalized and rotated) and values; entries past a request's cached length are arbitrary.
All inputs are finite; a program needn't handle non-finite values.
Results may differ from a plain program's by a relative error of at most 0.012.
The roundings to bfloat16 on the way count: a program that leaves them out, or rounds other values in their place, can miss the bound.
Values may be sent and summed in bfloat16 or wider, within the bound.
No kernel may reach another device: no remote copies, remote signals or barrier semaphores. Data moves between devices by JAX's collectives and lax.ppermute only.
A program may use at most 128 MiB of HBM per device.

v0:
```python
import math

import jax
import jax.numpy as jnp
from jax import lax
from jax.sharding import PartitionSpec as P

NH = 8
KVH = 2
HD = 256
REQ_DEV = 4
CH = 512
PAGE = 64
MAXP = 16


epsilon = 1e-06


def extended_2(block, sides, width):
    for axis, dim in sides:
        count = lax.axis_size(axis)
        forward = [(i, i + 1) for i in range(count - 1)]
        forward.append((count - 1, 0))
        backward = [(target, source) for source, target in forward]
        low = lax.ppermute(
            lax.slice_in_dim(block, block.shape[dim] - width, None, axis=dim), axis, forward
        )
        high = lax.ppermute(lax.slice_in_dim(block, 0, width, axis=dim), axis, backward)
        block = jnp.concatenate([low, block, high], axis=dim)
    return block


def normalize(values_in):
    return values_in * lax.rsqrt(jnp.mean(values_in * values_in, axis=-1, keepdims=True) + epsilon)


def rotate(values_in, position):
    half = values_in.shape[-1] // 2
    exponent = jnp.arange(half, dtype=jnp.float32) * (2.0 / values_in.shape[-1])
    inverse = jnp.power(jnp.float32(1000000.0), -exponent)
    angle = position.astype(jnp.float32)[:, None] * inverse[None, :]
    cosine = jnp.cos(angle)[:, None, :]
    sine = jnp.sin(angle)[:, None, :]
    first_half = values_in[..., :half]
    second_half = values_in[..., half:]
    return jnp.concatenate(
        [first_half * cosine - second_half * sine, second_half * cosine + first_half * sine],
        axis=-1,
    )


def shards(
    tokens,
    input_gain,
    w_query,
    w_keyval,
    query_gain,
    key_gain,
    w_output,
    laurel_left,
    laurel_right,
    laurel_gain,
    post_gain,
    cache_pool,
    page_table,
    cached_len,
    slot_of,
):
    group_count = lax.axis_size("req")
    head_count = lax.axis_size("head")
    group = lax.axis_index("req")
    member = lax.axis_index("head")
    tok_rows = tokens.shape[0]
    total_requests = slot_of.shape[0]
    group_rows = tok_rows * head_count
    per_device = NH // head_count
    per_kv = head_count // KVH
    query_width = per_device * HD
    inputs = tokens.astype(jnp.float32)
    normed = (normalize(inputs) * input_gain).astype(jnp.bfloat16)
    slots = jnp.arange(total_requests, dtype=jnp.int32)
    matches = slot_of[None, :] == slots[:, None]
    request_at = jnp.sum(jnp.where(matches, slots[None, :], 0), axis=1)
    token_rows = group * group_rows + member * tok_rows + jnp.arange(tok_rows, dtype=jnp.int32)
    starts = jnp.take(cached_len, jnp.take(request_at, token_rows // CH))
    position = starts + token_rows % CH
    query_raw = jnp.dot(normed, w_query, preferred_element_type=jnp.float32)
    keyval_raw = jnp.dot(normed, w_keyval, preferred_element_type=jnp.float32)
    query = rotate(normalize(query_raw.reshape(tok_rows, NH, HD)) * query_gain, position).astype(
        jnp.bfloat16
    )
    keyval = keyval_raw.reshape(tok_rows, KVH, 2, HD)
    key = rotate(normalize(keyval[:, :, 0]) * key_gain, position).astype(jnp.bfloat16)
    value = normalize(keyval[:, :, 1]).astype(jnp.bfloat16)
    packed_kv = jnp.concatenate([key, value], axis=-1)
    outgoing = jnp.concatenate(
        [query.reshape(tok_rows, head_count, query_width), jnp.repeat(packed_kv, per_kv, axis=1)],
        axis=-1,
    )
    incoming = lax.all_to_all(outgoing, "head", split_axis=1, concat_axis=0, tiled=True)[:, 0]
    queries_here = incoming[:, :query_width].reshape(group_rows, per_device, HD)
    fresh_keys = incoming[:, query_width : query_width + HD]
    fresh_values = incoming[:, query_width + HD :]
    low = jnp.dot(normed, laurel_left, preferred_element_type=jnp.float32).astype(jnp.bfloat16)
    laurel = (
        normed.astype(jnp.float32)
        + normalize(jnp.dot(low, laurel_right, preferred_element_type=jnp.float32)) * laurel_gain
    )
    kv_head = member * per_device // (NH // KVH)
    own_start = kv_head * 2 * HD

    def own_channels(block):
        return lax.dynamic_slice_in_dim(block, own_start, 2 * HD, block.ndim - 1)

    target = lax.dynamic_slice_in_dim(slot_of, group * REQ_DEV, REQ_DEV, 0) // REQ_DEV
    local_index = jnp.arange(REQ_DEV, dtype=jnp.int32)
    before = (group + group_count - 1) % group_count
    after = (group + 1) % group_count
    to_before = jnp.sum(jnp.where(target == before, local_index, 0))
    to_after = jnp.sum(jnp.where(target == after, local_index, 0))
    mover_pages = jnp.take(page_table, group * REQ_DEV + jnp.stack([to_before, to_after]), axis=0)
    outbound = jnp.take(cache_pool, mover_pages.reshape(-1), axis=0).reshape(
        2, MAXP, PAGE, 2 * KVH * HD
    )
    extended = extended_2(outbound, (("req", 0),), 1)
    arrived = own_channels(jnp.stack([extended[0], extended[3]]))
    arrived = arrived.reshape(2, MAXP * PAGE, 2 * HD)
    score_scale = HD ** (-0.5)
    cached_rows = MAXP * PAGE

    def one_slot(slot_index):
        request = jnp.take(request_at, group * REQ_DEV + slot_index)
        home_group = request // REQ_DEV
        length = jnp.take(cached_len, request)
        local_pages = jnp.take(page_table, request, axis=0)
        stayed = own_channels(jnp.take(cache_pool, local_pages, axis=0)).reshape(
            cached_rows, 2 * HD
        )
        stored = jnp.where(
            home_group == group, stayed, jnp.where(home_group == before, arrived[0], arrived[1])
        )
        begin = slot_index * CH
        block_queries = lax.dynamic_slice_in_dim(queries_here, begin, CH, 0)
        block_keys = lax.dynamic_slice_in_dim(fresh_keys, begin, CH, 0)
        block_values = lax.dynamic_slice_in_dim(fresh_values, begin, CH, 0)
        cached_scores = (
            jnp.einsum(
                "tnh,kh->ntk", block_queries, stored[:, :HD], preferred_element_type=jnp.float32
            )
            * score_scale
        )
        new_scores = (
            jnp.einsum("tnh,kh->ntk", block_queries, block_keys, preferred_element_type=jnp.float32)
            * score_scale
        )
        visible = (jnp.arange(cached_rows) < length)[None, None, :]
        causal = (jnp.arange(CH)[None, :] <= jnp.arange(CH)[:, None])[None]
        highest = jnp.maximum(
            jnp.max(jnp.where(visible, cached_scores, -jnp.inf), axis=-1),
            jnp.max(jnp.where(causal, new_scores, -jnp.inf), axis=-1),
        )[..., None]
        cached_exp = jnp.where(visible, jnp.exp(cached_scores - highest), 0.0)
        new_exp = jnp.where(causal, jnp.exp(new_scores - highest), 0.0)
        denominator = jnp.sum(cached_exp, axis=-1, keepdims=True) + jnp.sum(
            new_exp, axis=-1, keepdims=True
        )
        cached_weights = (cached_exp / denominator).astype(jnp.bfloat16)
        new_weights = (new_exp / denominator).astype(jnp.bfloat16)
        result = jnp.einsum(
            "ntk,kh->tnh", cached_weights, stored[:, HD:], preferred_element_type=jnp.float32
        )
        result = result + jnp.einsum(
            "ntk,kh->tnh", new_weights, block_values, preferred_element_type=jnp.float32
        )
        return result.astype(jnp.bfloat16).reshape(CH, query_width)

    attended = lax.map(one_slot, jnp.arange(REQ_DEV, dtype=jnp.int32)).reshape(
        group_rows, query_width
    )
    returned = lax.all_to_all(
        attended.reshape(head_count, tok_rows, query_width),
        "head",
        split_axis=0,
        concat_axis=2,
        tiled=True,
    )
    returned = returned.reshape(tok_rows, NH * HD)
    projected = jnp.dot(
        returned,
        lax.all_gather(w_output, "req", axis=0, tiled=True),
        preferred_element_type=jnp.float32,
    )
    attn = normalize(projected) * post_gain
    return ((attn + inputs + laurel) / math.sqrt(2.0)).astype(jnp.bfloat16)


def solution(mesh):
    in_specs = (
        P(("req", "head"), None),
        P(),
        P(),
        P(),
        P(),
        P(),
        P("req", None),
        P(),
        P(),
        P(),
        P(),
        P("req", None, None),
        P(),
        P(),
        P(),
    )
    out_specs = P(("req", "head"), None)
    return jax.shard_map(shards, mesh=mesh, in_specs=in_specs, out_specs=out_specs, check_vma=False)
```

profile of v0, /device:TPU:0, one launch (start us, length us, event | category | flops | bytes accessed | tf_op | source)
XLA Modules:
  0.0 362.0 jit_solution(4515196464969298434)
XLA Ops:
  8.8 2.1 fusion.53
  12.7 2.1 fusion.27
  14.8 7.7 %fusion.47 = f32[512,2048]{1,0:T(8,128)S(1)} fusion(bf16[2048,2048]{1,0:T(8,128)(2,1)} %param.21, bf16[512,2048]{1,0:T(8,128)(2,1)} %param.19, f32[2048]{0:T(1024)} %param.20, f32[512]{0:T(512)S(1)} %add_rsqrt_fusion.5), kind=kOutput, calls=%fused_computation.130 | convolution fusion | flops 4299161600 | bytes 14690304 | tf_op jit(solution)/shard_map/dot_general | solution.py:88
  22.4 2.0 copy.97
  24.4 1.9 copy-done.1
  27.2 40.0 %fusion.36 = f32[512]{0:T(512)S(1)} fusion(s32[]{:T(128)} %bitcast.89, s32[]{:T(128)} %bitcast.88, s32[]{:T(128)} %bitcast.87, s32[]{:T(128)} %bitcast.86, s32[]{:T(128)} %bitcast.85, s32[]{:T(128)} %bitcast.84, s32[]{:T(128)} %bitcast.83, s32[]{:T(128)} %bitcast.82, s32[]{:T(128)} %bitcast.81, s32[]{:T(128)} %bitcast.80, s32[]{:T(128)} %bitcast.79, ...), kind=kLoop, calls=%fused_computation.105 | loop fusion | flops 81920 | bytes 2308 | tf_op jit(solution)/shard_map/convert_element_type | solution.py:42
  68.2 2.6 multiply_multiply_fusion
  73.0 4.3 %copy.77 = bf16[512,8,256]{0,2,1:T(8,128)(2,1)} copy(bf16[512,8,256]{2,1,0:T(8,128)(2,1)} %pad_maximum_fusion.1) | data formatting | bytes 4194304 | tf_op jit(solution)/shard_map/concatenate | solution.py:47
  77.3 5.9 %fusion.45 = f32[512,1024]{1,0:T(8,128)} fusion(bf16[2048,1024]{1,0:T(8,128)(2,1)} %param.22, bf16[512,2048]{1,0:T(8,128)(2,1)S(1)} %copy-done.2, f32[2048]{0:T(1024)S(1)} %copy-done.8, f32[512]{0:T(512)S(1)} %add_rsqrt_fusion.5), kind=kOutput, calls=%fused_computation.129 | convolution fusion | flops 2151677952 | bytes 8398848 | tf_op jit(solution)/shard_map/dot_general | solution.py:89
  83.2 3.2 reshape.307
  91.6 1.8 pad_maximum_fusion.2
  93.4 2.4 copy.84
  96.0 2.2 pad_maximum_fusion
  98.3 6.5 %all-to-all-start = ((bf16[512,4,1024]{0,2,1:T(8,128)(2,1)}), bf16[512,4,1024]{0,2,1:T(8,128)(2,1)}, u32[]{:S(2)}, u32[]{:S(2)}) async-start(bf16[512,4,1024]{0,2,1:T(8,128)(2,1)} %pad_maximum_fusion), calls=%async_computation | async-start | bytes 8388608 | tf_op jit(solution)/shard_map/all_to_all | solution.py:101
  109.1 6.1 %gather_fusion.2 = bf16[32,64,1024]{2,1,0:T(8,128)(2,1)} fusion(bf16[64,64,1024]{2,1,0:T(8,128)(2,1)} %param.30, s32[1024]{0:T(1024)S(1)} %pad_clamp_fusion.1), kind=kCustom, calls=%fused_computation.2 | custom fusion | bytes 8388736 | tf_op jit(solution)/shard_map/jit(_take)/gather | solution.py:123
  115.2 2.6 broadcast_select_fusion.1
  117.9 2.4 slice_bitcast_fusion.4
  120.3 2.6 collective-permute-start.1
  123.0 68.6 %collective-permute-done = bf16[1,16,64,1024]{3,2,1,0:T(8,128)(2,1)S(1)} collective-permute-done((bf16[1,16,64,1024]{3,2,1,0:T(8,128)(2,1)}, bf16[1,16,64,1024]{3,2,1,0:T(8,128)(2,1)S(1)}, u32[]{:S(2)}, u32[]{:S(2)}) %collective-permute-start) | collective-permute-done | bytes 2097184 | tf_op jit(solution)/shard_map/ppermute | solution.py:26
  191.5 5.4 %collective-permute-done.1 = bf16[1,16,64,1024]{3,2,1,0:T(8,128)(2,1)} collective-permute-done((bf16[1,16,64,1024]{3,2,1,0:T(8,128)(2,1)}, bf16[1,16,64,1024]{3,2,1,0:T(8,128)(2,1)}, u32[]{:S(2)}, u32[]{:S(2)}) %collective-permute-start.1) | collective-permute-done | bytes 2097184 | tf_op jit(solution)/shard_map/ppermute | solution.py:29
  196.9 2.8 fusion.33
  199.8 5.5 %copy.85 = bf16[4,512,1,1024]{1,0,3,2:T(4,128)(2,1)S(1)} copy(bf16[4,512,1,1024]{1,3,0,2:T(8,128)(2,1)} %bitcast.95) | data formatting | bytes 8388608 | tf_op jit(solution)/shard_map/all_to_all | solution.py:101
  209.6 79.6 %while.15 = (s32[]{:T(128)}, bf16[4,512,512]{1,2,0:T(8,128)(2,1)}, s32[4]{0:T(128)S(1)}, s32[]{:T(128)}, s32[32]{0:T(128)S(1)}, /*index=5*/s32[]{:T(128)}, s32[3...) while((s32[]{:T(128)}, bf16[4,512,512]{1,2,0:T(8,128)(2,1)}, ...), condition=%wide.region_12.14_spmd, body=%wide.region_7.13_spmd.sunk | while | flops 1631846656 | bytes 36776420 | solution.py:178
  212.2 4.1 %gather_fusion = bf16[16,64,1024]{2,1,0:T(8,128)(2,1)S(1)} fusion(bf16[64,64,1024]{2,1,0:T(8,128)(2,1)} %get-tuple-element.590, s32[1024]{0:T(1024)S(1)} %pad_clamp_fusion.4), kind=kCustom, calls=%fused_computation.clone.1 | custom fusion | bytes 4194368 | tf_op jit(solution)/shard_map/while/body/eval_jaxpr/jit(_take)/gather | solution.py:137
  232.1 4.1 %gather_fusion = bf16[16,64,1024]{2,1,0:T(8,128)(2,1)S(1)} fusion(bf16[64,64,1024]{2,1,0:T(8,128)(2,1)} %get-tuple-element.590, s32[1024]{0:T(1024)S(1)} %pad_clamp_fusion.4), kind=kCustom, calls=%fused_computation.clone.1 | custom fusion | bytes 4194368 | tf_op jit(solution)/shard_map/while/body/eval_jaxpr/jit(_take)/gather | solution.py:137
  252.0 4.1 %gather_fusion = bf16[16,64,1024]{2,1,0:T(8,128)(2,1)S(1)} fusion(bf16[64,64,1024]{2,1,0:T(8,128)(2,1)} %get-tuple-element.590, s32[1024]{0:T(1024)S(1)} %pad_clamp_fusion.4), kind=kCustom, calls=%fused_computation.clone.1 | custom fusion | bytes 4194368 | tf_op jit(solution)/shard_map/while/body/eval_jaxpr/jit(_take)/gather | solution.py:137
  271.9 4.1 %gather_fusion = bf16[16,64,1024]{2,1,0:T(8,128)(2,1)S(1)} fusion(bf16[64,64,1024]{2,1,0:T(8,128)(2,1)} %get-tuple-element.590, s32[1024]{0:T(1024)S(1)} %pad_clamp_fusion.4), kind=kCustom, calls=%fused_computation.clone.1 | custom fusion | bytes 4194368 | tf_op jit(solution)/shard_map/while/body/eval_jaxpr/jit(_take)/gather | solution.py:137
  289.2 5.4 %all-to-all-start.1 = ((bf16[4,512,512]{1,2,0:T(8,128)(2,1)}), bf16[4,512,512]{1,2,0:T(8,128)(2,1)}, u32[]{:S(2)}, u32[]{:S(2)}) async-start(bf16[4,512,512]{1,2,0:T(8,128)(2,1)} %get-tuple-element.190), calls=%async_computation.1 | async-start | bytes 4194304 | tf_op jit(solution)/shard_map/all_to_all | solution.py:181
  294.6 3.5 multiply_reduce_fusion
  298.1 46.2 %all-to-all-done.1 = bf16[4,512,512]{1,2,0:T(8,128)(2,1)} async-done(((bf16[4,512,512]{1,2,0:T(8,128)(2,1)}), bf16[4,512,512]{1,2,0:T(8,128)(2,1)}, u32[]{:S(2)}, u32[]{:S(2)}) %all-to-all-start.1) | async-done | bytes 2097184 | tf_op jit(solution)/shard_map/all_to_all | solution.py:181
  344.2 7.9 %multiply_reduce_fusion.1 = (f32[512]{0:T(512)S(1)}, f32[512,2048]{1,0:T(8,128)S(1)}) fusion(bf16[512,2048]{0,1:T(8,128)(2,1)} %bitcast.99, bf16[2048,2048]{1,0:T(8,128)(2,1)} %all-gather.2.cloned.1.call-done), kind=kOutput, calls=%fused_computation.63 | convolution fusion | flops 4297063936 | bytes 14682112 | tf_op jit(solution)/shard_map/dot_general | solution.py:189
  352.2 3.0 fusion.32
  (150 shorter events, 74.2 us)
Async XLA Ops:
  6.5 288.0 %copy-start = (bf16[64,2048]{1,0:T(8,128)(2,1)S(1)}, bf16[64,2048]{1,0:T(8,128)(2,1)}, u32[]{:S(2)}) copy-start(bf16[64,2048]{1,0:T(8,128)(2,1)} %param.27) | copy-start | bytes 786436
  24.4 1.9 copy-start.1
  24.4 43.8 %copy-start.12 = (f32[256]{0:T(256)S(1)}, f32[256]{0:T(256)}, u32[]{:S(2)}) copy-start(f32[256]{0:T(256)} %param.23) | copy-start | bytes 3076
  71.4 5.9 %copy-start.2 = (bf16[512,2048]{1,0:T(8,128)(2,1)S(1)}, bf16[512,2048]{1,0:T(8,128)(2,1)}, u32[]{:S(2)}) copy-start(bf16[512,2048]{1,0:T(8,128)(2,1)} %param.19) | copy-start | bytes 6291460
  71.4 5.9 %copy-start.8 = (f32[2048]{0:T(1024)S(1)}, f32[2048]{0:T(1024)}, u32[]{:S(2)}) copy-start(f32[2048]{0:T(1024)} %param.20) | copy-start | bytes 24580
  86.4 3.0 copy-start.13
  91.5 4.5 %copy-start.5 = (bf16[512,8,256]{0,2,1:T(8,128)(2,1)S(1)}, bf16[512,8,256]{0,2,1:T(8,128)(2,1)}, u32[]{:S(2)}) copy-start(bf16[512,8,256]{0,2,1:T(8,128)(2,1)} %copy.77) | copy-start | bytes 6291460
  98.3 6.5 %copy-start.9 = (s32[32,16]{0,1:T(8,128)S(1)}, s32[32,16]{0,1:T(8,128)}, u32[]{:S(2)}) copy-start(s32[32,16]{0,1:T(8,128)} %param.31) | copy-start | bytes 6148
  98.3 6.5 %copy-start.14 = (s32[32]{0:T(128)S(1)}, s32[32]{0:T(128)}, u32[]{:S(2)}) copy-start(s32[32]{0:T(128)} %param.33) | copy-start | bytes 388
  98.3 101.5 %all-to-all-start = ((bf16[512,4,1024]{0,2,1:T(8,128)(2,1)}), bf16[512,4,1024]{0,2,1:T(8,128)(2,1)}, u32[]{:S(2)}, u32[]{:S(2)}) async-start(bf16[512,4,1024]{0,2,1:T(8,128)(2,1)} %pad_maximum_fusion), calls=%async_computation | async-start | bytes 8388608 | tf_op jit(solution)/shard_map/all_to_all | solution.py:101
  104.7 239.5 %all-gather.2.cloned.1.call-start = ((), (), s32[]{:S(2)}) async-start(), calls=%async_computation.2 | async-start | bytes 9437184 | tf_op jit(solution)/shard_map/all_gather | solution.py:191
  120.3 71.3 %collective-permute-start = (bf16[1,16,64,1024]{3,2,1,0:T(8,128)(2,1)}, bf16[1,16,64,1024]{3,2,1,0:T(8,128)(2,1)S(1)}, u32[]{:S(2)}, u32[]{:S(2)}) collective-permute-start(bf16[1,16,64,1024]{3,2,1,0:T(8,128)(2,1)} %get-tuple-element.355), channel_id=1, source_target_pairs={{0,4},{4,8},{8,12},{12,16},{16,20},{20,24},{24,28},{28,0},{1,5},{5... | collective-permute-start | bytes 6291464 | tf_op jit(solution)/shard_map/ppermute | solution.py:26
  120.3 76.7 %collective-permute-start.1 = (bf16[1,16,64,1024]{3,2,1,0:T(8,128)(2,1)}, bf16[1,16,64,1024]{3,2,1,0:T(8,128)(2,1)}, u32[]{:S(2)}, u32[]{:S(2)}) collective-permute-start(bf16[1,16,64,1024]{3,2,1,0:T(8,128)(2,1)} %get-tuple-element.354), channel_id=1, source_target_pairs={{4,0},{8,4},{12,8},{16,12},{20,16},{24,20},{28,24},{0,28},{5,1},{9... | collective-permute-start | bytes 6291464 | tf_op jit(solution)/shard_map/ppermute | solution.py:29
  206.6 3.0 copy-start.6
  289.2 5.4 %copy-start.3 = (bf16[512,2048]{1,0:T(8,128)(2,1)S(1)}, bf16[512,2048]{1,0:T(8,128)(2,1)}, u32[]{:S(2)}) copy-start(bf16[512,2048]{1,0:T(8,128)(2,1)} %param.19) | copy-start | bytes 6291460
  289.2 5.4 %copy-start.7 = (bf16[2048,64]{0,1:T(8,128)(2,1)S(1)}, bf16[2048,64]{0,1:T(8,128)(2,1)}, u32[]{:S(2)}) copy-start(bf16[2048,64]{0,1:T(8,128)(2,1)} %param.26) | copy-start | bytes 786436
  289.2 55.1 %all-to-all-start.1 = ((bf16[4,512,512]{1,2,0:T(8,128)(2,1)}), bf16[4,512,512]{1,2,0:T(8,128)(2,1)}, u32[]{:S(2)}, u32[]{:S(2)}) async-start(bf16[4,512,512]{1,2,0:T(8,128)(2,1)} %get-tuple-element.190), calls=%async_computation.1 | async-start | bytes 4194304 | tf_op jit(solution)/shard_map/all_to_all | solution.py:181
  344.2 7.9 %copy-start.4 = (f32[512,2048]{1,0:T(8,128)S(1)}, f32[512,2048]{1,0:T(8,128)}, u32[]{:S(2)}) copy-start(f32[512,2048]{1,0:T(8,128)} %get-tuple-element.427) | copy-start | bytes 12582916
  344.2 7.9 %copy-start.10 = (f32[2048]{0:T(1024)S(1)}, f32[2048]{0:T(1024)}, u32[]{:S(2)}) copy-start(f32[2048]{0:T(1024)} %param.28) | copy-start | bytes 24580
  344.2 7.9 %copy-start.11 = (f32[2048]{0:T(1024)S(1)}, f32[2048]{0:T(1024)}, u32[]{:S(2)}) copy-start(f32[2048]{0:T(1024)} %param.29) | copy-start | bytes 24580
Sparse Core Ops, SparseCore 0:
  123.0 81.7 all-gather.1
where the time goes:
time: 364 us; the launch traced here: 362 us
  waiting for transfers between devices  120 us (33%)
  other arithmetic  83.4 us (23%)
  local copies, waits for them, and re-layouts  67.5 us (19%)
  matrix products  51.6 us (14%)
  starting transfers between devices  14.5 us (4%)
  between operations  13.8 us (4%)
  loops' own time  11.2 us (3%)
    ppermute x1, waiting for transfers between devices, extended_2(): lax.ppermute(lax.slice_in_dim(block, block.shape[dim] - width, None, axis...  68.6 us
    all_to_all x1, waiting for transfers between devices, shards(): lax.all_to_all(attended.reshape(head_count, tok_rows, query_width), 'head...  46.2 us
    convert_element_type x1, other arithmetic, rotate(): angle = position.astype(jnp.float32)[:, None] * inverse[None, :]  40 us
    gather x4, local copies, waits for them, and re-layouts, one_slot(): jnp.take(cache_pool, local_pages, axis=0)  16.3 us
    another operation x1, loops' own time, shards(): lax.map(one_slot, jnp.arange(REQ_DEV, dtype=jnp.int32))  11.2 us
    dot_general x1, matrix products, shards(): jnp.dot(returned, lax.all_gather(w_output, 'req', axis=0, tiled=True), pr...  7.9 us
    dot_general x1, matrix products, shards(): query_raw = jnp.dot(normed, w_query, preferred_element_type=jnp.float32)  7.67 us
    dot_general x4, matrix products, one_slot(): jnp.einsum('ntk,kh->tnh', new_weights, block_values, preferred_element_ty...  7.35 us
  transfers between devices with their start and end apart: 5, of which 3 were waited for; matrix products, arithmetic and copies ran while one was open for 28% of the time, Pallas kernels for 0%

commit v1 on v0

v1 whole, which is shorter than its diff:
```python
import functools
import math

import jax
import jax.numpy as jnp
import numpy as np
from jax import lax
from jax.experimental import pallas as pl
from jax.experimental.pallas import tpu as pltpu
from jax.sharding import PartitionSpec as P

NH = 8
KVH = 2
HD = 256
REQ_DEV = 4
CH = 512
EPS = 1e-06
LOG2E = 1.4426950408889634
MASKED = -1e30
VMEM_BYTES = 56 * 1024 * 1024

ANY = pl.BlockSpec(memory_space=pl.ANY)
SMEM = pl.BlockSpec(memory_space=pltpu.SMEM)
VMEM = pl.BlockSpec(memory_space=pltpu.VMEM)


def params(**more):
    return pltpu.CompilerParams(vmem_limit_bytes=VMEM_BYTES, **more)


def rope_table(rows):
    half = HD // 2
    inverse = 1000000.0 ** (-2.0 * np.arange(half) / HD)
    angle = np.arange(rows)[:, None] * inverse[None, :]
    return np.concatenate([np.cos(angle), np.sin(angle)], axis=1).astype(np.float32)


def normalize(values):
    return values * lax.rsqrt(jnp.mean(values * values, axis=-1, keepdims=True) + EPS)


def request_of(slot_of, slot):
    return lax.fori_loop(
        0,
        slot_of.shape[0],
        lambda i, found: jnp.where(slot_of[i] == slot, i, found),
        jnp.int32(0),
    )


def mover_to(slot_of, group, target):
    def step(i, found):
        request = group * REQ_DEV + i
        return jnp.where(slot_of[request] // REQ_DEV == target, request, found)

    return lax.fori_loop(0, REQ_DEV, step, jnp.int32(0))


def pages_kernel(me, slot_of, page_table, pool, near, far, sems):
    group, member = me[0], me[1]
    to_near = mover_to(slot_of, group, me[2])
    to_far = mover_to(slot_of, group, me[3])
    count, part = near.shape[0], far.shape[0]
    copies = []
    for p in range(part):
        page = page_table[to_far, (member % 2) * part + p]
        copies.append(pltpu.make_async_copy(pool.at[page], far.at[p], sems.at[p]))
    for p in range(count):
        page = page_table[to_near, p]
        copies.append(pltpu.make_async_copy(pool.at[page], near.at[p], sems.at[part + p]))
    for copy in copies:
        copy.start()
    for copy in copies:
        copy.wait()


def qkv_kernel(
    me, slot_of, cached_len, tokens, gain, w_query, w_keyval, query_gain, key_gain, table,
    query, key, value, normed, cosine, sine,
):
    step = pl.program_id(0)
    rows = tokens.shape[0]
    per_step = w_query.shape[1] // HD
    query_steps = NH // per_step

    @pl.when(step == 0)
    def _():
        request = request_of(slot_of, me[4])
        start = cached_len[request] + me[5]
        base = table[pl.ds(start, 1), :]
        half = HD // 2
        cos_base, sin_base = base[:, :half], base[:, half:]
        cos_row, sin_row = table[:rows, :half], table[:rows, half:]
        cosine[...] = cos_base * cos_row - sin_base * sin_row
        sine[...] = sin_base * cos_row + cos_base * sin_row
        tile = 64

        def norm_rows(i, _):
            at = pl.ds(pl.multiple_of(i * tile, tile), tile)
            inputs = tokens[at, :].astype(jnp.float32)
            normed[at, :] = (normalize(inputs) * gain[...]).astype(jnp.bfloat16)
            return 0

        lax.fori_loop(0, rows // tile, norm_rows, 0)

    def rotated(raw, head_gain):
        half = HD // 2
        v = normalize(raw) * head_gain[...]
        a, b = v[:, :half], v[:, half:]
        c, s = cosine[...], sine[...]
        return jnp.concatenate([a * c - b * s, b * c + a * s], axis=1).astype(jnp.bfloat16)

    @pl.when(step < query_steps)
    def _():
        for h in range(per_step):
            raw = jnp.dot(
                normed[...], w_query[:, h * HD : (h + 1) * HD], preferred_element_type=jnp.float32
            )
            query[h] = rotated(raw, query_gain)

    @pl.when(step >= query_steps)
    def _():
        raw = jnp.dot(normed[...], w_keyval[:, :HD], preferred_element_type=jnp.float32)
        key[0] = rotated(raw, key_gain)
        raw = jnp.dot(normed[...], w_keyval[:, HD:], preferred_element_type=jnp.float32)
        value[0] = normalize(raw).astype(jnp.bfloat16)


def residual_kernel(tokens, gain, left, right, laurel_gain, out):
    tile = 128
    rows = tokens.shape[0]
    for i in range(rows // tile):
        at = slice(i * tile, (i + 1) * tile)
        inputs = tokens[at, :].astype(jnp.float32)
        normed = (normalize(inputs) * gain[...]).astype(jnp.bfloat16)
        low = jnp.dot(normed, left[...], preferred_element_type=jnp.float32).astype(jnp.bfloat16)
        up = jnp.dot(low, right[...], preferred_element_type=jnp.float32)
        laurel = normed.astype(jnp.float32) + normalize(up) * laurel_gain[...]
        out[at, :] = inputs + laurel


def attention_kernel(
    me, slot_of, cached_len, page_table, query, key, value, pool, near, far_own, far_other,
    out, stored, sems,
):
    kv = pl.program_id(0)
    group, member = me[0], me[1]
    slot = me[4]
    request = request_of(slot_of, slot)
    length = cached_len[request]
    home = request // REQ_DEV
    page_count, page_rows = near.shape[0], near.shape[1]
    cached_rows = page_count * page_rows
    part = page_count // 2
    width = 2 * HD

    @pl.when(kv == 0)
    def _():
        def fetch(source_of):
            for p in range(page_count):
                source = source_of(p)
                for g in range(KVH):
                    pltpu.make_async_copy(
                        source.at[:, g * width : (g + 1) * width],
                        stored.at[g, p * page_rows : (p + 1) * page_rows],
                        sems.at[g, p],
                    ).start()

        @pl.when(home == group)
        def _():
            fetch(lambda p: pool.at[page_table[request, p]])

        @pl.when(home == me[2])
        def _():
            fetch(lambda p: near.at[p])

        @pl.when(home == me[3])
        def _():
            @pl.when(member % 2 == 0)
            def _():
                fetch(lambda p: far_own.at[p] if p < part else far_other.at[p - part])

            @pl.when(member % 2 == 1)
            def _():
                fetch(lambda p: far_other.at[p] if p < part else far_own.at[p - part])

    for p in range(page_count):
        pltpu.make_async_copy(
            near.at[p, :, :width],
            stored.at[kv, p * page_rows : (p + 1) * page_rows],
            sems.at[kv, p],
        ).wait()

    scale = HD ** (-0.5) * LOG2E
    heads, rows = query.shape[0], query.shape[1]
    fresh = key.shape[1]
    tile = 256
    at_key = lax.broadcasted_iota(jnp.int32, (1, cached_rows), 1)
    bias = jnp.where(at_key < length, 0.0, MASKED)
    contract = (((1,), (1,)), ((), ()))

    def one_head(h, _):
        for t in range(rows // tile):
            q = query[h, t * tile : (t + 1) * tile]
            old = lax.dot_general(
                q, stored[kv, :, :HD], contract, preferred_element_type=jnp.float32
            ) * scale + bias
            seen = fresh if fresh > rows else (t + 1) * tile
            new = lax.dot_general(
                q, key[0, :seen], contract, preferred_element_type=jnp.float32
            ) * scale
            row = me[5] + t * tile + lax.broadcasted_iota(jnp.int32, (tile, seen), 0)
            column = lax.broadcasted_iota(jnp.int32, (tile, seen), 1)
            new = jnp.where(column <= row, new, MASKED)
            highest = jnp.maximum(
                jnp.max(old, axis=1, keepdims=True), jnp.max(new, axis=1, keepdims=True)
            )
            old = jnp.exp2(old - highest)
            new = jnp.exp2(new - highest)
            total = jnp.sum(old, axis=1, keepdims=True) + jnp.sum(new, axis=1, keepdims=True)
            result = jnp.dot(
                old.astype(jnp.bfloat16), stored[kv, :, HD:], preferred_element_type=jnp.float32
            ) + jnp.dot(
                new.astype(jnp.bfloat16), value[0, :seen], preferred_element_type=jnp.float32
            )
            out[h, t * tile : (t + 1) * tile] = (result / total).astype(jnp.bfloat16)
        return 0

    lax.fori_loop(0, heads, one_head, 0)


def output_kernel(count, me, attended, residual, post_gain, *rest):
    weights, out = rest[:count], rest[count]
    held, total, sems = rest[count + 1 :]
    copies = [pltpu.make_async_copy(weights[i], held.at[i], sems.at[i]) for i in range(count)]
    for copy in copies:
        copy.start()
    rows = attended.shape[1]
    depth = held.shape[1]
    per_head = HD // depth
    tile = 256
    for i in range(count):
        copies[i].wait()
        block = me[0] ^ i
        head, part = block // per_head, block % per_head
        for t in range(rows // tile):
            at = slice(t * tile, (t + 1) * tile)
            if per_head == 1:
                lhs = attended[head, at]
            else:
                lhs = attended[head, at, pl.ds(pl.multiple_of(part * depth, depth), depth)]
            product = jnp.dot(lhs, held[i], preferred_element_type=jnp.float32)
            if i == 0:
                total[at] = product
            elif i < count - 1:
                total[at] += product
            else:
                projected = total[at] + product
                attn = normalize(projected) * post_gain[...]
                out[at] = ((attn + residual[at]) * (1.0 / math.sqrt(2.0))).astype(jnp.bfloat16)


def shards(
    tokens, input_gain, w_query, w_keyval, query_gain, key_gain, w_output, laurel_left,
    laurel_right, laurel_gain, post_gain, cache_pool, page_table, cached_len, slot_of,
):
    groups = lax.axis_size("req")
    members = lax.axis_size("head")
    group = lax.axis_index("req")
    member = lax.axis_index("head")
    rows, width = tokens.shape
    page_count = page_table.shape[1]
    page_rows = cache_pool.shape[1]
    channels = cache_pool.shape[2]
    share = CH // rows

    near_pairs = [(i, i ^ 1) for i in range(groups)]
    far_pairs = [(i, (i + 1) % groups if i % 2 else (i - 1) % groups) for i in range(groups)]
    far_group = jnp.where(group % 2 == 1, group + 1, group + groups - 1) % groups
    me = jnp.stack(
        [
            group,
            member,
            group ^ 1,
            far_group,
            group * REQ_DEV + member // share,
            member % share * rows,
        ]
    ).astype(jnp.int32)

    part = page_count // 2
    page_shape = (page_rows, channels)
    near_out, far_out = pl.pallas_call(
        pages_kernel,
        out_shape=(
            jax.ShapeDtypeStruct((page_count,) + page_shape, jnp.bfloat16),
            jax.ShapeDtypeStruct((part,) + page_shape, jnp.bfloat16),
        ),
        in_specs=[SMEM, SMEM, SMEM, ANY],
        out_specs=(ANY, ANY),
        scratch_shapes=[pltpu.SemaphoreType.DMA((page_count + part,))],
        compiler_params=params(),
        name="pages",
    )(me, slot_of, page_table, cache_pool)
    far_own = lax.ppermute(far_out, "req", far_pairs)
    near = lax.ppermute(near_out, "req", near_pairs)
    far_other = lax.ppermute(far_own, "head", [(i, i ^ 1) for i in range(members)])

    blocks = {0: w_output}
    for k in range(2, groups, 2):
        blocks[k] = lax.ppermute(w_output, "req", [(i, i ^ k) for i in range(groups)])
    for k in range(0, groups, 2):
        blocks[k + 1] = lax.ppermute(blocks[k], "req", near_pairs)

    gain = input_gain.reshape(1, width)
    table = rope_table(page_count * page_rows + CH)
    per_step = 2
    query_steps = NH // per_step
    whole = lambda shape: pl.BlockSpec(shape, lambda j: (0,) * len(shape))
    query, key, value = pl.pallas_call(
        qkv_kernel,
        grid=(query_steps + KVH,),
        out_shape=(
            jax.ShapeDtypeStruct((NH, rows, HD), jnp.bfloat16),
            jax.ShapeDtypeStruct((KVH, rows, HD), jnp.bfloat16),
            jax.ShapeDtypeStruct((KVH, rows, HD), jnp.bfloat16),
        ),
        in_specs=[
            SMEM,
            SMEM,
            SMEM,
            whole((rows, width)),
            whole((1, width)),
            pl.BlockSpec((width, per_step * HD), lambda j: (0, jnp.minimum(j, query_steps - 1))),
            pl.BlockSpec((width, 2 * HD), lambda j: (0, jnp.maximum(j - query_steps, 0))),
            whole((1, HD)),
            whole((1, HD)),
            whole(table.shape),
        ],
        out_specs=(
            pl.BlockSpec((per_step, rows, HD), lambda j: (jnp.minimum(j, query_steps - 1), 0, 0)),
            pl.BlockSpec((1, rows, HD), lambda j: (jnp.maximum(j - query_steps, 0), 0, 0)),
            pl.BlockSpec((1, rows, HD), lambda j: (jnp.maximum(j - query_steps, 0), 0, 0)),
        ),
        scratch_shapes=[
            pltpu.VMEM((rows, width), jnp.bfloat16),
            pltpu.VMEM((rows, HD // 2), jnp.float32),
            pltpu.VMEM((rows, HD // 2), jnp.float32),
        ],
        compiler_params=params(),
        cost_estimate=pl.CostEstimate(
            flops=2 * rows * width * 3072, bytes_accessed=20 << 20, transcendentals=0
        ),
        name="qkv",
    )(
        me, slot_of, cached_len, tokens, gain, w_query, w_keyval,
        query_gain.reshape(1, HD), key_gain.reshape(1, HD), table,
    )

    residual = pl.pallas_call(
        residual_kernel,
        out_shape=jax.ShapeDtypeStruct((rows, width), jnp.float32),
        in_specs=[VMEM] * 5,
        out_specs=VMEM,
        compiler_params=params(),
        cost_estimate=pl.CostEstimate(
            flops=4 * rows * width * 64, bytes_accessed=6 << 20, transcendentals=0
        ),
        name="residual",
    )(tokens, gain, laurel_left, laurel_right, laurel_gain.reshape(1, width))

    if share > 1:
        team = [list(range(m, m + share)) for m in range(0, members, share)]
        both = lax.all_gather(
            jnp.concatenate([key, value], axis=2), "head", axis=1, tiled=True,
            axis_index_groups=team,
        )
        key, value = both[:, :, :HD], both[:, :, HD:]

    per_kv = NH // KVH
    attended = pl.pallas_call(
        attention_kernel,
        grid=(KVH,),
        out_shape=jax.ShapeDtypeStruct((NH, rows, HD), jnp.bfloat16),
        in_specs=[
            SMEM,
            SMEM,
            SMEM,
            SMEM,
            pl.BlockSpec((per_kv, rows, HD), lambda j: (j, 0, 0)),
            pl.BlockSpec((1, CH, HD), lambda j: (j, 0, 0)),
            pl.BlockSpec((1, CH, HD), lambda j: (j, 0, 0)),
            ANY,
            ANY,
            ANY,
            ANY,
        ],
        out_specs=pl.BlockSpec((per_kv, rows, HD), lambda j: (j, 0, 0)),
        scratch_shapes=[
            pltpu.VMEM((KVH, page_count * page_rows, 2 * HD), jnp.bfloat16),
            pltpu.SemaphoreType.DMA((KVH, page_count)),
        ],
        compiler_params=params(),
        cost_estimate=pl.CostEstimate(
            flops=4 * NH * rows * 1536 * HD, bytes_accessed=8 << 20,
            transcendentals=NH * rows * 1536,
        ),
        name="attention",
    )(
        me, slot_of, cached_len, page_table, query, key, value, cache_pool,
        near, far_own, far_other,
    )

    depth = w_output.shape[0]
    return pl.pallas_call(
        functools.partial(output_kernel, groups),
        out_shape=jax.ShapeDtypeStruct((rows, width), jnp.bfloat16),
        in_specs=[SMEM, VMEM, VMEM, VMEM] + [ANY] * groups,
        out_specs=VMEM,
        scratch_shapes=[
            pltpu.VMEM((groups, depth, width), jnp.bfloat16),
            pltpu.VMEM((rows, width), jnp.float32),
            pltpu.SemaphoreType.DMA((groups,)),
        ],
        compiler_params=params(),
        cost_estimate=pl.CostEstimate(
            flops=2 * rows * width * width, bytes_accessed=16 << 20, transcendentals=0
        ),
        name="project",
    )(me, attended, residual, post_gain.reshape(1, width), *[blocks[k] for k in range(groups)])


def solution(mesh):
    in_specs = (
        P(("req", "head"), None),
        P(),
        P(),
        P(),
        P(),
        P(),
        P("req", None),
        P(),
        P(),
        P(),
        P(),
        P("req", None, None),
        P(),
        P(),
        P(),
    )
    out_specs = P(("req", "head"), None)
    return jax.shard_map(shards, mesh=mesh, in_specs=in_specs, out_specs=out_specs, check_vma=False)
```

time: 364 us -> 223 us (0.61)
  Pallas kernels: 0 us -> 152 us
  other arithmetic: 83.4 us -> 0 us
  waiting for transfers between devices: 120 us -> 54.3 us
  local copies, waits for them, and re-layouts: 67.5 us -> 5.11 us
  matrix products: 51.6 us -> 0 us
  between operations: 13.8 us -> 0.28 us
  loops' own time: 11.2 us -> 0 us
    pallas_call x0 -> x5, Pallas kernels: none -> 152 us  [the longest x1 97.8 us: shards(): pl.pallas_call(pages_kernel, out_shape=(jax.ShapeDtypeStruct((page_count,...]
    dot_general x20 -> x0, matrix products: 51.6 us -> none  [the longest x1 7.9 us: shards(): jnp.dot(returned, lax.all_gather(w_output, 'req', axis=0, tiled=True), pr...]
    all_to_all x2 -> x0, waiting for transfers between devices: 46.2 us -> none  [the longest x1 46.2 us: shards(): lax.all_to_all(attended.reshape(head_count, tok_rows, query_width), 'head...]
    convert_element_type x3 -> x0, other arithmetic: 44.5 us -> none  [the longest x1 40 us: rotate(): angle = position.astype(jnp.float32)[:, None] * inverse[None, :]]
    gather x10 -> x0, local copies, waits for them, and re-layouts: 28.3 us -> none  [the longest x4 16.3 us: one_slot(): jnp.take(cache_pool, local_pages, axis=0)]
    ppermute x2 -> x10, waiting for transfers between devices: 74 us -> 54.3 us  [the longest x3 33.9 us: shards(): lax.ppermute(w_output, 'req', [(i, i ^ k) for i in range(groups)])]
    select_n x16 -> x0, other arithmetic: 12.8 us -> none  [the longest x4 7.06 us: one_slot(): jnp.where(home_group == group, stayed, jnp.where(home_group == before, ar...]
    all_to_all x2 -> x0, starting transfers between devices: 11.8 us -> none  [the longest x1 6.46 us: shards(): lax.all_to_all(outgoing, 'head', split_axis=1, concat_axis=0, tiled=True)]
  transfers between devices with their start and end apart: 5 -> 10, of which waited for: 3 -> 3; matrix products, arithmetic and copies ran while one was open for 28% -> 0% of each run, Pallas kernels for 0% -> 19%
where the time goes in v1:
time: 223 us; the launch traced here: 222 us
  Pallas kernels  152 us (68%)
  waiting for transfers between devices  54.3 us (24%)
  starting transfers between devices  11.1 us (5%)
  local copies, waits for them, and re-layouts  5.11 us (2%)
    pallas_call x1, Pallas kernels, shards(): pl.pallas_call(pages_kernel, out_shape=(jax.ShapeDtypeStruct((page_count,...  97.8 us
    ppermute x3, waiting for transfers between devices, shards(): lax.ppermute(w_output, 'req', [(i, i ^ k) for i in range(groups)])  33.9 us
    ppermute x1, waiting for transfers between devices, shards(): far_own = lax.ppermute(far_out, 'req', far_pairs)  20.4 us
    pallas_call x1, Pallas kernels, shards(): pl.pallas_call(attention_kernel, grid=(KVH,), out_shape=jax.ShapeDtypeStr...  19.5 us
    pallas_call x1, Pallas kernels, shards(): pl.pallas_call(qkv_kernel, grid=(query_steps + KVH,), out_shape=(jax.Shap...  15.4 us
    pallas_call x1, Pallas kernels, shards(): pl.pallas_call(functools.partial(output_kernel, groups), out_shape=jax.Sh...  12.2 us
    pallas_call x1, Pallas kernels, shards(): pl.pallas_call(residual_kernel, out_shape=jax.ShapeDtypeStruct((rows, wid...  6.56 us
  transfers between devices with their start and end apart: 10, of which 3 were waited for; matrix products, arithmetic and copies ran while one was open for 0% of the time, Pallas kernels for 19%

profile of v1, /device:TPU:0, one launch (start us, length us, event | category | flops | bytes accessed | tf_op | source)
XLA Modules:
  0.0 222.2 jit_solution(12704374641868588018)
XLA Ops:
  0.0 1.4 copy.18.page_table
  1.4 0.7 stack.24.me
  2.1 97.8 %pages.1 = (bf16[16,64,1024]{2,1,0:T(8,128)(2,1)}, bf16[8,64,1024]{2,1,0:T(8,128)(2,1)}) custom-call(s32[6]{0:T(128)} %stack.24.me, s32[32]{0:T(128)} %slot_of.5, s32[32,16]{1,0:T(8,128)} %copy.18.page_table, bf16[64,64,1024]{2,1,0:T(8,128)(2,1)} %pool.3), custom_call_target="tpu_custom_call" | custom-call | tf_op jit(solution)/shard_map/pages/pallas_call | solution.py:293
  99.9 3.4 %collective-permute-start.1 = (bf16[8,64,1024]{2,1,0:T(8,128)(2,1)}, bf16[8,64,1024]{2,1,0:T(8,128)(2,1)}, u32[]{:S(2)}, u32[]{:S(2)}) collective-permute-start(bf16[8,64,1024]{2,1,0:T(8,128)(2,1)} %get-tuple-element.14), channel_id=1, source_target_pairs={{0,28},{4,8},{8,4},{12,16},{16,12},{20,24},{24,20},{28,0},{1,29},{... | collective-permute-start | bytes 3145736 | tf_op jit(solution)/shard_map/ppermute | solution.py:305
  103.3 0.0 collective-permute-start
  103.3 1.2 collective-permute-start.4
  104.5 0.1 collective-permute-start.6
  104.6 2.2 collective-permute-start.8
  106.8 20.4 %collective-permute-done.1.far_own = bf16[8,64,1024]{2,1,0:T(8,128)(2,1)} collective-permute-done((bf16[8,64,1024]{2,1,0:T(8,128)(2,1)}, bf16[8,64,1024]{2,1,0:T(8,128)(2,1)}, u32[]{:S(2)}, u32[]{:S(2)}) %collective-permute-start.1) | collective-permute-done | bytes 1048608 | tf_op jit(solution)/shard_map/ppermute | solution.py:305
  127.1 2.4 %collective-permute-start.2 = (bf16[8,64,1024]{2,1,0:T(8,128)(2,1)}, bf16[8,64,1024]{2,1,0:T(8,128)(2,1)}, u32[]{:S(2)}, u32[]{:S(2)}) collective-permute-start(bf16[8,64,1024]{2,1,0:T(8,128)(2,1)} %collective-permute-done.1.far_own), channel_id=1, source_target_pairs={{0,1},{1,0},{2,3},{3,2},{4,5},{5,4},{6,7},{7,6},{8,9},{9,8},{10,11... | collective-permute-start | bytes 3145736 | tf_op jit(solution)/shard_map/ppermute | solution.py:307
  129.5 1.0 copy.19.left
  130.5 6.6 %residual.1 = f32[512,2048]{1,0:T(8,128)} custom-call(bf16[512,2048]{1,0:T(8,128)(2,1)} %tokens.3, f32[1,2048]{1,0:T(1,128)} %bitcast.11, bf16[2048,64]{1,0:T(8,128)(2,1)} %copy.19.left, bf16[64,2048]{1,0:T(8,128)(2,1)} %right.1, f32[1,2048]{1,0:T(1,128)} %bitcast.10), custom_call_target="tpu_custom_call" | custom-call | flops 268435456 | bytes 6291456 | tf_op jit(solution)/shard_map/residual/pallas_call | solution.py:360
  137.1 12.4 %collective-permute-done.4.rest_2_ = bf16[256,2048]{1,0:T(8,128)(2,1)S(1)} collective-permute-done((bf16[256,2048]{1,0:T(8,128)(2,1)S(1)}, bf16[256,2048]{1,0:T(8,128)(2,1)S(1)}, u32[]{:S(2)}, u32[]{:S(2)}) %collective-permute-start.4) | collective-permute-done | bytes 1048608 | tf_op jit(solution)/shard_map/ppermute | solution.py:311
  149.5 1.2 collective-permute-start.3
  150.7 0.0 collective-permute-done.6.rest_4_
  150.7 0.1 collective-permute-start.5
  150.8 21.5 %collective-permute-done.8.rest_6_ = bf16[256,2048]{1,0:T(8,128)(2,1)} collective-permute-done((bf16[256,2048]{1,0:T(8,128)(2,1)S(1)}, bf16[256,2048]{1,0:T(8,128)(2,1)}, u32[]{:S(2)}, u32[]{:S(2)}) %collective-permute-start.8) | collective-permute-done | bytes 1048608 | tf_op jit(solution)/shard_map/ppermute | solution.py:311
  172.2 0.0 collective-permute-start.7
  172.3 0.0 collective-permute-done.2.far_other
  172.3 0.5 collective-permute-start.9
  172.8 15.4 %qkv.1 = (bf16[8,512,256]{2,1,0:T(8,128)(2,1)}, bf16[2,512,256]{2,1,0:T(8,128)(2,1)}, bf16[2,512,256]{2,1,0:T(8,128)(2,1)}) custom-call(s32[6]{0:T(128)} %stack.24.me, s32[32]{0:T(128)} %slot_of.5, s32[32]{0:T(128)} %cached_len.3, bf16[512,2048]{1,0:T(8,128)(2,1)} %tokens.3, f32[1,2048]{1,0:T(1,128)} %bitcast.12, bf16[2048,2048]{1,0:T(8,128)(2,1)} %w_query.1, ...), custom_call_target="tpu_custom_call" | custom-call | flops 6442450944 | bytes 20971520 | tf_op jit(solution)/shard_map/qkv/pallas_call | solution.py:320
  188.2 0.0 collective-permute-done.near
  188.2 19.5 %attention.1.attended = bf16[8,512,256]{2,1,0:T(8,128)(2,1)} custom-call(s32[6]{0:T(128)} %stack.24.me, s32[32]{0:T(128)} %slot_of.5, s32[32]{0:T(128)} %cached_len.3, s32[32,16]{1,0:T(8,128)} %copy.18.page_table, bf16[8,512,256]{2,1,0:T(8,128)(2,1)} %get-tuple-element.10.query, bf16[2,512,256]{2,1,0:T(8,128)(2,1)} %get-tuple-element.11.key, ...), custom_call_target="tpu_custom_call" | custom-call | flops 6442450944 | bytes 8388608 | tf_op jit(solution)/shard_map/attention/pallas_call | solution.py:381
  207.7 0.0 collective-permute-done.3.rest_1_
  207.7 0.0 collective-permute-done.5.rest_3_
  207.8 0.0 collective-permute-done.7.rest_5_
  207.8 0.0 collective-permute-done.9.rest_7_
  207.8 0.9 copy-done.3
  208.7 0.4 copy-done.4
  209.1 0.3 copy-done.5
  209.4 0.4 copy-done.6
  209.8 12.2 %project.1 = bf16[512,2048]{1,0:T(8,128)(2,1)} custom-call(s32[6]{0:T(128)} %stack.24.me, bf16[8,512,256]{2,1,0:T(8,128)(2,1)} %attention.1.attended, f32[512,2048]{1,0:T(8,128)} %residual.1, f32[1,2048]{1,0:T(1,128)} %bitcast.13, bf16[256,2048]{1,0:T(8,128)(2,1)} %rest_0_.1, bf16[256,2048]{1,0:T(8,128)(2,1)} %copy-done.3, bf16[256,2048]{1,0:T(8,128)(2,1)} %copy-done.1, ...), custom_call_target="tpu_custom_call" | custom-call | flops 4294967296 | bytes 16777216 | tf_op jit(solution)/shard_map/project/pallas_call | solution.py:415
  (12 shorter events, 0.0 us)
Async XLA Ops:
  2.0 101.2 %copy-start = (bf16[256,2048]{1,0:T(8,128)(2,1)S(1)}, bf16[256,2048]{1,0:T(8,128)(2,1)}, u32[]{:S(2)}) copy-start(bf16[256,2048]{1,0:T(8,128)(2,1)} %rest_0_.1) | copy-start | bytes 3145732
  2.0 127.5 %copy-start.7 = (bf16[2048,64]{0,1:T(8,128)(2,1)S(1)}, bf16[2048,64]{0,1:T(8,128)(2,1)}, u32[]{:S(2)}) copy-start(bf16[2048,64]{0,1:T(8,128)(2,1)} %param.23) | copy-start | bytes 786436
  99.9 27.3 %collective-permute-start.1 = (bf16[8,64,1024]{2,1,0:T(8,128)(2,1)}, bf16[8,64,1024]{2,1,0:T(8,128)(2,1)}, u32[]{:S(2)}, u32[]{:S(2)}) collective-permute-start(bf16[8,64,1024]{2,1,0:T(8,128)(2,1)} %get-tuple-element.14), channel_id=1, source_target_pairs={{0,28},{4,8},{8,4},{12,16},{16,12},{20,24},{24,20},{28,0},{1,29},{... | collective-permute-start | bytes 3145736 | tf_op jit(solution)/shard_map/ppermute | solution.py:305
  103.3 85.0 %collective-permute-start = (bf16[16,64,1024]{2,1,0:T(8,128)(2,1)}, bf16[16,64,1024]{2,1,0:T(8,128)(2,1)}, u32[]{:S(2)}, u32[]{:S(2)}) collective-permute-start(bf16[16,64,1024]{2,1,0:T(8,128)(2,1)} %get-tuple-element.13), channel_id=1, source_target_pairs={{0,4},{4,0},{8,12},{12,8},{16,20},{20,16},{24,28},{28,24},{1,5},{5... | collective-permute-start | bytes 6291464 | tf_op jit(solution)/shard_map/ppermute | solution.py:306
  103.3 46.2 %collective-permute-start.4 = (bf16[256,2048]{1,0:T(8,128)(2,1)S(1)}, bf16[256,2048]{1,0:T(8,128)(2,1)S(1)}, u32[]{:S(2)}, u32[]{:S(2)}) collective-permute-start(bf16[256,2048]{1,0:T(8,128)(2,1)S(1)} %copy-done), channel_id=1, source_target_pairs={{0,8},{4,12},{8,0},{12,4},{16,24},{20,28},{24,16},{28,20},{1,9},{5... | collective-permute-start | bytes 3145736 | tf_op jit(solution)/shard_map/ppermute | solution.py:311
  104.5 46.2 %collective-permute-start.6 = (bf16[256,2048]{1,0:T(8,128)(2,1)S(1)}, bf16[256,2048]{1,0:T(8,128)(2,1)S(1)}, u32[]{:S(2)}, u32[]{:S(2)}) collective-permute-start(bf16[256,2048]{1,0:T(8,128)(2,1)S(1)} %copy-done), channel_id=1, source_target_pairs={{0,16},{4,20},{8,24},{12,28},{16,0},{20,4},{24,8},{28,12},{1,17},{... | collective-permute-start | bytes 3145736 | tf_op jit(solution)/shard_map/ppermute | solution.py:311
  104.6 67.7 %collective-permute-start.8 = (bf16[256,2048]{1,0:T(8,128)(2,1)S(1)}, bf16[256,2048]{1,0:T(8,128)(2,1)}, u32[]{:S(2)}, u32[]{:S(2)}) collective-permute-start(bf16[256,2048]{1,0:T(8,128)(2,1)S(1)} %copy-done), channel_id=1, source_target_pairs={{0,24},{4,28},{8,16},{12,20},{16,8},{20,12},{24,0},{28,4},{1,25},{... | collective-permute-start | bytes 3145736 | tf_op jit(solution)/shard_map/ppermute | solution.py:311
  127.1 45.1 %collective-permute-start.2 = (bf16[8,64,1024]{2,1,0:T(8,128)(2,1)}, bf16[8,64,1024]{2,1,0:T(8,128)(2,1)}, u32[]{:S(2)}, u32[]{:S(2)}) collective-permute-start(bf16[8,64,1024]{2,1,0:T(8,128)(2,1)} %collective-permute-done.1.far_own), channel_id=1, source_target_pairs={{0,1},{1,0},{2,3},{3,2},{4,5},{5,4},{6,7},{7,6},{8,9},{9,8},{10,11... | collective-permute-start | bytes 3145736 | tf_op jit(solution)/shard_map/ppermute | solution.py:307
  149.5 38.7 %copy-start.1 = (bf16[256,2048]{1,0:T(8,128)(2,1)}, bf16[256,2048]{1,0:T(8,128)(2,1)S(1)}, u32[]{:S(2)}) copy-start(bf16[256,2048]{1,0:T(8,128)(2,1)S(1)} %collective-permute-done.4.rest_2_) | copy-start | bytes 3145732
  149.5 58.2 %collective-permute-start.3 = (bf16[256,2048]{1,0:T(8,128)(2,1)S(1)}, bf16[256,2048]{1,0:T(8,128)(2,1)S(1)}, u32[]{:S(2)}, u32[]{:S(2)}) collective-permute-start(bf16[256,2048]{1,0:T(8,128)(2,1)S(1)} %copy-done), channel_id=1, source_target_pairs={{0,4},{4,0},{8,12},{12,8},{16,20},{20,16},{24,28},{28,24},{1,5},{5... | collective-permute-start | bytes 3145736 | tf_op jit(solution)/shard_map/ppermute | solution.py:313
  150.7 37.5 %copy-start.2 = (bf16[256,2048]{1,0:T(8,128)(2,1)}, bf16[256,2048]{1,0:T(8,128)(2,1)S(1)}, u32[]{:S(2)}) copy-start(bf16[256,2048]{1,0:T(8,128)(2,1)S(1)} %collective-permute-done.6.rest_4_) | copy-start | bytes 3145732
  150.7 57.1 %collective-permute-start.5 = (bf16[256,2048]{1,0:T(8,128)(2,1)S(1)}, bf16[256,2048]{1,0:T(8,128)(2,1)S(1)}, u32[]{:S(2)}, u32[]{:S(2)}) collective-permute-start(bf16[256,2048]{1,0:T(8,128)(2,1)S(1)} %collective-permute-done.4.rest_2_), channel_id=1, source_target_pairs={{0,4},{4,0},{8,12},{12,8},{16,20},{20,16},{24,28},{28,24},{1,5},{5... | collective-permute-start | bytes 3145736 | tf_op jit(solution)/shard_map/ppermute | solution.py:313
  172.2 35.5 %collective-permute-start.7 = (bf16[256,2048]{1,0:T(8,128)(2,1)S(1)}, bf16[256,2048]{1,0:T(8,128)(2,1)S(1)}, u32[]{:S(2)}, u32[]{:S(2)}) collective-permute-start(bf16[256,2048]{1,0:T(8,128)(2,1)S(1)} %collective-permute-done.6.rest_4_), channel_id=1, source_target_pairs={{0,4},{4,0},{8,12},{12,8},{16,20},{20,16},{24,28},{28,24},{1,5},{5... | collective-permute-start | bytes 3145736 | tf_op jit(solution)/shard_map/ppermute | solution.py:313
  172.3 35.5 %collective-permute-start.9 = (bf16[256,2048]{1,0:T(8,128)(2,1)}, bf16[256,2048]{1,0:T(8,128)(2,1)S(1)}, u32[]{:S(2)}, u32[]{:S(2)}) collective-permute-start(bf16[256,2048]{1,0:T(8,128)(2,1)} %collective-permute-done.8.rest_6_), channel_id=1, source_target_pairs={{0,4},{4,0},{8,12},{12,8},{16,20},{20,16},{24,28},{28,24},{1,5},{5... | collective-permute-start | bytes 3145736 | tf_op jit(solution)/shard_map/ppermute | solution.py:313
  207.7 1.0 copy-start.3
  207.8 1.3 copy-start.4
  207.8 1.6 copy-start.5
  207.8 2.1 copy-start.6

commit v2 on v1

--- a/solution.py
+++ b/solution.py
@@ -17,7 +17,9 @@
 EPS = 1e-06
 LOG2E = 1.4426950408889634
 MASKED = -1e30
-VMEM_BYTES = 56 * 1024 * 1024
+VMEM_BYTES = 63 * 1024 * 1024
+
+SHORT = pl.CostEstimate(flops=1, bytes_accessed=1, transcendentals=0)
 
 ANY = pl.BlockSpec(memory_space=pl.ANY)
 SMEM = pl.BlockSpec(memory_space=pltpu.SMEM)
@@ -56,22 +58,38 @@
     return lax.fori_loop(0, REQ_DEV, step, jnp.int32(0))
 
 
-def pages_kernel(me, slot_of, page_table, pool, near, far, sems):
-    group, member = me[0], me[1]
-    to_near = mover_to(slot_of, group, me[2])
-    to_far = mover_to(slot_of, group, me[3])
-    count, part = near.shape[0], far.shape[0]
+def pages_kernel(me, slot_of, page_table, pool, near, *rest):
+    fars, (near_held, far_held, sems, out_sems) = rest[:KVH], rest[KVH:]
+    member = me[1]
+    to_near = mover_to(slot_of, me[0], me[2])
+    to_far = mover_to(slot_of, me[0], me[3])
+    count, part = near.shape[0], fars[0].shape[0]
+    width = 2 * HD
     copies = []
     for p in range(part):
         page = page_table[to_far, (member % 2) * part + p]
-        copies.append(pltpu.make_async_copy(pool.at[page], far.at[p], sems.at[p]))
+        copies.append(pltpu.make_async_copy(pool.at[page], far_held.at[p], sems.at[p]))
     for p in range(count):
         page = page_table[to_near, p]
-        copies.append(pltpu.make_async_copy(pool.at[page], near.at[p], sems.at[part + p]))
+        copies.append(pltpu.make_async_copy(pool.at[page], near_held.at[p], sems.at[part + p]))
     for copy in copies:
         copy.start()
-    for copy in copies:
-        copy.wait()
+    moves = []
+    for p in range(part):
+        copies[p].wait()
+        for g in range(KVH):
+            move = pltpu.make_async_copy(
+                far_held.at[p, :, g * width : (g + 1) * width], fars[g].at[p], out_sems.at[g, p]
+            )
+            move.start()
+            moves.append(move)
+    for p in range(count):
+        copies[part + p].wait()
+        move = pltpu.make_async_copy(near_held.at[p], near.at[p], out_sems.at[KVH, p])
+        move.start()
+        moves.append(move)
+    for move in moves:
+        move.wait()
 
 
 def qkv_kernel(
@@ -133,63 +151,52 @@
         at = slice(i * tile, (i + 1) * tile)
         inputs = tokens[at, :].astype(jnp.float32)
         normed = (normalize(inputs) * gain[...]).astype(jnp.bfloat16)
-        low = jnp.dot(normed, left[...], preferred_element_type=jnp.float32).astype(jnp.bfloat16)
+        low = lax.dot_general(
+            normed, left[...], (((1,), (1,)), ((), ())), preferred_element_type=jnp.float32
+        ).astype(jnp.bfloat16)
         up = jnp.dot(low, right[...], preferred_element_type=jnp.float32)
         laurel = normed.astype(jnp.float32) + normalize(up) * laurel_gain[...]
         out[at, :] = inputs + laurel
 
 
 def attention_kernel(
-    me, slot_of, cached_len, page_table, query, key, value, pool, near, far_own, far_other,
+    kv, me, slot_of, cached_len, page_table, query, key, value, pool, near, far_own, far_other,
     out, stored, sems,
 ):
-    kv = pl.program_id(0)
     group, member = me[0], me[1]
-    slot = me[4]
-    request = request_of(slot_of, slot)
+    request = request_of(slot_of, me[4])
     length = cached_len[request]
     home = request // REQ_DEV
     page_count, page_rows = near.shape[0], near.shape[1]
     cached_rows = page_count * page_rows
     part = page_count // 2
     width = 2 * HD
-
-    @pl.when(kv == 0)
+    channels = slice(kv * width, (kv + 1) * width)
+
+    def copy_page(source, p):
+        return pltpu.make_async_copy(
+            source, stored.at[pl.ds(p * page_rows, page_rows)], sems.at[p]
+        )
+
+    @pl.when(home == group)
     def _():
-        def fetch(source_of):
-            for p in range(page_count):
-                source = source_of(p)
-                for g in range(KVH):
-                    pltpu.make_async_copy(
-                        source.at[:, g * width : (g + 1) * width],
-                        stored.at[g, p * page_rows : (p + 1) * page_rows],
-                        sems.at[g, p],
-                    ).start()
-
-        @pl.when(home == group)
-        def _():
-            fetch(lambda p: pool.at[page_table[request, p]])
-
-        @pl.when(home == me[2])
-        def _():
-            fetch(lambda p: near.at[p])
-
-        @pl.when(home == me[3])
-        def _():
-            @pl.when(member % 2 == 0)
-            def _():
-                fetch(lambda p: far_own.at[p] if p < part else far_other.at[p - part])
-
-            @pl.when(member % 2 == 1)
-            def _():
-                fetch(lambda p: far_other.at[p] if p < part else far_own.at[p - part])
+        for p in range(page_count):
+            copy_page(pool.at[page_table[request, p], :, channels], p).start()
+
+    @pl.when(home == me[2])
+    def _():
+        for p in range(page_count):
+            copy_page(near.at[p, :, channels], p).start()
+
+    @pl.when(home == me[3])
+    def _():
+        own_first = (member % 2) * part
+        for p in range(part):
+            copy_page(far_own.at[p], own_first + p).start()
+            copy_page(far_other.at[p], part - own_first + p).start()
 
     for p in range(page_count):
-        pltpu.make_async_copy(
-            near.at[p, :, :width],
-            stored.at[kv, p * page_rows : (p + 1) * page_rows],
-            sems.at[kv, p],
-        ).wait()
+        copy_page(near.at[p, :, channels], p).wait()
 
     scale = HD ** (-0.5) * LOG2E
     heads, rows = query.shape[0], query.shape[1]
@@ -203,7 +210,7 @@
         for t in range(rows // tile):
             q = query[h, t * tile : (t + 1) * tile]
             old = lax.dot_general(
-                q, stored[kv, :, :HD], contract, preferred_element_type=jnp.float32
+                q, stored[:, :HD], contract, preferred_element_type=jnp.float32
             ) * scale + bias
             seen = fresh if fresh > rows else (t + 1) * tile
             new = lax.dot_general(
@@ -219,7 +226,7 @@
             new = jnp.exp2(new - highest)
             total = jnp.sum(old, axis=1, keepdims=True) + jnp.sum(new, axis=1, keepdims=True)
             result = jnp.dot(
-                old.astype(jnp.bfloat16), stored[kv, :, HD:], preferred_element_type=jnp.float32
+                old.astype(jnp.bfloat16), stored[:, HD:], preferred_element_type=jnp.float32
             ) + jnp.dot(
                 new.astype(jnp.bfloat16), value[0, :seen], preferred_element_type=jnp.float32
             )
@@ -229,30 +236,39 @@
     lax.fori_loop(0, heads, one_head, 0)
 
 
-def output_kernel(count, me, attended, residual, post_gain, *rest):
-    weights, out = rest[:count], rest[count]
-    held, total, sems = rest[count + 1 :]
-    copies = [pltpu.make_async_copy(weights[i], held.at[i], sems.at[i]) for i in range(count)]
-    for copy in copies:
+def output_kernel(places, me, *refs):
+    attended, residual, post_gain = refs[:KVH], refs[KVH], refs[KVH + 1]
+    weights, out = refs[KVH + 2 : -5], refs[-5]
+    held, heads, total, sems = refs[-4:]
+    depth = held.shape[1]
+    copies = {}
+    for i, (k, offset) in enumerate(places):
+        copy = pltpu.make_async_copy(
+            weights[i], held.at[k, offset : offset + weights[i].shape[0]], sems.at[i]
+        )
         copy.start()
-    rows = attended.shape[1]
-    depth = held.shape[1]
+        copies.setdefault(k, []).append(copy)
+    per_kv, rows = attended[0].shape[0], attended[0].shape[1]
+    for g in range(KVH):
+        heads[g * per_kv : (g + 1) * per_kv] = attended[g][...]
     per_head = HD // depth
     tile = 256
-    for i in range(count):
-        copies[i].wait()
-        block = me[0] ^ i
+    order = list(copies)
+    for i, k in enumerate(order):
+        for copy in copies[k]:
+            copy.wait()
+        block = me[0] ^ k
         head, part = block // per_head, block % per_head
         for t in range(rows // tile):
             at = slice(t * tile, (t + 1) * tile)
             if per_head == 1:
-                lhs = attended[head, at]
+                lhs = heads[head, at]
             else:
-                lhs = attended[head, at, pl.ds(pl.multiple_of(part * depth, depth), depth)]
-            product = jnp.dot(lhs, held[i], preferred_element_type=jnp.float32)
+                lhs = heads[head, at, pl.ds(pl.multiple_of(part * depth, depth), depth)]
+            product = jnp.dot(lhs, held[k], preferred_element_type=jnp.float32)
             if i == 0:
                 total[at] = product
-            elif i < count - 1:
+            elif i < len(order) - 1:
                 total[at] += product
             else:
                 projected = total[at] + product
@@ -289,28 +305,42 @@
     ).astype(jnp.int32)
 
     part = page_count // 2
-    page_shape = (page_rows, channels)
-    near_out, far_out = pl.pallas_call(
+    near_shape = (page_count, page_rows, channels)
+    far_shape = (part, page_rows, 2 * HD)
+    near_out, *far_out = pl.pallas_call(
         pages_kernel,
-        out_shape=(
-            jax.ShapeDtypeStruct((page_count,) + page_shape, jnp.bfloat16),
-            jax.ShapeDtypeStruct((part,) + page_shape, jnp.bfloat16),
-        ),
+        out_shape=(jax.ShapeDtypeStruct(near_shape, jnp.bfloat16),)
+        + (jax.ShapeDtypeStruct(far_shape, jnp.bfloat16),) * KVH,
         in_specs=[SMEM, SMEM, SMEM, ANY],
-        out_specs=(ANY, ANY),
-        scratch_shapes=[pltpu.SemaphoreType.DMA((page_count + part,))],
+        out_specs=(ANY,) * (1 + KVH),
+        scratch_shapes=[
+            pltpu.VMEM(near_shape, jnp.bfloat16),
+            pltpu.VMEM((part, page_rows, channels), jnp.bfloat16),
+            pltpu.SemaphoreType.DMA((page_count + part,)),
+            pltpu.SemaphoreType.DMA((KVH + 1, page_count)),
+        ],
         compiler_params=params(),
         name="pages",
     )(me, slot_of, page_table, cache_pool)
-    far_own = lax.ppermute(far_out, "req", far_pairs)
-    near = lax.ppermute(near_out, "req", near_pairs)
-    far_other = lax.ppermute(far_own, "head", [(i, i ^ 1) for i in range(members)])
-
-    blocks = {0: w_output}
-    for k in range(2, groups, 2):
-        blocks[k] = lax.ppermute(w_output, "req", [(i, i ^ k) for i in range(groups)])
-    for k in range(0, groups, 2):
-        blocks[k + 1] = lax.ppermute(blocks[k], "req", near_pairs)
+
+    def send(block, axis, pairs):
+        return lax.ppermute(block, axis, pairs)
+
+    def flip(k):
+        return [(i, i ^ k) for i in range(groups)]
+
+    def after(block, *others):
+        return lax.optimization_barrier((block,) + others)[0]
+
+    side = [(i, i ^ 1) for i in range(members)]
+    far_hop = groups // 2
+    across = send(w_output, "req", flip(far_hop))
+    half = w_output.shape[0] // 2
+    halves = [w_output[:half], w_output[half:]]
+    hops = range(2, far_hop, 2)
+    first = {k: send(halves[0], "req", flip(k)) for k in hops}
+    far_own = [send(far, "req", far_pairs) for far in far_out]
+    near = send(near_out, "req", near_pairs)
 
     gain = input_gain.reshape(1, width)
     table = rope_table(page_count * page_rows + CH)
@@ -348,14 +378,16 @@
             pltpu.VMEM((rows, HD // 2), jnp.float32),
         ],
         compiler_params=params(),
-        cost_estimate=pl.CostEstimate(
-            flops=2 * rows * width * 3072, bytes_accessed=20 << 20, transcendentals=0
-        ),
+        cost_estimate=SHORT,
         name="qkv",
     )(
         me, slot_of, cached_len, tokens, gain, w_query, w_keyval,
         query_gain.reshape(1, HD), key_gain.reshape(1, HD), table,
     )
+
+    far_other = [None] * KVH
+    far_other[0] = send(after(far_own[0], query), "head", side)
+    tokens_later = after(tokens, far_own[0], query)
 
     residual = pl.pallas_call(
         residual_kernel,
@@ -363,11 +395,21 @@
         in_specs=[VMEM] * 5,
         out_specs=VMEM,
         compiler_params=params(),
-        cost_estimate=pl.CostEstimate(
-            flops=4 * rows * width * 64, bytes_accessed=6 << 20, transcendentals=0
-        ),
+        cost_estimate=SHORT,
         name="residual",
-    )(tokens, gain, laurel_left, laurel_right, laurel_gain.reshape(1, width))
+    )(tokens_later, gain, laurel_left.T, laurel_right, laurel_gain.reshape(1, width))
+
+    far_other[1] = send(after(far_own[1], residual), "head", side)
+    pieces = [(0, 0, w_output), (far_hop, 0, across)]
+    pieces += [(k + 1, 0, send(after(w, residual), "req", near_pairs)) for k, _, w in pieces]
+    rest = after(halves[1], residual, far_own[1])
+    second = {k: send(rest, "req", flip(k)) for k in hops}
+    relays = {}
+    for k in hops:
+        block = after(first[k], residual)
+        relays[k] = send(block, "req", flip(far_hop))
+        pieces += [(k, 0, block), (k + 1, 0, send(block, "req", near_pairs))]
+        pieces += [(k + far_hop, 0, relays[k])]
 
     if share > 1:
         team = [list(range(m, m + share)) for m in range(0, members, share)]
@@ -378,56 +420,69 @@
         key, value = both[:, :, :HD], both[:, :, HD:]
 
     per_kv = NH // KVH
-    attended = pl.pallas_call(
-        attention_kernel,
-        grid=(KVH,),
-        out_shape=jax.ShapeDtypeStruct((NH, rows, HD), jnp.bfloat16),
-        in_specs=[
-            SMEM,
-            SMEM,
-            SMEM,
-            SMEM,
-            pl.BlockSpec((per_kv, rows, HD), lambda j: (j, 0, 0)),
-            pl.BlockSpec((1, CH, HD), lambda j: (j, 0, 0)),
-            pl.BlockSpec((1, CH, HD), lambda j: (j, 0, 0)),
-            ANY,
-            ANY,
-            ANY,
-            ANY,
-        ],
-        out_specs=pl.BlockSpec((per_kv, rows, HD), lambda j: (j, 0, 0)),
+    def attend(g):
+        return pl.pallas_call(
+            functools.partial(attention_kernel, g),
+            grid=(1,),
+            out_shape=jax.ShapeDtypeStruct((per_kv, rows, HD), jnp.bfloat16),
+            in_specs=[
+                SMEM,
+                SMEM,
+                SMEM,
+                SMEM,
+                pl.BlockSpec((per_kv, rows, HD), lambda j: (g, 0, 0)),
+                pl.BlockSpec((1, CH, HD), lambda j: (g, 0, 0)),
+                pl.BlockSpec((1, CH, HD), lambda j: (g, 0, 0)),
+                ANY,
+                ANY,
+                ANY,
+                ANY,
+            ],
+            out_specs=pl.BlockSpec((per_kv, rows, HD), lambda j: (0, 0, 0)),
+            scratch_shapes=[
+                pltpu.VMEM((page_count * page_rows, 2 * HD), jnp.bfloat16),
+                pltpu.SemaphoreType.DMA((page_count,)),
+            ],
+            compiler_params=params(),
+            cost_estimate=SHORT,
+            name="attention",
+        )(
+            me, slot_of, cached_len, page_table, query, key, value, cache_pool,
+            near, far_own[g], far_other[g],
+        )
+
+    attended = [attend(0)]
+    late = []
+    for k in hops:
+        block = after(second[k], attended[0])
+        relayed = send(block, "req", flip(far_hop))
+        early = after(relays[k], attended[0])
+        pieces += [(k + far_hop + 1, 0, send(early, "req", near_pairs))]
+        pieces += [(k, half, block), (k + 1, half, send(block, "req", near_pairs))]
+        late.append((k, relayed))
+    attended += [attend(g) for g in range(1, KVH)]
+    for k, relayed in late:
+        relayed = after(relayed, attended[-1])
+        pieces += [(k + far_hop, half, relayed)]
+        pieces += [(k + far_hop + 1, half, send(relayed, "req", near_pairs))]
+
+    places = [(k, offset) for k, offset, _ in pieces]
+    weights = [w for _, _, w in pieces]
+    return pl.pallas_call(
+        functools.partial(output_kernel, places),
+        out_shape=jax.ShapeDtypeStruct((rows, width), jnp.bfloat16),
+        in_specs=[SMEM] + [VMEM] * (KVH + 2) + [ANY] * len(pieces),
+        out_specs=VMEM,
         scratch_shapes=[
-            pltpu.VMEM((KVH, page_count * page_rows, 2 * HD), jnp.bfloat16),
-            pltpu.SemaphoreType.DMA((KVH, page_count)),
+            pltpu.VMEM((groups, w_output.shape[0], width), jnp.bfloat16),
+            pltpu.VMEM((NH, rows, HD), jnp.bfloat16),
+            pltpu.VMEM((rows, width), jnp.float32),
+            pltpu.SemaphoreType.DMA((len(pieces),)),
         ],
         compiler_params=params(),
-        cost_estimate=pl.CostEstimate(
-            flops=4 * NH * rows * 1536 * HD, bytes_accessed=8 << 20,
-            transcendentals=NH * rows * 1536,
-        ),
-        name="attention",
-    )(
-        me, slot_of, cached_len, page_table, query, key, value, cache_pool,
-        near, far_own, far_other,
-    )
-
-    depth = w_output.shape[0]
-    return pl.pallas_call(
-        functools.partial(output_kernel, groups),
-        out_shape=jax.ShapeDtypeStruct((rows, width), jnp.bfloat16),
-        in_specs=[SMEM, VMEM, VMEM, VMEM] + [ANY] * groups,
-        out_specs=VMEM,
-        scratch_shapes=[
-            pltpu.VMEM((groups, depth, width), jnp.bfloat16),
-            pltpu.VMEM((rows, width), jnp.float32),
-            pltpu.SemaphoreType.DMA((groups,)),
-        ],
-        compiler_params=params(),
-        cost_estimate=pl.CostEstimate(
-            flops=2 * rows * width * width, bytes_accessed=16 << 20, transcendentals=0
-        ),
+        cost_estimate=SHORT,
         name="project",
-    )(me, attended, residual, post_gain.reshape(1, width), *[blocks[k] for k in range(groups)])
+    )(me, *attended, residual, post_gain.reshape(1, width), *weights)
 
 
 def solution(mesh):

time: 223 us -> 92 us (0.41)
  Pallas kernels: 152 us -> 61.6 us
  waiting for transfers between devices: 54.3 us -> 10 us
  starting transfers between devices: 11.1 us -> 14.4 us
    pallas_call x3 -> x4, Pallas kernels: 130 us -> 39.5 us  [the longest x2 22.8 us: attend(): pl.pallas_call(functools.partial(attention_kernel, g), grid=(1,), out_sha...]
    ppermute x10 -> x16, waiting for transfers between devices: 54.3 us -> 10 us  [send(): return lax.ppermute(block, axis, pairs)]
    ppermute x10 -> x16, starting transfers between devices: 11.1 us -> 14.4 us  [send(): return lax.ppermute(block, axis, pairs)]
    slice x0 -> x1, local copies, waits for them, and re-layouts: none -> 2.29 us  [shards(): halves = [w_output[:half], w_output[half:]]]
    unnamed x18 -> x5, local copies, waits for them, and re-layouts: 4.43 us -> 2.18 us
  transfers between devices with their start and end apart: 10 -> 16, of which waited for: 3 -> 3; matrix products, arithmetic and copies ran while one was open for 0% -> 3% of each run, Pallas kernels for 19% -> 49%
where the time goes in v2:
time: 92 us; the launch traced here: 91.3 us
  Pallas kernels  61.6 us (67%)
  starting transfers between devices  14.4 us (16%)
  waiting for transfers between devices  10 us (11%)
  local copies, waits for them, and re-layouts  5.14 us (6%)
    pallas_call x2, Pallas kernels, attend(): pl.pallas_call(functools.partial(attention_kernel, g), grid=(1,), out_sha...  22.8 us
    pallas_call x1, Pallas kernels, shards(): pl.pallas_call(qkv_kernel, grid=(query_steps + KVH,), out_shape=(jax.Shap...  15.4 us
    ppermute x16, starting transfers between devices, send(): return lax.ppermute(block, axis, pairs)  14.4 us
    pallas_call x1, Pallas kernels, shards(): pl.pallas_call(functools.partial(output_kernel, places), out_shape=jax.Sh...  12.2 us
    ppermute x16, waiting for transfers between devices, send(): return lax.ppermute(block, axis, pairs)  10 us
    pallas_call x1, Pallas kernels, shards(): pl.pallas_call(residual_kernel, out_shape=jax.ShapeDtypeStruct((rows, wid...  6.63 us
    pallas_call x1, Pallas kernels, shards(): pl.pallas_call(pages_kernel, out_shape=(jax.ShapeDtypeStruct(near_shape,...  4.54 us
    slice x1, local copies, waits for them, and re-layouts, shards(): halves = [w_output[:half], w_output[half:]]  2.29 us
  transfers between devices with their start and end apart: 16, of which 3 were waited for; matrix products, arithmetic and copies ran while one was open for 3% of the time, Pallas kernels for 49%

profile of v2, /device:TPU:0, one launch (start us, length us, event | category | flops | bytes accessed | tf_op | source)
XLA Modules:
  0.0 91.3 jit_solution(3412577402507545558)
XLA Ops:
  0.0 1.4 %copy.18.page_table = s32[32,16]{1,0:T(8,128)} copy(s32[32,16]{0,1:T(8,128)} %param.28) | data formatting | bytes 4096 | tf_op args[12]
  1.4 0.7 stack.24.me
  2.0 4.5 %pages.1 = (bf16[16,64,1024]{2,1,0:T(8,128)(2,1)}, bf16[8,64,512]{2,1,0:T(8,128)(2,1)}, bf16[8,64,512]{2,1,0:T(8,128)(2,1)}) custom-call(s32[6]{0:T(128)} %stack.24.me, s32[32]{0:T(128)} %slot_of.7, s32[32,16]{1,0:T(8,128)} %copy.18.page_table, bf16[64,64,1024]{2,1,0:T(8,128)(2,1)} %pool.5), custom_call_target="tpu_custom_call" | custom-call | tf_op jit(solution)/shard_map/pages/pallas_call | solution.py:310
  6.6 0.5 collective-permute-start
  7.1 2.6 %collective-permute-start.5 = (bf16[256,2048]{1,0:T(8,128)(2,1)}, bf16[256,2048]{1,0:T(8,128)(2,1)}, u32[]{:S(2)}, u32[]{:S(2)}) collective-permute-start(bf16[256,2048]{1,0:T(8,128)(2,1)} %refs_4_.1), channel_id=1, source_target_pairs={{0,16},{4,20},{8,24},{12,28},{16,0},{20,4},{24,8},{28,12},{1,17},{... | collective-permute-start | bytes 3145736 | tf_op jit(solution)/shard_map/ppermute | solution.py:327
  9.7 1.2 %collective-permute-start.1 = (bf16[8,64,512]{2,1,0:T(8,128)(2,1)}, bf16[8,64,512]{2,1,0:T(8,128)(2,1)}, u32[]{:S(2)}, u32[]{:S(2)}) collective-permute-start(bf16[8,64,512]{2,1,0:T(8,128)(2,1)} %get-tuple-element.25), channel_id=1, source_target_pairs={{0,28},{4,8},{8,4},{12,16},{16,12},{20,24},{24,20},{28,0},{1,29},{... | collective-permute-start | bytes 1572872 | tf_op jit(solution)/shard_map/ppermute | solution.py:327
  10.9 1.4 %collective-permute-start.3 = (bf16[8,64,512]{2,1,0:T(8,128)(2,1)}, bf16[8,64,512]{2,1,0:T(8,128)(2,1)}, u32[]{:S(2)}, u32[]{:S(2)}) collective-permute-start(bf16[8,64,512]{2,1,0:T(8,128)(2,1)} %get-tuple-element.27), channel_id=1, source_target_pairs={{0,28},{4,8},{8,4},{12,16},{16,12},{20,24},{24,20},{28,0},{1,29},{... | collective-permute-start | bytes 1572872 | tf_op jit(solution)/shard_map/ppermute | solution.py:327
  12.3 2.3 %fusion = (bf16[128,2048]{1,0:T(8,128)(2,1)}, bf16[128,2048]{1,0:T(8,128)(2,1)}) fusion(bf16[256,2048]{1,0:T(8,128)(2,1)} %refs_4_.1), kind=kLoop, calls=%fused_computation | loop fusion | bytes 2097152 | tf_op jit(solution)/shard_map/slice | solution.py:339
  14.6 0.6 collective-permute-start.8
  15.2 15.4 %qkv.1 = (bf16[8,512,256]{2,1,0:T(8,128)(2,1)}, bf16[2,512,256]{2,1,0:T(8,128)(2,1)}, bf16[2,512,256]{2,1,0:T(8,128)(2,1)}) custom-call(s32[6]{0:T(128)} %stack.24.me, s32[32]{0:T(128)} %slot_of.7, s32[32]{0:T(128)} %cached_len.5, bf16[512,2048]{1,0:T(8,128)(2,1)} %tokens.2, f32[1,2048]{1,0:T(1,128)} %bitcast.12, bf16[2048,2048]{1,0:T(8,128)(2,1)} %w_query.1, ...), custom_call_target="tpu_custom_call" | custom-call | flops 1 | bytes 1 | tf_op jit(solution)/shard_map/qkv/pallas_call | solution.py:350
  30.7 1.6 %collective-permute-start.2 = (bf16[8,64,512]{2,1,0:T(8,128)(2,1)}, bf16[8,64,512]{2,1,0:T(8,128)(2,1)}, u32[]{:S(2)}, u32[]{:S(2)}) collective-permute-start(bf16[8,64,512]{2,1,0:T(8,128)(2,1)} %collective-permute-done.1.far_own), channel_id=1, source_target_pairs={{0,1},{1,0},{2,3},{3,2},{4,5},{5,4},{6,7},{7,6},{8,9},{9,8},{10,11... | collective-permute-start | bytes 1572872 | tf_op jit(solution)/shard_map/ppermute | solution.py:327
  32.3 6.6 %residual.1.refs_2_ = f32[512,2048]{1,0:T(8,128)} custom-call(bf16[512,2048]{1,0:T(8,128)(2,1)} %tokens.2, f32[1,2048]{1,0:T(1,128)} %bitcast.13, bf16[64,2048]{1,0:T(8,128)(2,1)} %bitcast.11, bf16[64,2048]{1,0:T(8,128)(2,1)} %right.1, f32[1,2048]{1,0:T(1,128)} %bitcast.14), custom_call_target="tpu_custom_call" | custom-call | flops 1 | bytes 1 | tf_op jit(solution)/shard_map/residual/pallas_call | solution.py:392
  39.0 0.0 collective-permute-done.3.far_own
  39.0 1.4 %collective-permute-start.12 = (bf16[128,2048]{1,0:T(8,128)(2,1)}, bf16[128,2048]{1,0:T(8,128)(2,1)}, u32[]{:S(2)}, u32[]{:S(2)}) collective-permute-start(bf16[128,2048]{1,0:T(8,128)(2,1)} %get-tuple-element.34), channel_id=1, source_target_pairs={{0,8},{4,12},{8,0},{12,4},{16,24},{20,28},{24,16},{28,20},{1,9},{5... | collective-permute-start | bytes 1572872 | tf_op jit(solution)/shard_map/ppermute | solution.py:327
  40.4 6.5 %collective-permute-done.8.refs_8_ = bf16[128,2048]{1,0:T(8,128)(2,1)S(1)} collective-permute-done((bf16[128,2048]{1,0:T(8,128)(2,1)}, bf16[128,2048]{1,0:T(8,128)(2,1)S(1)}, u32[]{:S(2)}, u32[]{:S(2)}) %collective-permute-start.8) | collective-permute-done | bytes 524320 | tf_op jit(solution)/shard_map/ppermute | solution.py:327
  46.9 1.5 %collective-permute-start.4 = (bf16[8,64,512]{2,1,0:T(8,128)(2,1)}, bf16[8,64,512]{2,1,0:T(8,128)(2,1)}, u32[]{:S(2)}, u32[]{:S(2)}) collective-permute-start(bf16[8,64,512]{2,1,0:T(8,128)(2,1)} %collective-permute-done.3.far_own), channel_id=1, source_target_pairs={{0,1},{1,0},{2,3},{3,2},{4,5},{5,4},{6,7},{7,6},{8,9},{9,8},{10,11... | collective-permute-start | bytes 1572872 | tf_op jit(solution)/shard_map/ppermute | solution.py:327
  48.4 0.0 collective-permute-done.5.refs_5_
  48.4 0.7 collective-permute-start.10
  49.2 0.0 collective-permute-done.2.far_other
  49.2 0.1 collective-permute-start.6
  49.3 11.4 %attention.2.refs_0_ = bf16[4,512,256]{2,1,0:T(8,128)(2,1)} custom-call(s32[6]{0:T(128)} %stack.24.me, s32[32]{0:T(128)} %slot_of.7, s32[32]{0:T(128)} %cached_len.5, s32[32,16]{1,0:T(8,128)} %copy.18.page_table, bf16[8,512,256]{2,1,0:T(8,128)(2,1)} %get-tuple-element.21.query, bf16[2,512,256]{2,1,0:T(8,128)(2,1)} %get-tuple-element.22.key, ...), custom_call_target="tpu_custom_call" | custom-call | flops 1 | bytes 1 | tf_op jit(solution)/shard_map/attention/pallas_call | solution.py:424
  60.6 0.0 collective-permute-done.12.refs_12_
  60.7 1.3 %collective-permute-start.14 = (bf16[128,2048]{1,0:T(8,128)(2,1)}, bf16[128,2048]{1,0:T(8,128)(2,1)}, u32[]{:S(2)}, u32[]{:S(2)}) collective-permute-start(bf16[128,2048]{1,0:T(8,128)(2,1)} %collective-permute-done.12.refs_12_), channel_id=1, source_target_pairs={{0,16},{4,20},{8,24},{12,28},{16,0},{20,4},{24,8},{28,12},{1,17},{... | collective-permute-start | bytes 1572872 | tf_op jit(solution)/shard_map/ppermute | solution.py:327
  62.0 0.3 collective-permute-start.7
  62.2 0.3 collective-permute-start.9
  62.5 11.4 %attention.3.refs_1_ = bf16[4,512,256]{2,1,0:T(8,128)(2,1)} custom-call(s32[6]{0:T(128)} %stack.24.me, s32[32]{0:T(128)} %slot_of.7, s32[32]{0:T(128)} %cached_len.5, s32[32,16]{1,0:T(8,128)} %copy.18.page_table, bf16[8,512,256]{2,1,0:T(8,128)(2,1)} %get-tuple-element.21.query, bf16[2,512,256]{2,1,0:T(8,128)(2,1)} %get-tuple-element.22.key, ...), custom_call_target="tpu_custom_call" | custom-call | flops 1 | bytes 1 | tf_op jit(solution)/shard_map/attention/pallas_call | solution.py:424
  73.9 0.3 collective-permute-start.13
  74.2 1.0 %collective-permute-done.14.refs_14_ = bf16[128,2048]{1,0:T(8,128)(2,1)} collective-permute-done((bf16[128,2048]{1,0:T(8,128)(2,1)}, bf16[128,2048]{1,0:T(8,128)(2,1)}, u32[]{:S(2)}, u32[]{:S(2)}) %collective-permute-start.14) | collective-permute-done | bytes 524320 | tf_op jit(solution)/shard_map/ppermute | solution.py:327
  75.3 0.5 collective-permute-start.15
  75.8 2.4 %collective-permute-done.11.refs_11_ = bf16[128,2048]{1,0:T(8,128)(2,1)} collective-permute-done((bf16[128,2048]{1,0:T(8,128)(2,1)}, bf16[128,2048]{1,0:T(8,128)(2,1)}, u32[]{:S(2)}, u32[]{:S(2)}) %collective-permute-start.11) | collective-permute-done | bytes 524320 | tf_op jit(solution)/shard_map/ppermute | solution.py:327
  78.2 0.8 copy-done.1
  79.0 12.2 %project.1 = bf16[512,2048]{1,0:T(8,128)(2,1)} custom-call(s32[6]{0:T(128)} %stack.24.me, bf16[4,512,256]{2,1,0:T(8,128)(2,1)} %attention.2.refs_0_, bf16[4,512,256]{2,1,0:T(8,128)(2,1)} %attention.3.refs_1_, f32[512,2048]{1,0:T(8,128)} %residual.1.refs_2_, f32[1,2048]{1,0:T(1,128)} %bitcast.15, bf16[256,2048]{1,0:T(8,128)(2,1)} %refs_4_.1, ...), custom_call_target="tpu_custom_call" | custom-call | flops 1 | bytes 1 | tf_op jit(solution)/shard_map/project/pallas_call | solution.py:471
  (13 shorter events, 0.0 us)
Async XLA Ops:
  6.6 42.7 %collective-permute-start = (bf16[16,64,1024]{2,1,0:T(8,128)(2,1)}, bf16[16,64,1024]{2,1,0:T(8,128)(2,1)}, u32[]{:S(2)}, u32[]{:S(2)}) collective-permute-start(bf16[16,64,1024]{2,1,0:T(8,128)(2,1)} %get-tuple-element.24), channel_id=1, source_target_pairs={{0,4},{4,0},{8,12},{12,8},{16,20},{20,16},{24,28},{28,24},{1,5},{5... | collective-permute-start | bytes 6291464 | tf_op jit(solution)/shard_map/ppermute | solution.py:327
  7.1 41.3 %collective-permute-start.5 = (bf16[256,2048]{1,0:T(8,128)(2,1)}, bf16[256,2048]{1,0:T(8,128)(2,1)}, u32[]{:S(2)}, u32[]{:S(2)}) collective-permute-start(bf16[256,2048]{1,0:T(8,128)(2,1)} %refs_4_.1), channel_id=1, source_target_pairs={{0,16},{4,20},{8,24},{12,28},{16,0},{20,4},{24,8},{28,12},{1,17},{... | collective-permute-start | bytes 3145736 | tf_op jit(solution)/shard_map/ppermute | solution.py:327
  9.7 21.0 %collective-permute-start.1 = (bf16[8,64,512]{2,1,0:T(8,128)(2,1)}, bf16[8,64,512]{2,1,0:T(8,128)(2,1)}, u32[]{:S(2)}, u32[]{:S(2)}) collective-permute-start(bf16[8,64,512]{2,1,0:T(8,128)(2,1)} %get-tuple-element.25), channel_id=1, source_target_pairs={{0,28},{4,8},{8,4},{12,16},{16,12},{20,24},{24,20},{28,0},{1,29},{... | collective-permute-start | bytes 1572872 | tf_op jit(solution)/shard_map/ppermute | solution.py:327
  10.9 28.1 %collective-permute-start.3 = (bf16[8,64,512]{2,1,0:T(8,128)(2,1)}, bf16[8,64,512]{2,1,0:T(8,128)(2,1)}, u32[]{:S(2)}, u32[]{:S(2)}) collective-permute-start(bf16[8,64,512]{2,1,0:T(8,128)(2,1)} %get-tuple-element.27), channel_id=1, source_target_pairs={{0,28},{4,8},{8,4},{12,16},{16,12},{20,24},{24,20},{28,0},{1,29},{... | collective-permute-start | bytes 1572872 | tf_op jit(solution)/shard_map/ppermute | solution.py:327
  14.6 32.3 %collective-permute-start.8 = (bf16[128,2048]{1,0:T(8,128)(2,1)}, bf16[128,2048]{1,0:T(8,128)(2,1)S(1)}, u32[]{:S(2)}, u32[]{:S(2)}) collective-permute-start(bf16[128,2048]{1,0:T(8,128)(2,1)} %get-tuple-element.38), channel_id=1, source_target_pairs={{0,8},{4,12},{8,0},{12,4},{16,24},{20,28},{24,16},{28,20},{1,9},{5... | collective-permute-start | bytes 1572872 | tf_op jit(solution)/shard_map/ppermute | solution.py:327
  30.7 18.5 %collective-permute-start.2 = (bf16[8,64,512]{2,1,0:T(8,128)(2,1)}, bf16[8,64,512]{2,1,0:T(8,128)(2,1)}, u32[]{:S(2)}, u32[]{:S(2)}) collective-permute-start(bf16[8,64,512]{2,1,0:T(8,128)(2,1)} %collective-permute-done.1.far_own), channel_id=1, source_target_pairs={{0,1},{1,0},{2,3},{3,2},{4,5},{5,4},{6,7},{7,6},{8,9},{9,8},{10,11... | collective-permute-start | bytes 1572872 | tf_op jit(solution)/shard_map/ppermute | solution.py:327
  39.0 21.7 %collective-permute-start.12 = (bf16[128,2048]{1,0:T(8,128)(2,1)}, bf16[128,2048]{1,0:T(8,128)(2,1)}, u32[]{:S(2)}, u32[]{:S(2)}) collective-permute-start(bf16[128,2048]{1,0:T(8,128)(2,1)} %get-tuple-element.34), channel_id=1, source_target_pairs={{0,8},{4,12},{8,0},{12,4},{16,24},{20,28},{24,16},{28,20},{1,9},{5... | collective-permute-start | bytes 1572872 | tf_op jit(solution)/shard_map/ppermute | solution.py:327
  46.9 15.3 %copy-start = (bf16[128,2048]{1,0:T(8,128)(2,1)}, bf16[128,2048]{1,0:T(8,128)(2,1)S(1)}, u32[]{:S(2)}) copy-start(bf16[128,2048]{1,0:T(8,128)(2,1)S(1)} %collective-permute-done.8.refs_8_) | copy-start | bytes 1572868
  46.9 15.3 %collective-permute-start.4 = (bf16[8,64,512]{2,1,0:T(8,128)(2,1)}, bf16[8,64,512]{2,1,0:T(8,128)(2,1)}, u32[]{:S(2)}, u32[]{:S(2)}) collective-permute-start(bf16[8,64,512]{2,1,0:T(8,128)(2,1)} %collective-permute-done.3.far_own), channel_id=1, source_target_pairs={{0,1},{1,0},{2,3},{3,2},{4,5},{5,4},{6,7},{7,6},{8,9},{9,8},{10,11... | collective-permute-start | bytes 1572872 | tf_op jit(solution)/shard_map/ppermute | solution.py:327
  48.4 25.4 %collective-permute-start.10 = (bf16[128,2048]{1,0:T(8,128)(2,1)S(1)}, bf16[128,2048]{1,0:T(8,128)(2,1)}, u32[]{:S(2)}, u32[]{:S(2)}) collective-permute-start(bf16[128,2048]{1,0:T(8,128)(2,1)S(1)} %collective-permute-done.8.refs_8_), channel_id=1, source_target_pairs={{0,16},{4,20},{8,24},{12,28},{16,0},{20,4},{24,8},{28,12},{1,17},{... | collective-permute-start | bytes 1572872 | tf_op jit(solution)/shard_map/ppermute | solution.py:327
  49.2 26.6 %collective-permute-start.6 = (bf16[256,2048]{1,0:T(8,128)(2,1)}, bf16[256,2048]{1,0:T(8,128)(2,1)}, u32[]{:S(2)}, u32[]{:S(2)}) collective-permute-start(bf16[256,2048]{1,0:T(8,128)(2,1)} %refs_4_.1), channel_id=1, source_target_pairs={{0,4},{4,0},{8,12},{12,8},{16,20},{20,16},{24,28},{28,24},{1,5},{5... | collective-permute-start | bytes 3145736 | tf_op jit(solution)/shard_map/ppermute | solution.py:327
  60.7 14.6 %collective-permute-start.14 = (bf16[128,2048]{1,0:T(8,128)(2,1)}, bf16[128,2048]{1,0:T(8,128)(2,1)}, u32[]{:S(2)}, u32[]{:S(2)}) collective-permute-start(bf16[128,2048]{1,0:T(8,128)(2,1)} %collective-permute-done.12.refs_12_), channel_id=1, source_target_pairs={{0,16},{4,20},{8,24},{12,28},{16,0},{20,4},{24,8},{28,12},{1,17},{... | collective-permute-start | bytes 1572872 | tf_op jit(solution)/shard_map/ppermute | solution.py:327
  62.0 13.8 %collective-permute-start.7 = (bf16[256,2048]{1,0:T(8,128)(2,1)}, bf16[256,2048]{1,0:T(8,128)(2,1)}, u32[]{:S(2)}, u32[]{:S(2)}) collective-permute-start(bf16[256,2048]{1,0:T(8,128)(2,1)} %collective-permute-done.5.refs_5_), channel_id=1, source_target_pairs={{0,4},{4,0},{8,12},{12,8},{16,20},{20,16},{24,28},{28,24},{1,5},{5... | collective-permute-start | bytes 3145736 | tf_op jit(solution)/shard_map/ppermute | solution.py:327
  62.2 13.0 %collective-permute-start.9 = (bf16[128,2048]{1,0:T(8,128)(2,1)S(1)}, bf16[128,2048]{1,0:T(8,128)(2,1)}, u32[]{:S(2)}, u32[]{:S(2)}) collective-permute-start(bf16[128,2048]{1,0:T(8,128)(2,1)S(1)} %collective-permute-done.8.refs_8_), channel_id=1, source_target_pairs={{0,4},{4,0},{8,12},{12,8},{16,20},{20,16},{24,28},{28,24},{1,5},{5... | collective-permute-start | bytes 1572872 | tf_op jit(solution)/shard_map/ppermute | solution.py:327
  73.9 4.3 %collective-permute-start.13 = (bf16[128,2048]{1,0:T(8,128)(2,1)}, bf16[128,2048]{1,0:T(8,128)(2,1)}, u32[]{:S(2)}, u32[]{:S(2)}) collective-permute-start(bf16[128,2048]{1,0:T(8,128)(2,1)} %collective-permute-done.12.refs_12_), channel_id=1, source_target_pairs={{0,4},{4,0},{8,12},{12,8},{16,20},{20,16},{24,28},{28,24},{1,5},{5... | collective-permute-start | bytes 1572872 | tf_op jit(solution)/shard_map/ppermute | solution.py:327
  75.3 2.9 %collective-permute-start.11 = (bf16[128,2048]{1,0:T(8,128)(2,1)}, bf16[128,2048]{1,0:T(8,128)(2,1)}, u32[]{:S(2)}, u32[]{:S(2)}) collective-permute-start(bf16[128,2048]{1,0:T(8,128)(2,1)} %collective-permute-done.10.refs_10_), channel_id=1, source_target_pairs={{0,4},{4,0},{8,12},{12,8},{16,20},{20,16},{24,28},{28,24},{1,5},{5... | collective-permute-start | bytes 1572872 | tf_op jit(solution)/shard_map/ppermute | solution.py:327
  75.3 2.9 %collective-permute-start.15 = (bf16[128,2048]{1,0:T(8,128)(2,1)}, bf16[128,2048]{1,0:T(8,128)(2,1)S(1)}, u32[]{:S(2)}, u32[]{:S(2)}) collective-permute-start(bf16[128,2048]{1,0:T(8,128)(2,1)} %collective-permute-done.14.refs_14_), channel_id=1, source_target_pairs={{0,4},{4,0},{8,12},{12,8},{16,20},{20,16},{24,28},{28,24},{1,5},{5... | collective-permute-start | bytes 1572872 | tf_op jit(solution)/shard_map/ppermute | solution.py:327
  78.2 0.8 copy-start.1

commit v3 on v2

v3 whole, which is shorter than its diff:
```python
import functools
import math

import jax
import jax.numpy as jnp
import numpy as np
from jax import lax
from jax.experimental import pallas as pl
from jax.experimental.pallas import tpu as pltpu
from jax.sharding import PartitionSpec as P

NH = 8
KVH = 2
HD = 256
REQ_DEV = 4
CH = 512
EPS = 1e-06
LOG2E = 1.4426950408889634
MASKED = -1e30
VMEM_BYTES = 64 * 1024 * 1024

SHORT = pl.CostEstimate(flops=1, bytes_accessed=1, transcendentals=0)

ANY = pl.BlockSpec(memory_space=pl.ANY)
SMEM = pl.BlockSpec(memory_space=pltpu.SMEM)
VMEM = pl.BlockSpec(memory_space=pltpu.VMEM)


def params(**more):
    return pltpu.CompilerParams(vmem_limit_bytes=VMEM_BYTES, **more)


def rope_table(rows):
    half = HD // 2
    inverse = 1000000.0 ** (-2.0 * np.arange(half) / HD)
    angle = np.arange(rows)[:, None] * inverse[None, :]
    return np.concatenate([np.cos(angle), np.sin(angle)], axis=1).astype(np.float32)


def place():
    groups = lax.axis_size("req")
    group = lax.axis_index("req").astype(jnp.int32)
    member = lax.axis_index("head").astype(jnp.int32)
    odd = group % 2
    near = group + 1 - 2 * odd
    far = lax.rem(group + 2 * odd - 1 + groups, jnp.int32(groups))
    return group, member, near, far


def slot_here(rows):
    share = CH // rows
    group, member, _, _ = place()
    return group * REQ_DEV + member // share, member % share * rows


def normalize(values):
    return values * lax.rsqrt(jnp.mean(values * values, axis=-1, keepdims=True) + EPS)


def request_of(slot_of, slot):
    return lax.fori_loop(
        0,
        slot_of.shape[0],
        lambda i, found: jnp.where(slot_of[i] == slot, i, found),
        jnp.int32(0),
    )


def mover_to(slot_of, group, target):
    def step(i, found):
        request = group * REQ_DEV + i
        return jnp.where(slot_of[request] // REQ_DEV == target, request, found)

    return lax.fori_loop(0, REQ_DEV, step, jnp.int32(0))


def pages_kernel(slot_of, page_table_in, pool, w_output, near, *rest):
    fars, pieces_out = rest[:KVH], rest[KVH : KVH + 2]
    page_table, near_held, far_held, middle, last, sems, in_sems, out_sems = rest[KVH + 2 :]
    table_copy = pltpu.make_async_copy(page_table_in, page_table, in_sems.at[0])
    table_copy.start()
    quarter = last.shape[0]
    pieces = [
        pltpu.make_async_copy(w_output.at[pl.ds(quarter, 2 * quarter)], middle, in_sems.at[1]),
        pltpu.make_async_copy(w_output.at[pl.ds(3 * quarter, quarter)], last, in_sems.at[2]),
    ]
    group, member, near_group, far_group = place()
    to_near = mover_to(slot_of, group, near_group)
    to_far = mover_to(slot_of, group, far_group)
    count, part = near.shape[0], fars[0].shape[0]
    width = 2 * HD
    table_copy.wait()
    copies = []
    for p in range(part):
        page = page_table[(member % 2) * part + p, to_far]
        copies.append(pltpu.make_async_copy(pool.at[page], far_held.at[p], sems.at[p]))
    for p in range(count):
        page = page_table[p, to_near]
        copies.append(pltpu.make_async_copy(pool.at[page], near_held.at[p], sems.at[part + p]))
    for copy in copies + pieces:
        copy.start()
    moves = []
    for p in range(part):
        copies[p].wait()
        for g in range(KVH):
            source = far_held.at[p, :, g * width : (g + 1) * width]
            moves.append(pltpu.make_async_copy(source, fars[g].at[p], out_sems.at[g, p]))
            moves[-1].start()
    for p in range(count):
        copies[part + p].wait()
        moves.append(pltpu.make_async_copy(near_held.at[p], near.at[p], out_sems.at[KVH, p]))
        moves[-1].start()
    for i, (held, out) in enumerate(zip((middle, last), pieces_out)):
        pieces[i].wait()
        moves.append(pltpu.make_async_copy(held, out, in_sems.at[1 + i]))
        moves[-1].start()
    for move in moves:
        move.wait()


def residual_kernel(gain, left, right, laurel_gain, tokens_in, out, tokens, residual, sems, out_sems):
    rows = tokens.shape[0]
    tile = 128
    tiles = rows // tile
    inputs, moves = [], []
    for i in range(tiles):
        at = slice(i * tile, (i + 1) * tile)
        inputs.append(pltpu.make_async_copy(tokens_in.at[at], tokens.at[at], sems.at[i]))
        inputs[i].start()
    for i in range(tiles):
        inputs[i].wait()
        at = slice(i * tile, (i + 1) * tile)
        x = tokens[at, :].astype(jnp.float32)
        normed = (normalize(x) * gain[...]).astype(jnp.bfloat16)
        low = lax.dot_general(
            normed, left[...], (((1,), (1,)), ((), ())), preferred_element_type=jnp.float32
        ).astype(jnp.bfloat16)
        up = jnp.dot(low, right[...], preferred_element_type=jnp.float32)
        laurel = normed.astype(jnp.float32) + normalize(up) * laurel_gain[...]
        residual[at, :] = x + laurel
        moves.append(pltpu.make_async_copy(residual.at[at], out.at[at], out_sems.at[i]))
        moves[i].start()
    for move in moves:
        move.wait()


def qkv_kernel(
    slot_of, cached_len, gain, query_gain, key_gain, tokens_in, w_query_in, w_keyval_in,
    table_in, query_out, key_out, value_out,
    tokens, w_query, w_keyval, table, table_row, normed, cosine, sine, query, key, value,
    in_sems, w_sems, out_sems,
):
    rows = tokens.shape[0]
    half = HD // 2
    chunk = min(128, rows)
    chunks = rows // chunk
    wide = 4 * HD
    tokens_copies = []
    for i in range(chunks):
        at = slice(i * chunk, (i + 1) * chunk)
        copy = pltpu.make_async_copy(tokens_in.at[at], tokens.at[at], in_sems.at[i])
        copy.start()
        tokens_copies.append(copy)
    units = [(0, c) for c in range(0, NH * HD // 2, wide)]
    units += [(1, c) for c in range(0, 2 * KVH * HD, wide)]
    units += [(0, c) for c in range(NH * HD // 2, NH * HD, wide)]
    w_copies = []
    for i, (which, c) in enumerate(units):
        source, held = ((w_query_in, w_query), (w_keyval_in, w_keyval))[which]
        columns = slice(c, c + wide)
        w_copies.append(
            pltpu.make_async_copy(source.at[:, columns], held.at[:, columns], w_sems.at[i])
        )
    w_copies[0].start()
    slot, first_row = slot_here(rows)
    start = cached_len[request_of(slot_of, slot)] + first_row
    aligned = pl.multiple_of(start // 8 * 8, 8)
    row_copy = pltpu.make_async_copy(
        table_in.at[pl.ds(aligned, 8)], table_row, in_sems.at[chunks]
    )
    row_copy.start()
    table_copy = pltpu.make_async_copy(
        table_in.at[pl.ds(0, rows)], table, in_sems.at[chunks + 1]
    )
    tile = 64
    for i in range(rows // tile):
        if i * tile % chunk == 0:
            tokens_copies[i * tile // chunk].wait()
            if i == 0:
                table_copy.start()
                w_copies[1].start()
        at = slice(i * tile, (i + 1) * tile)
        inputs = tokens[at, :].astype(jnp.float32)
        normed[at, :] = (normalize(inputs) * gain[...]).astype(jnp.bfloat16)
    row_copy.wait()
    table_copy.wait()
    base = table_row[pl.ds(start - aligned, 1), :]
    cos_base, sin_base = base[:, :half], base[:, half:]
    cos_row, sin_row = table[:, :half], table[:, half:]
    cosine[...] = cos_base * cos_row - sin_base * sin_row
    sine[...] = sin_base * cos_row + cos_base * sin_row

    sent = []
    tile = 256

    def finish(which, head, t, raw):
        at = slice(t * tile, (t + 1) * tile)
        if which == 1 and head % 2 == 1:
            held, out, place = value, value_out, head // 2
            value[place, at] = normalize(raw).astype(jnp.bfloat16)
        else:
            held, out, place = (query, query_out, head) if which == 0 else (key, key_out, head // 2)
            v = normalize(raw) * (query_gain, key_gain)[which][...]
            x, y = v[:, :half], v[:, half:]
            c, s = cosine[at], sine[at]
            held[place, at, :half] = (x * c - y * s).astype(jnp.bfloat16)
            held[place, at, half:] = (y * c + x * s).astype(jnp.bfloat16)
        if t == rows // tile - 1:
            copy = pltpu.make_async_copy(held.at[place], out.at[place], out_sems.at[len(sent)])
            copy.start()
            sent.append(copy)

    waiting = None
    for i, (which, first) in enumerate(units):
        w_copies[i].wait()
        if i + 2 < len(units):
            w_copies[i + 2].start()
        held = (w_query, w_keyval)[which]
        for c in range(first, first + wide, HD):
            for t in range(rows // tile):
                raw = jnp.dot(
                    normed[t * tile : (t + 1) * tile],
                    held[:, c : c + HD],
                    preferred_element_type=jnp.float32,
                )
                if waiting is not None:
                    finish(*waiting)
                waiting = (which, c // HD, t, raw)
    finish(*waiting)
    for copy in sent:
        copy.wait()


def attention_kernel(
    kv, slot_of, cached_len, page_table_in, query_in, key_in, value_in, pool, near, far_own,
    far_other, *rest,
):
    out_in, (page_table, query, key, value, out, stored, sems, in_sems, out_sems) = (
        rest[-10],
        rest[-9:],
    )
    group, member, near_group, far_group = place()
    table_copy = pltpu.make_async_copy(page_table_in, page_table, in_sems.at[3])
    table_copy.start()
    per_kv, rows = query.shape[0], query.shape[1]
    inputs = [
        pltpu.make_async_copy(query_in.at[pl.ds(kv * per_kv, per_kv)], query, in_sems.at[0]),
        pltpu.make_async_copy(key_in.at[kv], key, in_sems.at[1]),
        pltpu.make_async_copy(value_in.at[kv], value, in_sems.at[2]),
    ]
    for copy in inputs:
        copy.start()
    slot, first_row = slot_here(rows)
    request = request_of(slot_of, slot)
    length = cached_len[request]
    home = request // REQ_DEV
    page_count, page_rows = near.shape[0], near.shape[1]
    cached_rows = page_count * page_rows
    part = page_count // 2
    width = 2 * HD
    channels = slice(kv * width, (kv + 1) * width)

    def copy_page(source, p):
        return pltpu.make_async_copy(
            source, stored.at[pl.ds(p * page_rows, page_rows)], sems.at[p]
        )

    table_copy.wait()

    @pl.when(home == group)
    def _():
        for p in range(page_count):
            copy_page(pool.at[page_table[p, request], :, channels], p).start()

    @pl.when(home == near_group)
    def _():
        for p in range(page_count):
            copy_page(near.at[p, :, channels], p).start()

    @pl.when(home == far_group)
    def _():
        own_first = (member % 2) * part
        for p in range(part):
            copy_page(far_own.at[p], own_first + p).start()
            copy_page(far_other.at[p], part - own_first + p).start()

    for copy in inputs:
        copy.wait()
    for p in range(page_count):
        copy_page(near.at[p, :, channels], p).wait()

    scale = HD ** (-0.5) * LOG2E
    fresh = key.shape[0]
    tile = 256
    at_key = lax.broadcasted_iota(jnp.int32, (1, cached_rows), 1)
    bias = jnp.where(at_key < length, 0.0, MASKED)
    contract = (((1,), (1,)), ((), ()))

    def scores(h, t):
        q = query[h, t * tile : (t + 1) * tile]
        seen = fresh if fresh > rows else (t + 1) * tile
        old = lax.dot_general(q, stored[:, :HD], contract, preferred_element_type=jnp.float32)
        new = lax.dot_general(q, key[:seen], contract, preferred_element_type=jnp.float32)
        return old, new

    def finish(h, t, old, new):
        seen = new.shape[1]
        clear = 0 if fresh > rows else t * tile
        old = old + bias
        row = first_row + t * tile + lax.broadcasted_iota(jnp.int32, (tile, seen - clear), 0)
        column = clear + lax.broadcasted_iota(jnp.int32, (tile, seen - clear), 1)
        edge = jnp.where(column <= row, new[:, clear:], MASKED)
        parts = [(old, stored[:, HD:]), (edge, value[clear:seen])]
        if clear:
            parts.append((new[:, :clear], value[:clear]))
        highest = functools.reduce(
            jnp.maximum, [jnp.max(x, axis=1, keepdims=True) for x, _ in parts]
        )
        parts = [(jnp.exp2((x - highest) * scale), v) for x, v in parts]
        total = functools.reduce(jnp.add, [jnp.sum(x, axis=1, keepdims=True) for x, _ in parts])
        result = functools.reduce(
            jnp.add,
            [
                jnp.dot(x.astype(jnp.bfloat16), v, preferred_element_type=jnp.float32)
                for x, v in parts
            ],
        )
        out[h, t * tile : (t + 1) * tile] = (result / total).astype(jnp.bfloat16)

    def send(h):
        return pltpu.make_async_copy(out.at[h], out_in.at[kv * per_kv + h], out_sems.at[h])

    items = [(h, t) for h in range(per_kv) for t in range(rows // tile)]
    current = scores(*items[0])
    for i, (h, t) in enumerate(items):
        following = scores(*items[i + 1]) if i + 1 < len(items) else None
        finish(h, t, *current)
        current = following
        if t == rows // tile - 1:
            send(h).start()
    for h in range(per_kv):
        send(h).wait()


def output_kernel(places, post_gain, attended, residual_in, *refs):
    arrays = 1 + max(i for _, _, i, _, _ in places)
    weights, out = refs[:arrays], refs[arrays]
    lhs, held, total, residual, result, sems, lhs_sems, res_sems, out_sems = refs[-9:]
    rows, width = total.shape
    depth = refs[0].shape[0]
    per_head = HD // depth
    order = list(dict.fromkeys(k for k, *_ in places))
    wide = 512
    group = place()[0]
    lhs_copies = []
    for i, k in enumerate(order):
        block = group ^ k
        head = block // per_head
        source = attended.at[head]
        if per_head > 1:
            part = pl.multiple_of(block % per_head * depth, depth)
            source = attended.at[head, :, pl.ds(part, depth)]
        copy = pltpu.make_async_copy(
            source, lhs.at[:, i * depth : (i + 1) * depth], lhs_sems.at[i]
        )
        copy.start()
        lhs_copies.append(copy)
    copies = []
    for n in range(width // wide):
        columns = slice(n * wide, (n + 1) * wide)
        copies.append([])
        for p, (k, offset, i, row, count) in enumerate(places):
            first = order.index(k) * depth + offset
            copies[n].append(
                pltpu.make_async_copy(
                    weights[i].at[row : row + count, columns],
                    held.at[first : first + count, columns],
                    sems.at[n, p],
                )
            )
    tile = 128
    res_copies = []
    for t in range(rows // tile):
        at = slice(t * tile, (t + 1) * tile)
        res_copies.append(
            pltpu.make_async_copy(residual_in.at[at], residual.at[at], res_sems.at[t])
        )
    for copy in copies[0] + copies[1]:
        copy.start()
    for copy in lhs_copies:
        copy.wait()
    squares = 0.0
    for n in range(width // wide):
        columns = slice(n * wide, (n + 1) * wide)
        for copy in copies[n]:
            copy.wait()
        for copy in copies[n + 2] if n + 2 < len(copies) else res_copies if n + 2 == len(copies) else []:
            copy.start()
        product = jnp.dot(lhs[...], held[:, columns], preferred_element_type=jnp.float32)
        total[:, columns] = product
        squares += jnp.sum(product * product, axis=1, keepdims=True)
    ratio = lax.rsqrt(squares * (1.0 / width) + EPS)
    out_copies = []
    for t in range(rows // tile):
        at = slice(t * tile, (t + 1) * tile)
        res_copies[t].wait()
        attn = total[at] * ratio[at] * post_gain[...]
        result[at] = ((attn + residual[at]) * (1.0 / math.sqrt(2.0))).astype(jnp.bfloat16)
        copy = pltpu.make_async_copy(result.at[at], out.at[at], out_sems.at[t])
        copy.start()
        out_copies.append(copy)
    for copy in out_copies:
        copy.wait()


def shards(
    tokens, input_gain, w_query, w_keyval, query_gain, key_gain, w_output, laurel_left,
    laurel_right, laurel_gain, post_gain, cache_pool, page_table, cached_len, slot_of,
):
    groups = lax.axis_size("req")
    members = lax.axis_size("head")
    rows, width = tokens.shape
    page_count = page_table.shape[1]
    page_rows = cache_pool.shape[1]
    channels = cache_pool.shape[2]
    share = CH // rows

    near_pairs = [(i, i ^ 1) for i in range(groups)]
    far_pairs = [(i, (i + 1) % groups if i % 2 else (i - 1) % groups) for i in range(groups)]
    def send(block, axis, pairs):
        return lax.ppermute(block, axis, pairs)

    def flip(k):
        return [(i, i ^ k) for i in range(groups)]

    def after(block, *others):
        return lax.optimization_barrier((block,) + others)[0]

    side = [(i, i ^ 1) for i in range(members)]
    far_hop = groups // 2
    top = w_output[: w_output.shape[0] // 4]
    hops = range(2, far_hop, 2)
    side = [(i, i ^ 1) for i in range(members)]
    first = {k: send(top, "req", flip(k)) for k in hops}
    first[far_hop] = send(top, "req", flip(far_hop))
    own_near = send(w_output, "req", near_pairs)
    early_done = [*first.values(), own_near]
    pages_of = page_table.T
    part = page_count // 2
    near_shape = (page_count, page_rows, channels)
    far_shape = (part, page_rows, 2 * HD)
    gain = input_gain.reshape(1, width)
    quarter = w_output.shape[0] // 4
    piece = lambda n: (n * quarter, width)
    near_out, *far_out, middle, last = pl.pallas_call(
        pages_kernel,
        out_shape=(jax.ShapeDtypeStruct(near_shape, jnp.bfloat16),)
        + (jax.ShapeDtypeStruct(far_shape, jnp.bfloat16),) * KVH
        + tuple(jax.ShapeDtypeStruct(piece(n), jnp.bfloat16) for n in (2, 1)),
        in_specs=[SMEM, ANY, ANY, ANY],
        out_specs=(ANY,) * (3 + KVH),
        scratch_shapes=[
            pltpu.SMEM(pages_of.shape, jnp.int32),
            pltpu.VMEM(near_shape, jnp.bfloat16),
            pltpu.VMEM((part, page_rows, channels), jnp.bfloat16),
            pltpu.VMEM(piece(2), jnp.bfloat16),
            pltpu.VMEM(piece(1), jnp.bfloat16),
            pltpu.SemaphoreType.DMA((page_count + part,)),
            pltpu.SemaphoreType.DMA((3,)),
            pltpu.SemaphoreType.DMA((KVH + 1, page_count)),
        ],
        compiler_params=params(),
        cost_estimate=SHORT,
        name="pages",
    )(after(slot_of, top), pages_of, cache_pool, w_output)
    near = send(after(near_out, *early_done), "req", near_pairs)

    far_out = [after(far, *early_done) for far in far_out]
    far_own = [send(far, "req", far_pairs) for far in far_out]
    middle, last = (after(w, *early_done) for w in (middle, last))
    middles = {far_hop: send(middle, "req", flip(far_hop))}
    lasts = {far_hop: send(last, "req", flip(far_hop))}
    relays = {k: send(after(first[k], *early_done), "req", flip(far_hop)) for k in hops}

    table = rope_table(page_count * page_rows + CH)
    heads_shape = lambda heads: jax.ShapeDtypeStruct((heads, rows, HD), jnp.bfloat16)
    query, key, value = pl.pallas_call(
        qkv_kernel,
        out_shape=(heads_shape(NH), heads_shape(KVH), heads_shape(KVH)),
        in_specs=[SMEM, SMEM, VMEM, VMEM, VMEM, ANY, ANY, ANY, ANY],
        out_specs=(ANY,) * 3,
        scratch_shapes=[
            pltpu.VMEM((rows, width), jnp.bfloat16),
            pltpu.VMEM(w_query.shape, jnp.bfloat16),
            pltpu.VMEM(w_keyval.shape, jnp.bfloat16),
            pltpu.VMEM((rows, HD), jnp.float32),
            pltpu.VMEM((8, HD), jnp.float32),
            pltpu.VMEM((rows, width), jnp.bfloat16),
            pltpu.VMEM((rows, HD // 2), jnp.float32),
            pltpu.VMEM((rows, HD // 2), jnp.float32),
            pltpu.VMEM((NH, rows, HD), jnp.bfloat16),
            pltpu.VMEM((KVH, rows, HD), jnp.bfloat16),
            pltpu.VMEM((KVH, rows, HD), jnp.bfloat16),
            pltpu.SemaphoreType.DMA((8,)),
            pltpu.SemaphoreType.DMA((8,)),
            pltpu.SemaphoreType.DMA((NH + 2 * KVH,)),
        ],
        compiler_params=params(),
        cost_estimate=SHORT,
        name="qkv",
    )(
        slot_of, cached_len, gain, query_gain.reshape(1, HD),
        key_gain.reshape(1, HD), tokens, w_query, w_keyval, table,
    )

    far_other = [send(after(far_own[0], query), "head", side)]
    residual = pl.pallas_call(
        residual_kernel,
        out_shape=jax.ShapeDtypeStruct((rows, width), jnp.float32),
        in_specs=[VMEM] * 4 + [ANY],
        out_specs=ANY,
        scratch_shapes=[
            pltpu.VMEM((rows, width), jnp.bfloat16),
            pltpu.VMEM((rows, width), jnp.float32),
            pltpu.SemaphoreType.DMA((4,)),
            pltpu.SemaphoreType.DMA((4,)),
        ],
        compiler_params=params(),
        cost_estimate=SHORT,
        name="residual",
    )(
        gain, laurel_left.T, laurel_right, laurel_gain.reshape(1, width),
        after(tokens, far_own[0], query, near, *relays.values()),
    )
    pieces = [(0, 0, w_output), (1, 0, own_near)]
    shared = []
    for k, block in first.items():
        shared.append(send(after(block, query), "req", near_pairs))
        pieces += [(k, 0, block), (k + 1, 0, shared[-1])]
    far_other += [send(after(far, residual), "head", side) for far in far_own[1:]]
    for k in hops:
        middles[k] = send(after(middle, residual, *far_own), "req", flip(k))

    if share > 1:
        team = [list(range(m, m + share)) for m in range(0, members, share)]
        both = lax.all_gather(
            jnp.concatenate([key, value], axis=2), "head", axis=1, tiled=True,
            axis_index_groups=team,
        )
        key, value = both[:, :, :HD], both[:, :, HD:]

    per_kv = NH // KVH
    def attend(g, earlier=None):
        more = [] if earlier is None else [earlier]
        return pl.pallas_call(
            functools.partial(attention_kernel, g),
            out_shape=heads_shape(NH),
            in_specs=[SMEM] * 2 + [ANY] * (8 + len(more)),
            out_specs=ANY,
            scratch_shapes=[
                pltpu.SMEM(pages_of.shape, jnp.int32),
                pltpu.VMEM((per_kv, rows, HD), jnp.bfloat16),
                pltpu.VMEM((CH, HD), jnp.bfloat16),
                pltpu.VMEM((CH, HD), jnp.bfloat16),
                pltpu.VMEM((per_kv, rows, HD), jnp.bfloat16),
                pltpu.VMEM((page_count * page_rows, 2 * HD), jnp.bfloat16),
                pltpu.SemaphoreType.DMA((page_count,)),
                pltpu.SemaphoreType.DMA((4,)),
                pltpu.SemaphoreType.DMA((per_kv,)),
            ],
            input_output_aliases={10: 0} if more else {},
            compiler_params=params(),
            cost_estimate=SHORT,
            name="attention",
        )(
            slot_of, cached_len, pages_of, query, key, value, cache_pool,
            near, far_own[g], far_other[g], *more,
        )

    attended = [attend(0)]
    late = []
    ahead = after(attended[0], *far_other[1:], *middles.values())
    swapped = []

    def both_cores(k, offset, block):
        swapped.append(send(block, "req", near_pairs))
        if isinstance(k, tuple):
            pieces.append((k, offset, block))
            pieces.append((tuple(j + 1 for j in k), offset, swapped[-1]))
        else:
            pieces.extend([(k, offset, block), (k + 1, offset, swapped[-1])])

    for k in hops:
        here = after(middles[k], ahead)
        both_cores(k, quarter, here)
        both_cores(k + far_hop, 0, after(relays[k], ahead))
        late.append((k + far_hop, quarter, send(here, "req", flip(far_hop))))
        here = after(lasts[far_hop], ahead)
        both = send(jnp.concatenate([after(last, ahead), here], axis=0), "req", flip(k))
        late.append(((k, k + far_hop), 3 * quarter, both))
    for offset, block in ((quarter, middles[far_hop]), (3 * quarter, lasts[far_hop])):
        both_cores(far_hop, offset, after(block, ahead))
    for g in range(1, KVH):
        attended.append(attend(g, attended[-1]))
    earlier = [attended[-1], *swapped, *shared]
    for k, offset, block in late:
        both_cores(k, offset, after(block, *earlier))

    places = []
    for i, (k, offset, w) in enumerate(pieces):
        blocks = k if isinstance(k, tuple) else (k,)
        count = w.shape[0] // len(blocks)
        places += [(j, offset, i, n * count, count) for n, j in enumerate(blocks)]
    weights = [w for _, _, w in pieces]
    return pl.pallas_call(
        functools.partial(output_kernel, places),
        out_shape=jax.ShapeDtypeStruct((rows, width), jnp.bfloat16),
        in_specs=[VMEM] + [ANY] * (2 + len(pieces)),
        out_specs=ANY,
        scratch_shapes=[
            pltpu.VMEM((rows, NH * HD), jnp.bfloat16),
            pltpu.VMEM((NH * HD, width), jnp.bfloat16),
            pltpu.VMEM((rows, width), jnp.float32),
            pltpu.VMEM((rows, width), jnp.float32),
            pltpu.VMEM((rows, width), jnp.bfloat16),
            pltpu.SemaphoreType.DMA((4, len(places))),
            pltpu.SemaphoreType.DMA((groups,)),
            pltpu.SemaphoreType.DMA((4,)),
            pltpu.SemaphoreType.DMA((4,)),
        ],
        compiler_params=params(),
        cost_estimate=SHORT,
        name="project",
    )(post_gain.reshape(1, width), attended[-1], residual, *weights)


def solution(mesh):
    in_specs = (
        P(("req", "head"), None),
        P(),
        P(),
        P(),
        P(),
        P(),
        P("req", None),
        P(),
        P(),
        P(),
        P(),
        P("req", None, None),
        P(),
        P(),
        P(),
    )
    out_specs = P(("req", "head"), None)
    return jax.shard_map(shards, mesh=mesh, in_specs=in_specs, out_specs=out_specs, check_vma=False)
```

time: 92 us -> 88.1 us (0.958)
  Pallas kernels: 61.6 us -> 53.9 us
  local copies, waits for them, and re-layouts: 5.14 us -> 1.67 us
  starting transfers between devices: 14.4 us -> 17.4 us
  waiting for transfers between devices: 10 us -> 12.6 us
  other arithmetic: 0 us -> 1.87 us
    pallas_call x3, Pallas kernels: 38.2 us -> 28.8 us  [the longest x2 15.9 us: attend(): pl.pallas_call(functools.partial(attention_kernel, g), out_shape=heads_sh...]
    ppermute x16 -> x22, starting transfers between devices: 14.4 us -> 17.4 us  [send(): return lax.ppermute(block, axis, pairs)]
    ppermute x16 -> x22, waiting for transfers between devices: 10 us -> 12.6 us  [send(): return lax.ppermute(block, axis, pairs)]
    unnamed x5 -> x0, local copies, waits for them, and re-layouts: 2.18 us -> none
    concatenate x0 -> x1, other arithmetic: none -> 1.87 us  [shards(): jnp.concatenate([after(last, ahead), here], axis=0)]
    pallas_call x1, Pallas kernels: 4.54 us -> 6.1 us  [shards(): pl.pallas_call(pages_kernel, out_shape=(jax.ShapeDtypeStruct(near_shape,...]
    pallas_call x1, Pallas kernels: 6.63 us -> 7.73 us  [shards(): pl.pallas_call(residual_kernel, out_shape=jax.ShapeDtypeStruct((rows, wid...]
  transfers between devices with their start and end apart: 16 -> 22, of which waited for: 3 -> 6; matrix products, arithmetic and copies ran while one was open for 3% -> 4% of each run, Pallas kernels for 49% -> 49%
where the time goes in v3:
time: 88.1 us; the launch traced here: 87.7 us
  Pallas kernels  53.9 us (61%)
  starting transfers between devices  17.4 us (20%)
  waiting for transfers between devices  12.6 us (14%)
  other arithmetic  1.87 us (2%)
  local copies, waits for them, and re-layouts  1.67 us (2%)
    ppermute x22, starting transfers between devices, send(): return lax.ppermute(block, axis, pairs)  17.4 us
    pallas_call x2, Pallas kernels, attend(): pl.pallas_call(functools.partial(attention_kernel, g), out_shape=heads_sh...  15.9 us
    pallas_call x1, Pallas kernels, shards(): pl.pallas_call(qkv_kernel, out_shape=(heads_shape(NH), heads_shape(KVH),...  12.9 us
    ppermute x22, waiting for transfers between devices, send(): return lax.ppermute(block, axis, pairs)  12.6 us
    pallas_call x1, Pallas kernels, shards(): pl.pallas_call(functools.partial(output_kernel, places), out_shape=jax.Sh...  11.3 us
    pallas_call x1, Pallas kernels, shards(): pl.pallas_call(residual_kernel, out_shape=jax.ShapeDtypeStruct((rows, wid...  7.73 us
    pallas_call x1, Pallas kernels, shards(): pl.pallas_call(pages_kernel, out_shape=(jax.ShapeDtypeStruct(near_shape,...  6.1 us
    concatenate x1, other arithmetic, shards(): jnp.concatenate([after(last, ahead), here], axis=0)  1.87 us
  transfers between devices with their start and end apart: 22, of which 6 were waited for; matrix products, arithmetic and copies ran while one was open for 4% of the time, Pallas kernels for 49%

profile of v3, /device:TPU:0, one launch (start us, length us, event | category | flops | bytes accessed | tf_op | source)
XLA Modules:
  0.0 87.7 jit_solution(2296927705467317041)
XLA Ops:
  0.0 0.5 collective-permute-start.2
  0.5 1.7 %slice.3 = bf16[64,2048]{1,0:T(8,128)(2,1)} slice(bf16[256,2048]{1,0:T(8,128)(2,1)} %refs_0_.1), slice={[0:64], [0:2048]} | slice | bytes 524288 | tf_op jit(solution)/shard_map/slice | solution.py:451
  2.1 2.5 %collective-permute-start = (bf16[64,2048]{1,0:T(8,128)(2,1)}, bf16[64,2048]{1,0:T(8,128)(2,1)}, u32[]{:S(2)}, u32[]{:S(2)}) collective-permute-start(bf16[64,2048]{1,0:T(8,128)(2,1)} %slice.3), channel_id=1, source_target_pairs={{0,8},{4,12},{8,0},{12,4},{16,24},{20,28},{24,16},{28,20},{1,9},{5... | collective-permute-start | bytes 786440 | tf_op jit(solution)/shard_map/ppermute | solution.py:441
  4.6 1.5 %collective-permute-start.1 = (bf16[64,2048]{1,0:T(8,128)(2,1)}, bf16[64,2048]{1,0:T(8,128)(2,1)}, u32[]{:S(2)}, u32[]{:S(2)}) collective-permute-start(bf16[64,2048]{1,0:T(8,128)(2,1)} %slice.3), channel_id=1, source_target_pairs={{0,16},{4,20},{8,24},{12,28},{16,0},{20,4},{24,8},{28,12},{1,17},{... | collective-permute-start | bytes 786440 | tf_op jit(solution)/shard_map/ppermute | solution.py:441
  6.1 6.1 %pages.1 = (bf16[16,64,1024]{2,1,0:T(8,128)(2,1)}, bf16[8,64,512]{2,1,0:T(8,128)(2,1)}, bf16[8,64,512]{2,1,0:T(8,128)(2,1)}, bf16[128,2048]{1,0:T(8,128)(2,1)}, bf16[64,2048]{1,0:T(8,128)(2,1)}) custom-call(s32[32]{0:T(128)} %slot_of.6, s32[16,32]{1,0:T(8,128)} %bitcast.8, bf16[64,64,1024]{2,1,0:T(8,128)(2,1)} %pool.5, bf16[256,2048]{1,0:T(8,128)(2,1)} %refs_0_.1), custom_call_target="tpu_custom_call" | custom-call | flops 1 | bytes 1 | tf_op jit(solution)/shard_map/pages/pallas_call | solution.py:465
  12.2 1.1 %collective-permute-done.1.refs_4_ = bf16[64,2048]{1,0:T(8,128)(2,1)} collective-permute-done((bf16[64,2048]{1,0:T(8,128)(2,1)}, bf16[64,2048]{1,0:T(8,128)(2,1)}, u32[]{:S(2)}, u32[]{:S(2)}) %collective-permute-start.1) | collective-permute-done | bytes 262176 | tf_op jit(solution)/shard_map/ppermute | solution.py:441
  13.4 0.0 collective-permute-done.2.refs_1_
  13.4 0.0 collective-permute-start.3
  13.4 1.6 %collective-permute-start.5 = (bf16[8,64,512]{2,1,0:T(8,128)(2,1)}, bf16[8,64,512]{2,1,0:T(8,128)(2,1)}, u32[]{:S(2)}, u32[]{:S(2)}) collective-permute-start(bf16[8,64,512]{2,1,0:T(8,128)(2,1)} %get-tuple-element.43), channel_id=1, source_target_pairs={{0,28},{4,8},{8,4},{12,16},{16,12},{20,24},{24,20},{28,0},{1,29},{... | collective-permute-start | bytes 1572872 | tf_op jit(solution)/shard_map/ppermute | solution.py:441
  15.0 1.0 %collective-permute-start.4 = (bf16[8,64,512]{2,1,0:T(8,128)(2,1)}, bf16[8,64,512]{2,1,0:T(8,128)(2,1)}, u32[]{:S(2)}, u32[]{:S(2)}) collective-permute-start(bf16[8,64,512]{2,1,0:T(8,128)(2,1)} %get-tuple-element.41), channel_id=1, source_target_pairs={{0,28},{4,8},{8,4},{12,16},{16,12},{20,24},{24,20},{28,0},{1,29},{... | collective-permute-start | bytes 1572872 | tf_op jit(solution)/shard_map/ppermute | solution.py:441
  16.0 1.5 %collective-permute-start.6 = (bf16[64,2048]{1,0:T(8,128)(2,1)}, bf16[64,2048]{1,0:T(8,128)(2,1)}, u32[]{:S(2)}, u32[]{:S(2)}) collective-permute-start(bf16[64,2048]{1,0:T(8,128)(2,1)} %collective-permute-done.refs_2_), channel_id=1, source_target_pairs={{0,16},{4,20},{8,24},{12,28},{16,0},{20,4},{24,8},{28,12},{1,17},{... | collective-permute-start | bytes 786440 | tf_op jit(solution)/shard_map/ppermute | solution.py:441
  17.5 0.5 collective-permute-start.12
  18.0 12.9 %qkv.1 = (bf16[8,512,256]{2,1,0:T(8,128)(2,1)}, bf16[2,512,256]{2,1,0:T(8,128)(2,1)}, bf16[2,512,256]{2,1,0:T(8,128)(2,1)}) custom-call(s32[32]{0:T(128)} %slot_of.6, s32[32]{0:T(128)} %cached_len.5, f32[1,2048]{1,0:T(1,128)} %bitcast.11, f32[1,256]{1,0:T(1,128)} %bitcast.15, f32[1,256]{1,0:T(1,128)} %bitcast.16, bf16[512,2048]{1,0:T(8,128)(2,1)} %tokens_in.2, ...), custom_call_target="tpu_custom_call" | custom-call | flops 1 | bytes 1 | tf_op jit(solution)/shard_map/qkv/pallas_call | solution.py:497
  31.0 0.0 collective-permute-done.5.far_own
  31.0 1.6 %collective-permute-start.8 = (bf16[8,64,512]{2,1,0:T(8,128)(2,1)}, bf16[8,64,512]{2,1,0:T(8,128)(2,1)}, u32[]{:S(2)}, u32[]{:S(2)}) collective-permute-start(bf16[8,64,512]{2,1,0:T(8,128)(2,1)} %collective-permute-done.5.far_own), channel_id=1, source_target_pairs={{0,1},{1,0},{2,3},{3,2},{4,5},{5,4},{6,7},{7,6},{8,9},{9,8},{10,11... | collective-permute-start | bytes 1572872 | tf_op jit(solution)/shard_map/ppermute | solution.py:441
  32.6 7.7 %residual.1.residual_in = f32[512,2048]{1,0:T(8,128)} custom-call(f32[1,2048]{1,0:T(1,128)} %bitcast.12, bf16[64,2048]{1,0:T(8,128)(2,1)} %bitcast.7, bf16[64,2048]{1,0:T(8,128)(2,1)} %right.1, f32[1,2048]{1,0:T(1,128)} %bitcast.13, bf16[512,2048]{1,0:T(8,128)(2,1)} %tokens_in.2), custom_call_target="tpu_custom_call" | custom-call | flops 1 | bytes 1 | tf_op jit(solution)/shard_map/residual/pallas_call | solution.py:527
  40.4 0.5 collective-permute-start.7
  40.9 2.1 %collective-permute-start.16 = (bf16[64,2048]{1,0:T(8,128)(2,1)}, bf16[64,2048]{1,0:T(8,128)(2,1)}, u32[]{:S(2)}, u32[]{:S(2)}) collective-permute-start(bf16[64,2048]{1,0:T(8,128)(2,1)} %get-tuple-element.61), channel_id=1, source_target_pairs={{0,16},{4,20},{8,24},{12,28},{16,0},{20,4},{24,8},{28,12},{1,17},{... | collective-permute-start | bytes 786440 | tf_op jit(solution)/shard_map/ppermute | solution.py:441
  43.0 3.5 %collective-permute-done.12.refs_10_ = bf16[128,2048]{1,0:T(8,128)(2,1)} collective-permute-done((bf16[128,2048]{1,0:T(8,128)(2,1)}, bf16[128,2048]{1,0:T(8,128)(2,1)}, u32[]{:S(2)}, u32[]{:S(2)}) %collective-permute-start.12) | collective-permute-done | bytes 524320 | tf_op jit(solution)/shard_map/ppermute | solution.py:441
  46.5 0.5 collective-permute-start.10
  47.0 7.9 %attention.2.rest_0_ = bf16[8,512,256]{2,1,0:T(8,128)(2,1)} custom-call(s32[32]{0:T(128)} %slot_of.6, s32[32]{0:T(128)} %cached_len.5, s32[16,32]{1,0:T(8,128)} %bitcast.9, bf16[8,512,256]{2,1,0:T(8,128)(2,1)} %get-tuple-element.34.query_in, bf16[2,512,256]{2,1,0:T(8,128)(2,1)} %get-tuple-element.35.key_in, bf16[2,512,256]{2,1,0:T(8,128)(2,1)} %get-tuple-element.36.value_in, ...), custom_call_target="tpu_custom_call" | custom-call | flops 1 | bytes 1 | tf_op jit(solution)/shard_map/attention/pallas_call | solution.py:565
  55.0 0.5 collective-permute-done.7.far_other
  55.5 1.8 %collective-permute-start.18 = (bf16[128,2048]{1,0:T(8,128)(2,1)}, bf16[128,2048]{1,0:T(8,128)(2,1)}, u32[]{:S(2)}, u32[]{:S(2)}) collective-permute-start(bf16[128,2048]{1,0:T(8,128)(2,1)} %collective-permute-done.11.refs_6_), channel_id=1, source_target_pairs={{0,16},{4,20},{8,24},{12,28},{16,0},{20,4},{24,8},{28,12},{1,17},{... | collective-permute-start | bytes 1572872 | tf_op jit(solution)/shard_map/ppermute | solution.py:441
  57.3 0.2 collective-permute-start.14
  57.5 0.3 collective-permute-start.15
  57.8 1.9 %pad_maximum_fusion = bf16[128,2048]{1,0:T(8,128)(2,1)} fusion(bf16[64,2048]{1,0:T(8,128)(2,1)} %collective-permute-done.16.refs_12_, bf16[64,2048]{1,0:T(8,128)(2,1)} %get-tuple-element.61), kind=kLoop, calls=%fused_computation | loop fusion | flops 1048576 | bytes 1048576 | tf_op jit(solution)/shard_map/concatenate | solution.py:609
  59.6 1.2 %collective-permute-start.20 = (bf16[128,2048]{1,0:T(8,128)(2,1)}, bf16[128,2048]{1,0:T(8,128)(2,1)}, u32[]{:S(2)}, u32[]{:S(2)}) collective-permute-start(bf16[128,2048]{1,0:T(8,128)(2,1)} %pad_maximum_fusion), channel_id=1, source_target_pairs={{0,8},{4,12},{8,0},{12,4},{16,24},{20,28},{24,16},{28,20},{1,9},{5... | collective-permute-start | bytes 1572872 | tf_op jit(solution)/shard_map/ppermute | solution.py:441
  60.8 8.0 %attention.3.attended = bf16[8,512,256]{2,1,0:T(8,128)(2,1)} custom-call(s32[32]{0:T(128)} %slot_of.6, s32[32]{0:T(128)} %cached_len.5, s32[16,32]{1,0:T(8,128)} %bitcast.10, bf16[8,512,256]{2,1,0:T(8,128)(2,1)} %get-tuple-element.34.query_in, bf16[2,512,256]{2,1,0:T(8,128)(2,1)} %get-tuple-element.35.key_in, ...), custom_call_target="tpu_custom_call", output_to_operand_aliasing={{}: (10, {})} | custom-call | flops 1 | bytes 1 | tf_op jit(solution)/shard_map/attention/pallas_call | solution.py:565
  68.8 1.3 %collective-permute-done.18.refs_14_ = bf16[128,2048]{1,0:T(8,128)(2,1)} collective-permute-done((bf16[128,2048]{1,0:T(8,128)(2,1)}, bf16[128,2048]{1,0:T(8,128)(2,1)}, u32[]{:S(2)}, u32[]{:S(2)}) %collective-permute-start.18) | collective-permute-done | bytes 524320 | tf_op jit(solution)/shard_map/ppermute | solution.py:441
  70.2 3.9 %collective-permute-done.20.refs_16_ = bf16[128,2048]{1,0:T(8,128)(2,1)} collective-permute-done((bf16[128,2048]{1,0:T(8,128)(2,1)}, bf16[128,2048]{1,0:T(8,128)(2,1)}, u32[]{:S(2)}, u32[]{:S(2)}) %collective-permute-start.20) | collective-permute-done | bytes 524320 | tf_op jit(solution)/shard_map/ppermute | solution.py:441
  74.0 2.2 %collective-permute-done.21.refs_17_ = bf16[128,2048]{1,0:T(8,128)(2,1)} collective-permute-done((bf16[128,2048]{1,0:T(8,128)(2,1)}, bf16[128,2048]{1,0:T(8,128)(2,1)}, u32[]{:S(2)}, u32[]{:S(2)}) %collective-permute-start.21) | collective-permute-done | bytes 524320 | tf_op jit(solution)/shard_map/ppermute | solution.py:441
  76.3 11.3 %project.1 = bf16[512,2048]{1,0:T(8,128)(2,1)} custom-call(f32[1,2048]{1,0:T(1,128)} %bitcast.14, bf16[8,512,256]{2,1,0:T(8,128)(2,1)} %attention.3.attended, f32[512,2048]{1,0:T(8,128)} %residual.1.residual_in, bf16[256,2048]{1,0:T(8,128)(2,1)} %refs_0_.1, bf16[256,2048]{1,0:T(8,128)(2,1)} %collective-permute-done.2.refs_1_, ...), custom_call_target="tpu_custom_call" | custom-call | flops 1 | bytes 1 | tf_op jit(solution)/shard_map/project/pallas_call | solution.py:625
  (20 shorter events, 0.1 us)
Async XLA Ops:
  0.0 13.4 %collective-permute-start.2 = (bf16[256,2048]{1,0:T(8,128)(2,1)}, bf16[256,2048]{1,0:T(8,128)(2,1)}, u32[]{:S(2)}, u32[]{:S(2)}) collective-permute-start(bf16[256,2048]{1,0:T(8,128)(2,1)} %refs_0_.1), channel_id=1, source_target_pairs={{0,4},{4,0},{8,12},{12,8},{16,20},{20,16},{24,28},{28,24},{1,5},{5... | collective-permute-start | bytes 3145736 | tf_op jit(solution)/shard_map/ppermute | solution.py:441
  2.1 10.1 %collective-permute-start = (bf16[64,2048]{1,0:T(8,128)(2,1)}, bf16[64,2048]{1,0:T(8,128)(2,1)}, u32[]{:S(2)}, u32[]{:S(2)}) collective-permute-start(bf16[64,2048]{1,0:T(8,128)(2,1)} %slice.3), channel_id=1, source_target_pairs={{0,8},{4,12},{8,0},{12,4},{16,24},{20,28},{24,16},{28,20},{1,9},{5... | collective-permute-start | bytes 786440 | tf_op jit(solution)/shard_map/ppermute | solution.py:441
  4.6 8.8 %collective-permute-start.1 = (bf16[64,2048]{1,0:T(8,128)(2,1)}, bf16[64,2048]{1,0:T(8,128)(2,1)}, u32[]{:S(2)}, u32[]{:S(2)}) collective-permute-start(bf16[64,2048]{1,0:T(8,128)(2,1)} %slice.3), channel_id=1, source_target_pairs={{0,16},{4,20},{8,24},{12,28},{16,0},{20,4},{24,8},{28,12},{1,17},{... | collective-permute-start | bytes 786440 | tf_op jit(solution)/shard_map/ppermute | solution.py:441
  13.4 19.3 %collective-permute-start.3 = (bf16[16,64,1024]{2,1,0:T(8,128)(2,1)}, bf16[16,64,1024]{2,1,0:T(8,128)(2,1)}, u32[]{:S(2)}, u32[]{:S(2)}) collective-permute-start(bf16[16,64,1024]{2,1,0:T(8,128)(2,1)} %get-tuple-element.39), channel_id=1, source_target_pairs={{0,4},{4,0},{8,12},{12,8},{16,20},{20,16},{24,28},{28,24},{1,5},{5... | collective-permute-start | bytes 6291464 | tf_op jit(solution)/shard_map/ppermute | solution.py:441
  13.4 17.6 %collective-permute-start.5 = (bf16[8,64,512]{2,1,0:T(8,128)(2,1)}, bf16[8,64,512]{2,1,0:T(8,128)(2,1)}, u32[]{:S(2)}, u32[]{:S(2)}) collective-permute-start(bf16[8,64,512]{2,1,0:T(8,128)(2,1)} %get-tuple-element.43), channel_id=1, source_target_pairs={{0,28},{4,8},{8,4},{12,16},{16,12},{20,24},{24,20},{28,0},{1,29},{... | collective-permute-start | bytes 1572872 | tf_op jit(solution)/shard_map/ppermute | solution.py:441
  15.0 25.4 %collective-permute-start.4 = (bf16[8,64,512]{2,1,0:T(8,128)(2,1)}, bf16[8,64,512]{2,1,0:T(8,128)(2,1)}, u32[]{:S(2)}, u32[]{:S(2)}) collective-permute-start(bf16[8,64,512]{2,1,0:T(8,128)(2,1)} %get-tuple-element.41), channel_id=1, source_target_pairs={{0,28},{4,8},{8,4},{12,16},{16,12},{20,24},{24,20},{28,0},{1,29},{... | collective-permute-start | bytes 1572872 | tf_op jit(solution)/shard_map/ppermute | solution.py:441
  16.0 16.6 %collective-permute-start.6 = (bf16[64,2048]{1,0:T(8,128)(2,1)}, bf16[64,2048]{1,0:T(8,128)(2,1)}, u32[]{:S(2)}, u32[]{:S(2)}) collective-permute-start(bf16[64,2048]{1,0:T(8,128)(2,1)} %collective-permute-done.refs_2_), channel_id=1, source_target_pairs={{0,16},{4,20},{8,24},{12,28},{16,0},{20,4},{24,8},{28,12},{1,17},{... | collective-permute-start | bytes 786440 | tf_op jit(solution)/shard_map/ppermute | solution.py:441
  17.5 29.0 %collective-permute-start.12 = (bf16[128,2048]{1,0:T(8,128)(2,1)}, bf16[128,2048]{1,0:T(8,128)(2,1)}, u32[]{:S(2)}, u32[]{:S(2)}) collective-permute-start(bf16[128,2048]{1,0:T(8,128)(2,1)} %get-tuple-element.52), channel_id=1, source_target_pairs={{0,16},{4,20},{8,24},{12,28},{16,0},{20,4},{24,8},{28,12},{1,17},{... | collective-permute-start | bytes 1572872 | tf_op jit(solution)/shard_map/ppermute | solution.py:441
  31.0 15.6 %collective-permute-start.8 = (bf16[8,64,512]{2,1,0:T(8,128)(2,1)}, bf16[8,64,512]{2,1,0:T(8,128)(2,1)}, u32[]{:S(2)}, u32[]{:S(2)}) collective-permute-start(bf16[8,64,512]{2,1,0:T(8,128)(2,1)} %collective-permute-done.5.far_own), channel_id=1, source_target_pairs={{0,1},{1,0},{2,3},{3,2},{4,5},{5,4},{6,7},{7,6},{8,9},{9,8},{10,11... | collective-permute-start | bytes 1572872 | tf_op jit(solution)/shard_map/ppermute | solution.py:441
  40.4 15.1 %collective-permute-start.7 = (bf16[8,64,512]{2,1,0:T(8,128)(2,1)}, bf16[8,64,512]{2,1,0:T(8,128)(2,1)}, u32[]{:S(2)}, u32[]{:S(2)}) collective-permute-start(bf16[8,64,512]{2,1,0:T(8,128)(2,1)} %collective-permute-done.4.far_own), channel_id=1, source_target_pairs={{0,1},{1,0},{2,3},{3,2},{4,5},{5,4},{6,7},{7,6},{8,9},{9,8},{10,11... | collective-permute-start | bytes 1572872 | tf_op jit(solution)/shard_map/ppermute | solution.py:441
  40.9 14.6 %collective-permute-start.11 = (bf16[128,2048]{1,0:T(8,128)(2,1)}, bf16[128,2048]{1,0:T(8,128)(2,1)}, u32[]{:S(2)}, u32[]{:S(2)}) collective-permute-start(bf16[128,2048]{1,0:T(8,128)(2,1)} %get-tuple-element.52), channel_id=1, source_target_pairs={{0,8},{4,12},{8,0},{12,4},{16,24},{20,28},{24,16},{28,20},{1,9},{5... | collective-permute-start | bytes 1572872 | tf_op jit(solution)/shard_map/ppermute | solution.py:441
  40.9 16.3 %collective-permute-start.16 = (bf16[64,2048]{1,0:T(8,128)(2,1)}, bf16[64,2048]{1,0:T(8,128)(2,1)}, u32[]{:S(2)}, u32[]{:S(2)}) collective-permute-start(bf16[64,2048]{1,0:T(8,128)(2,1)} %get-tuple-element.61), channel_id=1, source_target_pairs={{0,16},{4,20},{8,24},{12,28},{16,0},{20,4},{24,8},{28,12},{1,17},{... | collective-permute-start | bytes 786440 | tf_op jit(solution)/shard_map/ppermute | solution.py:441
  46.5 11.0 %collective-permute-start.9 = (bf16[64,2048]{1,0:T(8,128)(2,1)}, bf16[64,2048]{1,0:T(8,128)(2,1)}, u32[]{:S(2)}, u32[]{:S(2)}) collective-permute-start(bf16[64,2048]{1,0:T(8,128)(2,1)} %collective-permute-done.refs_2_), channel_id=1, source_target_pairs={{0,4},{4,0},{8,12},{12,8},{16,20},{20,16},{24,28},{28,24},{1,5},{5... | collective-permute-start | bytes 786440 | tf_op jit(solution)/shard_map/ppermute | solution.py:441
  46.5 13.1 %collective-permute-start.10 = (bf16[64,2048]{1,0:T(8,128)(2,1)}, bf16[64,2048]{1,0:T(8,128)(2,1)}, u32[]{:S(2)}, u32[]{:S(2)}) collective-permute-start(bf16[64,2048]{1,0:T(8,128)(2,1)} %collective-permute-done.1.refs_4_), channel_id=1, source_target_pairs={{0,4},{4,0},{8,12},{12,8},{16,20},{20,16},{24,28},{28,24},{1,5},{5... | collective-permute-start | bytes 786440 | tf_op jit(solution)/shard_map/ppermute | solution.py:441
  55.5 13.3 %collective-permute-start.13 = (bf16[128,2048]{1,0:T(8,128)(2,1)}, bf16[128,2048]{1,0:T(8,128)(2,1)}, u32[]{:S(2)}, u32[]{:S(2)}) collective-permute-start(bf16[128,2048]{1,0:T(8,128)(2,1)} %collective-permute-done.11.refs_6_), channel_id=1, source_target_pairs={{0,4},{4,0},{8,12},{12,8},{16,20},{20,16},{24,28},{28,24},{1,5},{5... | collective-permute-start | bytes 1572872 | tf_op jit(solution)/shard_map/ppermute | solution.py:441
  55.5 14.7 %collective-permute-start.18 = (bf16[128,2048]{1,0:T(8,128)(2,1)}, bf16[128,2048]{1,0:T(8,128)(2,1)}, u32[]{:S(2)}, u32[]{:S(2)}) collective-permute-start(bf16[128,2048]{1,0:T(8,128)(2,1)} %collective-permute-done.11.refs_6_), channel_id=1, source_target_pairs={{0,16},{4,20},{8,24},{12,28},{16,0},{20,4},{24,8},{28,12},{1,17},{... | collective-permute-start | bytes 1572872 | tf_op jit(solution)/shard_map/ppermute | solution.py:441
  57.3 3.6 %collective-permute-start.14 = (bf16[64,2048]{1,0:T(8,128)(2,1)}, bf16[64,2048]{1,0:T(8,128)(2,1)}, u32[]{:S(2)}, u32[]{:S(2)}) collective-permute-start(bf16[64,2048]{1,0:T(8,128)(2,1)} %collective-permute-done.6.refs_8_), channel_id=1, source_target_pairs={{0,4},{4,0},{8,12},{12,8},{16,20},{20,16},{24,28},{28,24},{1,5},{5... | collective-permute-start | bytes 786440 | tf_op jit(solution)/shard_map/ppermute | solution.py:441
  57.5 11.3 %collective-permute-start.15 = (bf16[128,2048]{1,0:T(8,128)(2,1)}, bf16[128,2048]{1,0:T(8,128)(2,1)}, u32[]{:S(2)}, u32[]{:S(2)}) collective-permute-start(bf16[128,2048]{1,0:T(8,128)(2,1)} %collective-permute-done.12.refs_10_), channel_id=1, source_target_pairs={{0,4},{4,0},{8,12},{12,8},{16,20},{20,16},{24,28},{28,24},{1,5},{5... | collective-permute-start | bytes 1572872 | tf_op jit(solution)/shard_map/ppermute | solution.py:441
  59.6 14.4 %collective-permute-start.20 = (bf16[128,2048]{1,0:T(8,128)(2,1)}, bf16[128,2048]{1,0:T(8,128)(2,1)}, u32[]{:S(2)}, u32[]{:S(2)}) collective-permute-start(bf16[128,2048]{1,0:T(8,128)(2,1)} %pad_maximum_fusion), channel_id=1, source_target_pairs={{0,8},{4,12},{8,0},{12,4},{16,24},{20,28},{24,16},{28,20},{1,9},{5... | collective-permute-start | bytes 1572872 | tf_op jit(solution)/shard_map/ppermute | solution.py:441
  60.8 8.0 %collective-permute-start.17 = (bf16[64,2048]{1,0:T(8,128)(2,1)}, bf16[64,2048]{1,0:T(8,128)(2,1)}, u32[]{:S(2)}, u32[]{:S(2)}) collective-permute-start(bf16[64,2048]{1,0:T(8,128)(2,1)} %collective-permute-done.16.refs_12_), channel_id=1, source_target_pairs={{0,4},{4,0},{8,12},{12,8},{16,20},{20,16},{24,28},{28,24},{1,5},{5... | collective-permute-start | bytes 786440 | tf_op jit(solution)/shard_map/ppermute | solution.py:441
  70.2 3.9 %collective-permute-start.19 = (bf16[128,2048]{1,0:T(8,128)(2,1)}, bf16[128,2048]{1,0:T(8,128)(2,1)}, u32[]{:S(2)}, u32[]{:S(2)}) collective-permute-start(bf16[128,2048]{1,0:T(8,128)(2,1)} %collective-permute-done.18.refs_14_), channel_id=1, source_target_pairs={{0,4},{4,0},{8,12},{12,8},{16,20},{20,16},{24,28},{28,24},{1,5},{5... | collective-permute-start | bytes 1572872 | tf_op jit(solution)/shard_map/ppermute | solution.py:441
  74.0 2.3 %collective-permute-start.21 = (bf16[128,2048]{1,0:T(8,128)(2,1)}, bf16[128,2048]{1,0:T(8,128)(2,1)}, u32[]{:S(2)}, u32[]{:S(2)}) collective-permute-start(bf16[128,2048]{1,0:T(8,128)(2,1)} %collective-permute-done.20.refs_16_), channel_id=1, source_target_pairs={{0,4},{4,0},{8,12},{12,8},{16,20},{20,16},{24,28},{28,24},{1,5},{5... | collective-permute-start | bytes 1572872 | tf_op jit(solution)/shard_map/ppermute | solution.py:441

commit v4 on v3

--- a/solution.py
+++ b/solution.py
@@ -245,6 +245,18 @@
     kv, slot_of, cached_len, page_table_in, query_in, key_in, value_in, pool, near, far_own,
     far_other, *rest,
 ):
+    joined = None
+    if kv == 0:
+        (own_last, across_last, out_in, joined), rest = rest[:4], (None, *rest[4:])
+        held, join_sems = rest[-2:]
+        rest = (out_in, *rest[1:-2])
+        quarter = own_last.shape[0]
+        joins = [
+            pltpu.make_async_copy(w, held.at[i * quarter : (i + 1) * quarter], join_sems.at[i])
+            for i, w in enumerate((own_last, across_last))
+        ]
+        for copy in joins:
+            copy.start()
     out_in, (page_table, query, key, value, out, stored, sems, in_sems, out_sems) = (
         rest[-10],
         rest[-9:],
@@ -340,6 +352,11 @@
     def send(h):
         return pltpu.make_async_copy(out.at[h], out_in.at[kv * per_kv + h], out_sems.at[h])
 
+    if joined is not None:
+        for copy in joins:
+            copy.wait()
+        join = pltpu.make_async_copy(held, joined, join_sems.at[2])
+        join.start()
     items = [(h, t) for h in range(per_kv) for t in range(rows // tile)]
     current = scores(*items[0])
     for i, (h, t) in enumerate(items):
@@ -350,6 +367,8 @@
             send(h).start()
     for h in range(per_kv):
         send(h).wait()
+    if joined is not None:
+        join.wait()
 
 
 def output_kernel(places, post_gain, attended, residual_in, *refs):
@@ -395,10 +414,12 @@
         res_copies.append(
             pltpu.make_async_copy(residual_in.at[at], residual.at[at], res_sems.at[t])
         )
-    for copy in copies[0] + copies[1]:
+    for copy in copies[0]:
         copy.start()
     for copy in lhs_copies:
         copy.wait()
+    for copy in copies[1]:
+        copy.start()
     squares = 0.0
     for n in range(width // wide):
         columns = slice(n * wide, (n + 1) * wide)
@@ -488,8 +509,8 @@
     far_out = [after(far, *early_done) for far in far_out]
     far_own = [send(far, "req", far_pairs) for far in far_out]
     middle, last = (after(w, *early_done) for w in (middle, last))
-    middles = {far_hop: send(middle, "req", flip(far_hop))}
     lasts = {far_hop: send(last, "req", flip(far_hop))}
+    middles = {}
     relays = {k: send(after(first[k], *early_done), "req", flip(far_hop)) for k in hops}
 
     table = rope_table(page_count * page_rows + CH)
@@ -548,6 +569,7 @@
         shared.append(send(after(block, query), "req", near_pairs))
         pieces += [(k, 0, block), (k + 1, 0, shared[-1])]
     far_other += [send(after(far, residual), "head", side) for far in far_own[1:]]
+    middles[far_hop] = send(after(middle, residual, lasts[far_hop]), "req", flip(far_hop))
     for k in hops:
         middles[k] = send(after(middle, residual, *far_own), "req", flip(k))
 
@@ -561,12 +583,16 @@
 
     per_kv = NH // KVH
     def attend(g, earlier=None):
-        more = [] if earlier is None else [earlier]
+        first_call = earlier is None
+        more = [last, lasts[far_hop]] if first_call else [earlier]
+        joined = (2 * quarter, width)
         return pl.pallas_call(
             functools.partial(attention_kernel, g),
-            out_shape=heads_shape(NH),
+            out_shape=(heads_shape(NH), jax.ShapeDtypeStruct(joined, jnp.bfloat16))
+            if first_call
+            else heads_shape(NH),
             in_specs=[SMEM] * 2 + [ANY] * (8 + len(more)),
-            out_specs=ANY,
+            out_specs=(ANY, ANY) if first_call else ANY,
             scratch_shapes=[
                 pltpu.SMEM(pages_of.shape, jnp.int32),
                 pltpu.VMEM((per_kv, rows, HD), jnp.bfloat16),
@@ -577,8 +603,13 @@
                 pltpu.SemaphoreType.DMA((page_count,)),
                 pltpu.SemaphoreType.DMA((4,)),
                 pltpu.SemaphoreType.DMA((per_kv,)),
-            ],
-            input_output_aliases={10: 0} if more else {},
+            ]
+            + (
+                [pltpu.VMEM(joined, jnp.bfloat16), pltpu.SemaphoreType.DMA((3,))]
+                if first_call
+                else []
+            ),
+            input_output_aliases={} if first_call else {10: 0},
             compiler_params=params(),
             cost_estimate=SHORT,
             name="attention",
@@ -587,7 +618,8 @@
             near, far_own[g], far_other[g], *more,
         )
 
-    attended = [attend(0)]
+    first_heads, joined = attend(0)
+    attended = [first_heads]
     late = []
     ahead = after(attended[0], *far_other[1:], *middles.values())
     swapped = []
@@ -604,12 +636,11 @@
         here = after(middles[k], ahead)
         both_cores(k, quarter, here)
         both_cores(k + far_hop, 0, after(relays[k], ahead))
-        late.append((k + far_hop, quarter, send(here, "req", flip(far_hop))))
-        here = after(lasts[far_hop], ahead)
-        both = send(jnp.concatenate([after(last, ahead), here], axis=0), "req", flip(k))
+        late.append((k + far_hop, quarter, send(after(middles[k], first_heads), "req", flip(far_hop))))
+        both = send(joined, "req", flip(k))
         late.append(((k, k + far_hop), 3 * quarter, both))
-    for offset, block in ((quarter, middles[far_hop]), (3 * quarter, lasts[far_hop])):
-        both_cores(far_hop, offset, after(block, ahead))
+    both_cores(far_hop, 3 * quarter, lasts[far_hop])
+    both_cores(far_hop, quarter, after(middles[far_hop], ahead))
     for g in range(1, KVH):
         attended.append(attend(g, attended[-1]))
     earlier = [attended[-1], *swapped, *shared]

time: 88.1 us -> 85.5 us (0.970)
  other arithmetic: 1.87 us -> 0 us
  waiting for transfers between devices: 12.6 us -> 11.6 us
    concatenate x1 -> x0, other arithmetic: 1.87 us -> none  [shards(): jnp.concatenate([after(last, ahead), here], axis=0)]
    ppermute x22, waiting for transfers between devices: 12.6 us -> 11.6 us  [send(): return lax.ppermute(block, axis, pairs)]
  transfers between devices with their start and end apart: 22 -> 22, of which waited for: 6 -> 6; matrix products, arithmetic and copies ran while one was open for 4% -> 2% of each run, Pallas kernels for 49% -> 50%
where the time goes in v4:
time: 85.5 us; the launch traced here: 85 us
  Pallas kernels  53.4 us (62%)
  starting transfers between devices  18 us (21%)
  waiting for transfers between devices  11.6 us (14%)
  local copies, waits for them, and re-layouts  1.67 us (2%)
    ppermute x22, starting transfers between devices, send(): return lax.ppermute(block, axis, pairs)  18 us
    pallas_call x2, Pallas kernels, attend(): pl.pallas_call(functools.partial(attention_kernel, g), out_shape=(heads_s...  16 us
    pallas_call x1, Pallas kernels, shards(): pl.pallas_call(qkv_kernel, out_shape=(heads_shape(NH), heads_shape(KVH),...  12.9 us
    ppermute x22, waiting for transfers between devices, send(): return lax.ppermute(block, axis, pairs)  11.6 us
    pallas_call x1, Pallas kernels, shards(): pl.pallas_call(functools.partial(output_kernel, places), out_shape=jax.Sh...  10.7 us
    pallas_call x1, Pallas kernels, shards(): pl.pallas_call(residual_kernel, out_shape=jax.ShapeDtypeStruct((rows, wid...  7.74 us
    pallas_call x1, Pallas kernels, shards(): pl.pallas_call(pages_kernel, out_shape=(jax.ShapeDtypeStruct(near_shape,...  6.12 us
  transfers between devices with their start and end apart: 22, of which 6 were waited for; matrix products, arithmetic and copies ran while one was open for 2% of the time, Pallas kernels for 50%

profile of v4, /device:TPU:0, one launch (start us, length us, event | category | flops | bytes accessed | tf_op | source)
XLA Modules:
  0.0 85.0 jit_solution(9071949768210337485)
XLA Ops:
  0.0 0.5 collective-permute-start.2
  0.5 1.7 %slice.3 = bf16[64,2048]{1,0:T(8,128)(2,1)} slice(bf16[256,2048]{1,0:T(8,128)(2,1)} %refs_0_.1), slice={[0:64], [0:2048]} | slice | bytes 524288 | tf_op jit(solution)/shard_map/slice | solution.py:472
  2.1 2.5 %collective-permute-start = (bf16[64,2048]{1,0:T(8,128)(2,1)}, bf16[64,2048]{1,0:T(8,128)(2,1)}, u32[]{:S(2)}, u32[]{:S(2)}) collective-permute-start(bf16[64,2048]{1,0:T(8,128)(2,1)} %slice.3), channel_id=1, source_target_pairs={{0,8},{4,12},{8,0},{12,4},{16,24},{20,28},{24,16},{28,20},{1,9},{5... | collective-permute-start | bytes 786440 | tf_op jit(solution)/shard_map/ppermute | solution.py:462
  4.6 1.5 %collective-permute-start.1 = (bf16[64,2048]{1,0:T(8,128)(2,1)}, bf16[64,2048]{1,0:T(8,128)(2,1)}, u32[]{:S(2)}, u32[]{:S(2)}) collective-permute-start(bf16[64,2048]{1,0:T(8,128)(2,1)} %slice.3), channel_id=1, source_target_pairs={{0,16},{4,20},{8,24},{12,28},{16,0},{20,4},{24,8},{28,12},{1,17},{... | collective-permute-start | bytes 786440 | tf_op jit(solution)/shard_map/ppermute | solution.py:462
  6.1 6.1 %pages.1 = (bf16[16,64,1024]{2,1,0:T(8,128)(2,1)}, bf16[8,64,512]{2,1,0:T(8,128)(2,1)}, bf16[8,64,512]{2,1,0:T(8,128)(2,1)}, bf16[128,2048]{1,0:T(8,128)(2,1)}, bf16[64,2048]{1,0:T(8,128)(2,1)}) custom-call(s32[32]{0:T(128)} %slot_of.6, s32[16,32]{1,0:T(8,128)} %bitcast.8, bf16[64,64,1024]{2,1,0:T(8,128)(2,1)} %pool.5, bf16[256,2048]{1,0:T(8,128)(2,1)} %refs_0_.1), custom_call_target="tpu_custom_call" | custom-call | flops 1 | bytes 1 | tf_op jit(solution)/shard_map/pages/pallas_call | solution.py:486
  12.3 0.0 collective-permute-done.refs_2_
  12.3 1.1 %collective-permute-done.1.refs_4_ = bf16[64,2048]{1,0:T(8,128)(2,1)} collective-permute-done((bf16[64,2048]{1,0:T(8,128)(2,1)}, bf16[64,2048]{1,0:T(8,128)(2,1)}, u32[]{:S(2)}, u32[]{:S(2)}) %collective-permute-start.1) | collective-permute-done | bytes 262176 | tf_op jit(solution)/shard_map/ppermute | solution.py:462
  13.4 0.0 collective-permute-done.2.refs_1_
  13.4 0.0 collective-permute-start.3
  13.4 1.6 %collective-permute-start.5 = (bf16[8,64,512]{2,1,0:T(8,128)(2,1)}, bf16[8,64,512]{2,1,0:T(8,128)(2,1)}, u32[]{:S(2)}, u32[]{:S(2)}) collective-permute-start(bf16[8,64,512]{2,1,0:T(8,128)(2,1)} %get-tuple-element.45), channel_id=1, source_target_pairs={{0,28},{4,8},{8,4},{12,16},{16,12},{20,24},{24,20},{28,0},{1,29},{... | collective-permute-start | bytes 1572872 | tf_op jit(solution)/shard_map/ppermute | solution.py:462
  15.0 1.0 %collective-permute-start.4 = (bf16[8,64,512]{2,1,0:T(8,128)(2,1)}, bf16[8,64,512]{2,1,0:T(8,128)(2,1)}, u32[]{:S(2)}, u32[]{:S(2)}) collective-permute-start(bf16[8,64,512]{2,1,0:T(8,128)(2,1)} %get-tuple-element.43), channel_id=1, source_target_pairs={{0,28},{4,8},{8,4},{12,16},{16,12},{20,24},{24,20},{28,0},{1,29},{... | collective-permute-start | bytes 1572872 | tf_op jit(solution)/shard_map/ppermute | solution.py:462
  16.0 1.5 %collective-permute-start.6 = (bf16[64,2048]{1,0:T(8,128)(2,1)}, bf16[64,2048]{1,0:T(8,128)(2,1)}, u32[]{:S(2)}, u32[]{:S(2)}) collective-permute-start(bf16[64,2048]{1,0:T(8,128)(2,1)} %collective-permute-done.refs_2_), channel_id=1, source_target_pairs={{0,16},{4,20},{8,24},{12,28},{16,0},{20,4},{24,8},{28,12},{1,17},{... | collective-permute-start | bytes 786440 | tf_op jit(solution)/shard_map/ppermute | solution.py:462
  17.5 0.5 collective-permute-start.9
  18.0 12.9 %qkv.1 = (bf16[8,512,256]{2,1,0:T(8,128)(2,1)}, bf16[2,512,256]{2,1,0:T(8,128)(2,1)}, bf16[2,512,256]{2,1,0:T(8,128)(2,1)}) custom-call(s32[32]{0:T(128)} %slot_of.6, s32[32]{0:T(128)} %cached_len.5, f32[1,2048]{1,0:T(1,128)} %bitcast.11, f32[1,256]{1,0:T(1,128)} %bitcast.15, f32[1,256]{1,0:T(1,128)} %bitcast.16, bf16[512,2048]{1,0:T(8,128)(2,1)} %tokens_in.2, ...), custom_call_target="tpu_custom_call" | custom-call | flops 1 | bytes 1 | tf_op jit(solution)/shard_map/qkv/pallas_call | solution.py:518
  31.0 1.9 %collective-permute-start.8 = (bf16[8,64,512]{2,1,0:T(8,128)(2,1)}, bf16[8,64,512]{2,1,0:T(8,128)(2,1)}, u32[]{:S(2)}, u32[]{:S(2)}) collective-permute-start(bf16[8,64,512]{2,1,0:T(8,128)(2,1)} %collective-permute-done.5.far_own), channel_id=1, source_target_pairs={{0,1},{1,0},{2,3},{3,2},{4,5},{5,4},{6,7},{7,6},{8,9},{9,8},{10,11... | collective-permute-start | bytes 1572872 | tf_op jit(solution)/shard_map/ppermute | solution.py:462
  32.9 7.7 %residual.1.residual_in = f32[512,2048]{1,0:T(8,128)} custom-call(f32[1,2048]{1,0:T(1,128)} %bitcast.12, bf16[64,2048]{1,0:T(8,128)(2,1)} %bitcast.7, bf16[64,2048]{1,0:T(8,128)(2,1)} %right.1, f32[1,2048]{1,0:T(1,128)} %bitcast.13, bf16[512,2048]{1,0:T(8,128)(2,1)} %tokens_in.2), custom_call_target="tpu_custom_call" | custom-call | flops 1 | bytes 1 | tf_op jit(solution)/shard_map/residual/pallas_call | solution.py:548
  40.7 1.4 %collective-permute-start.13 = (bf16[128,2048]{1,0:T(8,128)(2,1)}, bf16[128,2048]{1,0:T(8,128)(2,1)}, u32[]{:S(2)}, u32[]{:S(2)}) collective-permute-start(bf16[128,2048]{1,0:T(8,128)(2,1)} %get-tuple-element.58), channel_id=1, source_target_pairs={{0,16},{4,20},{8,24},{12,28},{16,0},{20,4},{24,8},{28,12},{1,17},{... | collective-permute-start | bytes 1572872 | tf_op jit(solution)/shard_map/ppermute | solution.py:462
  42.1 0.9 %collective-permute-start.12 = (bf16[128,2048]{1,0:T(8,128)(2,1)}, bf16[128,2048]{1,0:T(8,128)(2,1)}, u32[]{:S(2)}, u32[]{:S(2)}) collective-permute-start(bf16[128,2048]{1,0:T(8,128)(2,1)} %get-tuple-element.58), channel_id=1, source_target_pairs={{0,8},{4,12},{8,0},{12,4},{16,24},{20,28},{24,16},{28,20},{1,9},{5... | collective-permute-start | bytes 1572872 | tf_op jit(solution)/shard_map/ppermute | solution.py:462
  43.0 1.6 %collective-permute-start.7 = (bf16[8,64,512]{2,1,0:T(8,128)(2,1)}, bf16[8,64,512]{2,1,0:T(8,128)(2,1)}, u32[]{:S(2)}, u32[]{:S(2)}) collective-permute-start(bf16[8,64,512]{2,1,0:T(8,128)(2,1)} %collective-permute-done.4.far_own), channel_id=1, source_target_pairs={{0,1},{1,0},{2,3},{3,2},{4,5},{5,4},{6,7},{7,6},{8,9},{9,8},{10,11... | collective-permute-start | bytes 1572872 | tf_op jit(solution)/shard_map/ppermute | solution.py:462
  44.6 0.5 collective-permute-start.11
  45.1 8.0 %attention.2 = (bf16[8,512,256]{2,1,0:T(8,128)(2,1)}, bf16[128,2048]{1,0:T(8,128)(2,1)}) custom-call(s32[32]{0:T(128)} %slot_of.6, s32[32]{0:T(128)} %cached_len.5, s32[16,32]{1,0:T(8,128)} %bitcast.9, bf16[8,512,256]{2,1,0:T(8,128)(2,1)} %get-tuple-element.36.query_in, bf16[2,512,256]{2,1,0:T(8,128)(2,1)} %get-tuple-element.37.key_in, ...), custom_call_target="tpu_custom_call" | custom-call | flops 1 | bytes 1 | tf_op jit(solution)/shard_map/attention/pallas_call | solution.py:589
  53.1 0.6 collective-permute-done.13.refs_12_
  53.7 1.8 %collective-permute-done.12.refs_6_ = bf16[128,2048]{1,0:T(8,128)(2,1)} collective-permute-done((bf16[128,2048]{1,0:T(8,128)(2,1)}, bf16[128,2048]{1,0:T(8,128)(2,1)}, u32[]{:S(2)}, u32[]{:S(2)}) %collective-permute-start.12) | collective-permute-done | bytes 524320 | tf_op jit(solution)/shard_map/ppermute | solution.py:462
  55.5 1.7 %collective-permute-start.20 = (bf16[128,2048]{1,0:T(8,128)(2,1)}, bf16[128,2048]{1,0:T(8,128)(2,1)}, u32[]{:S(2)}, u32[]{:S(2)}) collective-permute-start(bf16[128,2048]{1,0:T(8,128)(2,1)} %get-tuple-element.65), channel_id=1, source_target_pairs={{0,8},{4,12},{8,0},{12,4},{16,24},{20,28},{24,16},{28,20},{1,9},{5... | collective-permute-start | bytes 1572872 | tf_op jit(solution)/shard_map/ppermute | solution.py:462
  57.2 0.5 collective-permute-start.17
  57.7 0.3 collective-permute-start.18
  58.0 8.0 %attention.3.attended = bf16[8,512,256]{2,1,0:T(8,128)(2,1)} custom-call(s32[32]{0:T(128)} %slot_of.6, s32[32]{0:T(128)} %cached_len.5, s32[16,32]{1,0:T(8,128)} %bitcast.10, bf16[8,512,256]{2,1,0:T(8,128)(2,1)} %get-tuple-element.36.query_in, bf16[2,512,256]{2,1,0:T(8,128)(2,1)} %get-tuple-element.37.key_in, ...), custom_call_target="tpu_custom_call", output_to_operand_aliasing={{}: (10, {})} | custom-call | flops 1 | bytes 1 | tf_op jit(solution)/shard_map/attention/pallas_call | solution.py:589
  66.0 2.8 %collective-permute-done.20.refs_16_ = bf16[128,2048]{1,0:T(8,128)(2,1)} collective-permute-done((bf16[128,2048]{1,0:T(8,128)(2,1)}, bf16[128,2048]{1,0:T(8,128)(2,1)}, u32[]{:S(2)}, u32[]{:S(2)}) %collective-permute-start.20) | collective-permute-done | bytes 524320 | tf_op jit(solution)/shard_map/ppermute | solution.py:462
  68.8 0.1 collective-permute-start.21
  68.9 3.0 %collective-permute-done.18.refs_14_ = bf16[128,2048]{1,0:T(8,128)(2,1)} collective-permute-done((bf16[128,2048]{1,0:T(8,128)(2,1)}, bf16[128,2048]{1,0:T(8,128)(2,1)}, u32[]{:S(2)}, u32[]{:S(2)}) %collective-permute-start.18) | collective-permute-done | bytes 524320 | tf_op jit(solution)/shard_map/ppermute | solution.py:462
  71.9 2.2 %collective-permute-done.19.refs_15_ = bf16[128,2048]{1,0:T(8,128)(2,1)} collective-permute-done((bf16[128,2048]{1,0:T(8,128)(2,1)}, bf16[128,2048]{1,0:T(8,128)(2,1)}, u32[]{:S(2)}, u32[]{:S(2)}) %collective-permute-start.19) | collective-permute-done | bytes 524320 | tf_op jit(solution)/shard_map/ppermute | solution.py:462
  74.2 10.7 %project.1 = bf16[512,2048]{1,0:T(8,128)(2,1)} custom-call(f32[1,2048]{1,0:T(1,128)} %bitcast.14, bf16[8,512,256]{2,1,0:T(8,128)(2,1)} %attention.3.attended, f32[512,2048]{1,0:T(8,128)} %residual.1.residual_in, bf16[256,2048]{1,0:T(8,128)(2,1)} %refs_0_.1, bf16[256,2048]{1,0:T(8,128)(2,1)} %collective-permute-done.2.refs_1_, ...), custom_call_target="tpu_custom_call" | custom-call | flops 1 | bytes 1 | tf_op jit(solution)/shard_map/project/pallas_call | solution.py:656
  (19 shorter events, 0.1 us)
Async XLA Ops:
  0.0 13.4 %collective-permute-start.2 = (bf16[256,2048]{1,0:T(8,128)(2,1)}, bf16[256,2048]{1,0:T(8,128)(2,1)}, u32[]{:S(2)}, u32[]{:S(2)}) collective-permute-start(bf16[256,2048]{1,0:T(8,128)(2,1)} %refs_0_.1), channel_id=1, source_target_pairs={{0,4},{4,0},{8,12},{12,8},{16,20},{20,16},{24,28},{28,24},{1,5},{5... | collective-permute-start | bytes 3145736 | tf_op jit(solution)/shard_map/ppermute | solution.py:462
  2.1 10.1 %collective-permute-start = (bf16[64,2048]{1,0:T(8,128)(2,1)}, bf16[64,2048]{1,0:T(8,128)(2,1)}, u32[]{:S(2)}, u32[]{:S(2)}) collective-permute-start(bf16[64,2048]{1,0:T(8,128)(2,1)} %slice.3), channel_id=1, source_target_pairs={{0,8},{4,12},{8,0},{12,4},{16,24},{20,28},{24,16},{28,20},{1,9},{5... | collective-permute-start | bytes 786440 | tf_op jit(solution)/shard_map/ppermute | solution.py:462
  4.6 8.8 %collective-permute-start.1 = (bf16[64,2048]{1,0:T(8,128)(2,1)}, bf16[64,2048]{1,0:T(8,128)(2,1)}, u32[]{:S(2)}, u32[]{:S(2)}) collective-permute-start(bf16[64,2048]{1,0:T(8,128)(2,1)} %slice.3), channel_id=1, source_target_pairs={{0,16},{4,20},{8,24},{12,28},{16,0},{20,4},{24,8},{28,12},{1,17},{... | collective-permute-start | bytes 786440 | tf_op jit(solution)/shard_map/ppermute | solution.py:462
  13.4 19.5 %collective-permute-start.3 = (bf16[16,64,1024]{2,1,0:T(8,128)(2,1)}, bf16[16,64,1024]{2,1,0:T(8,128)(2,1)}, u32[]{:S(2)}, u32[]{:S(2)}) collective-permute-start(bf16[16,64,1024]{2,1,0:T(8,128)(2,1)} %get-tuple-element.41), channel_id=1, source_target_pairs={{0,4},{4,0},{8,12},{12,8},{16,20},{20,16},{24,28},{28,24},{1,5},{5... | collective-permute-start | bytes 6291464 | tf_op jit(solution)/shard_map/ppermute | solution.py:462
  13.4 17.6 %collective-permute-start.5 = (bf16[8,64,512]{2,1,0:T(8,128)(2,1)}, bf16[8,64,512]{2,1,0:T(8,128)(2,1)}, u32[]{:S(2)}, u32[]{:S(2)}) collective-permute-start(bf16[8,64,512]{2,1,0:T(8,128)(2,1)} %get-tuple-element.45), channel_id=1, source_target_pairs={{0,28},{4,8},{8,4},{12,16},{16,12},{20,24},{24,20},{28,0},{1,29},{... | collective-permute-start | bytes 1572872 | tf_op jit(solution)/shard_map/ppermute | solution.py:462
  15.0 27.1 %collective-permute-start.4 = (bf16[8,64,512]{2,1,0:T(8,128)(2,1)}, bf16[8,64,512]{2,1,0:T(8,128)(2,1)}, u32[]{:S(2)}, u32[]{:S(2)}) collective-permute-start(bf16[8,64,512]{2,1,0:T(8,128)(2,1)} %get-tuple-element.43), channel_id=1, source_target_pairs={{0,28},{4,8},{8,4},{12,16},{16,12},{20,24},{24,20},{28,0},{1,29},{... | collective-permute-start | bytes 1572872 | tf_op jit(solution)/shard_map/ppermute | solution.py:462
  16.0 16.9 %collective-permute-start.6 = (bf16[64,2048]{1,0:T(8,128)(2,1)}, bf16[64,2048]{1,0:T(8,128)(2,1)}, u32[]{:S(2)}, u32[]{:S(2)}) collective-permute-start(bf16[64,2048]{1,0:T(8,128)(2,1)} %collective-permute-done.refs_2_), channel_id=1, source_target_pairs={{0,16},{4,20},{8,24},{12,28},{16,0},{20,4},{24,8},{28,12},{1,17},{... | collective-permute-start | bytes 786440 | tf_op jit(solution)/shard_map/ppermute | solution.py:462
  17.5 23.1 %collective-permute-start.9 = (bf16[64,2048]{1,0:T(8,128)(2,1)}, bf16[64,2048]{1,0:T(8,128)(2,1)}, u32[]{:S(2)}, u32[]{:S(2)}) collective-permute-start(bf16[64,2048]{1,0:T(8,128)(2,1)} %get-tuple-element.51.rest_0_), channel_id=1, source_target_pairs={{0,16},{4,20},{8,24},{12,28},{16,0},{20,4},{24,8},{28,12},{1,17},{... | collective-permute-start | bytes 786440 | tf_op jit(solution)/shard_map/ppermute | solution.py:462
  31.0 13.6 %collective-permute-start.8 = (bf16[8,64,512]{2,1,0:T(8,128)(2,1)}, bf16[8,64,512]{2,1,0:T(8,128)(2,1)}, u32[]{:S(2)}, u32[]{:S(2)}) collective-permute-start(bf16[8,64,512]{2,1,0:T(8,128)(2,1)} %collective-permute-done.5.far_own), channel_id=1, source_target_pairs={{0,1},{1,0},{2,3},{3,2},{4,5},{5,4},{6,7},{7,6},{8,9},{9,8},{10,11... | collective-permute-start | bytes 1572872 | tf_op jit(solution)/shard_map/ppermute | solution.py:462
  40.7 13.0 %collective-permute-start.13 = (bf16[128,2048]{1,0:T(8,128)(2,1)}, bf16[128,2048]{1,0:T(8,128)(2,1)}, u32[]{:S(2)}, u32[]{:S(2)}) collective-permute-start(bf16[128,2048]{1,0:T(8,128)(2,1)} %get-tuple-element.58), channel_id=1, source_target_pairs={{0,16},{4,20},{8,24},{12,28},{16,0},{20,4},{24,8},{28,12},{1,17},{... | collective-permute-start | bytes 1572872 | tf_op jit(solution)/shard_map/ppermute | solution.py:462
  42.1 13.4 %collective-permute-start.12 = (bf16[128,2048]{1,0:T(8,128)(2,1)}, bf16[128,2048]{1,0:T(8,128)(2,1)}, u32[]{:S(2)}, u32[]{:S(2)}) collective-permute-start(bf16[128,2048]{1,0:T(8,128)(2,1)} %get-tuple-element.58), channel_id=1, source_target_pairs={{0,8},{4,12},{8,0},{12,4},{16,24},{20,28},{24,16},{28,20},{1,9},{5... | collective-permute-start | bytes 1572872 | tf_op jit(solution)/shard_map/ppermute | solution.py:462
  43.0 14.2 %collective-permute-start.7 = (bf16[8,64,512]{2,1,0:T(8,128)(2,1)}, bf16[8,64,512]{2,1,0:T(8,128)(2,1)}, u32[]{:S(2)}, u32[]{:S(2)}) collective-permute-start(bf16[8,64,512]{2,1,0:T(8,128)(2,1)} %collective-permute-done.4.far_own), channel_id=1, source_target_pairs={{0,1},{1,0},{2,3},{3,2},{4,5},{5,4},{6,7},{7,6},{8,9},{9,8},{10,11... | collective-permute-start | bytes 1572872 | tf_op jit(solution)/shard_map/ppermute | solution.py:462
  44.6 12.6 %collective-permute-start.10 = (bf16[64,2048]{1,0:T(8,128)(2,1)}, bf16[64,2048]{1,0:T(8,128)(2,1)}, u32[]{:S(2)}, u32[]{:S(2)}) collective-permute-start(bf16[64,2048]{1,0:T(8,128)(2,1)} %collective-permute-done.refs_2_), channel_id=1, source_target_pairs={{0,4},{4,0},{8,12},{12,8},{16,20},{20,16},{24,28},{28,24},{1,5},{5... | collective-permute-start | bytes 786440 | tf_op jit(solution)/shard_map/ppermute | solution.py:462
  44.6 13.1 %collective-permute-start.11 = (bf16[64,2048]{1,0:T(8,128)(2,1)}, bf16[64,2048]{1,0:T(8,128)(2,1)}, u32[]{:S(2)}, u32[]{:S(2)}) collective-permute-start(bf16[64,2048]{1,0:T(8,128)(2,1)} %collective-permute-done.1.refs_4_), channel_id=1, source_target_pairs={{0,4},{4,0},{8,12},{12,8},{16,20},{20,16},{24,28},{28,24},{1,5},{5... | collective-permute-start | bytes 786440 | tf_op jit(solution)/shard_map/ppermute | solution.py:462
  53.7 4.3 %collective-permute-start.16 = (bf16[64,2048]{1,0:T(8,128)(2,1)}, bf16[64,2048]{1,0:T(8,128)(2,1)}, u32[]{:S(2)}, u32[]{:S(2)}) collective-permute-start(bf16[64,2048]{1,0:T(8,128)(2,1)} %collective-permute-done.9.rest_1_.refs_10_), channel_id=1, source_target_pairs={{0,4},{4,0},{8,12},{12,8},{16,20},{20,16},{24,28},{28,24},{1,5},{5... | collective-permute-start | bytes 786440 | tf_op jit(solution)/shard_map/ppermute | solution.py:462
  55.5 13.3 %collective-permute-start.20 = (bf16[128,2048]{1,0:T(8,128)(2,1)}, bf16[128,2048]{1,0:T(8,128)(2,1)}, u32[]{:S(2)}, u32[]{:S(2)}) collective-permute-start(bf16[128,2048]{1,0:T(8,128)(2,1)} %get-tuple-element.65), channel_id=1, source_target_pairs={{0,8},{4,12},{8,0},{12,4},{16,24},{20,28},{24,16},{28,20},{1,9},{5... | collective-permute-start | bytes 1572872 | tf_op jit(solution)/shard_map/ppermute | solution.py:462
  57.2 11.6 %collective-permute-start.14 = (bf16[128,2048]{1,0:T(8,128)(2,1)}, bf16[128,2048]{1,0:T(8,128)(2,1)}, u32[]{:S(2)}, u32[]{:S(2)}) collective-permute-start(bf16[128,2048]{1,0:T(8,128)(2,1)} %collective-permute-done.12.refs_6_), channel_id=1, source_target_pairs={{0,4},{4,0},{8,12},{12,8},{16,20},{20,16},{24,28},{28,24},{1,5},{5... | collective-permute-start | bytes 1572872 | tf_op jit(solution)/shard_map/ppermute | solution.py:462
  57.2 11.6 %collective-permute-start.17 = (bf16[128,2048]{1,0:T(8,128)(2,1)}, bf16[128,2048]{1,0:T(8,128)(2,1)}, u32[]{:S(2)}, u32[]{:S(2)}) collective-permute-start(bf16[128,2048]{1,0:T(8,128)(2,1)} %collective-permute-done.13.refs_12_), channel_id=1, source_target_pairs={{0,4},{4,0},{8,12},{12,8},{16,20},{20,16},{24,28},{28,24},{1,5},{5... | collective-permute-start | bytes 1572872 | tf_op jit(solution)/shard_map/ppermute | solution.py:462
  57.7 14.2 %collective-permute-start.18 = (bf16[128,2048]{1,0:T(8,128)(2,1)}, bf16[128,2048]{1,0:T(8,128)(2,1)}, u32[]{:S(2)}, u32[]{:S(2)}) collective-permute-start(bf16[128,2048]{1,0:T(8,128)(2,1)} %collective-permute-done.12.refs_6_), channel_id=1, source_target_pairs={{0,16},{4,20},{8,24},{12,28},{16,0},{20,4},{24,8},{28,12},{1,17},{... | collective-permute-start | bytes 1572872 | tf_op jit(solution)/shard_map/ppermute | solution.py:462
  58.0 10.8 %collective-permute-start.15 = (bf16[64,2048]{1,0:T(8,128)(2,1)}, bf16[64,2048]{1,0:T(8,128)(2,1)}, u32[]{:S(2)}, u32[]{:S(2)}) collective-permute-start(bf16[64,2048]{1,0:T(8,128)(2,1)} %collective-permute-done.6.refs_8_), channel_id=1, source_target_pairs={{0,4},{4,0},{8,12},{12,8},{16,20},{20,16},{24,28},{28,24},{1,5},{5... | collective-permute-start | bytes 786440 | tf_op jit(solution)/shard_map/ppermute | solution.py:462
  68.8 3.1 %collective-permute-start.21 = (bf16[128,2048]{1,0:T(8,128)(2,1)}, bf16[128,2048]{1,0:T(8,128)(2,1)}, u32[]{:S(2)}, u32[]{:S(2)}) collective-permute-start(bf16[128,2048]{1,0:T(8,128)(2,1)} %collective-permute-done.20.refs_16_), channel_id=1, source_target_pairs={{0,4},{4,0},{8,12},{12,8},{16,20},{20,16},{24,28},{28,24},{1,5},{5... | collective-permute-start | bytes 1572872 | tf_op jit(solution)/shard_map/ppermute | solution.py:462
  71.9 2.3 %collective-permute-start.19 = (bf16[128,2048]{1,0:T(8,128)(2,1)}, bf16[128,2048]{1,0:T(8,128)(2,1)}, u32[]{:S(2)}, u32[]{:S(2)}) collective-permute-start(bf16[128,2048]{1,0:T(8,128)(2,1)} %collective-permute-done.18.refs_14_), channel_id=1, source_target_pairs={{0,4},{4,0},{8,12},{12,8},{16,20},{20,16},{24,28},{28,24},{1,5},{5... | collective-permute-start | bytes 1572872 | tf_op jit(solution)/shard_map/ppermute | solution.py:462

commit v5 on v4

--- a/solution.py
+++ b/solution.py
@@ -635,15 +635,16 @@
     for k in hops:
         here = after(middles[k], ahead)
         both_cores(k, quarter, here)
-        both_cores(k + far_hop, 0, after(relays[k], ahead))
         late.append((k + far_hop, quarter, send(after(middles[k], first_heads), "req", flip(far_hop))))
         both = send(joined, "req", flip(k))
         late.append(((k, k + far_hop), 3 * quarter, both))
     both_cores(far_hop, 3 * quarter, lasts[far_hop])
-    both_cores(far_hop, quarter, after(middles[far_hop], ahead))
     for g in range(1, KVH):
         attended.append(attend(g, attended[-1]))
     earlier = [attended[-1], *swapped, *shared]
+    for k in hops:
+        both_cores(k + far_hop, 0, after(relays[k], attended[-1]))
+    both_cores(far_hop, quarter, after(middles[far_hop], attended[-1]))
     for k, offset, block in late:
         both_cores(k, offset, after(block, *earlier))
 

time: 85.5 us -> 82.5 us (0.965)
  starting transfers between devices: 18 us -> 16.2 us
  waiting for transfers between devices: 11.6 us -> 10.4 us
    ppermute x22, starting transfers between devices: 18 us -> 16.2 us  [send(): return lax.ppermute(block, axis, pairs)]
    ppermute x22, waiting for transfers between devices: 11.6 us -> 10.4 us  [send(): return lax.ppermute(block, axis, pairs)]
  transfers between devices with their start and end apart: 22 -> 22, of which waited for: 6 -> 7; matrix products, arithmetic and copies ran while one was open for 2% -> 2% of each run, Pallas kernels for 50% -> 52%
where the time goes in v5:
time: 82.5 us; the launch traced here: 82 us
  Pallas kernels  53.4 us (65%)
  starting transfers between devices  16.2 us (20%)
  waiting for transfers between devices  10.4 us (13%)
  local copies, waits for them, and re-layouts  1.67 us (2%)
    ppermute x22, starting transfers between devices, send(): return lax.ppermute(block, axis, pairs)  16.2 us
    pallas_call x2, Pallas kernels, attend(): pl.pallas_call(functools.partial(attention_kernel, g), out_shape=(heads_s...  16 us
    pallas_call x1, Pallas kernels, shards(): pl.pallas_call(qkv_kernel, out_shape=(heads_shape(NH), heads_shape(KVH),...  12.9 us
    pallas_call x1, Pallas kernels, shards(): pl.pallas_call(functools.partial(output_kernel, places), out_shape=jax.Sh...  10.7 us
    ppermute x22, waiting for transfers between devices, send(): return lax.ppermute(block, axis, pairs)  10.4 us
    pallas_call x1, Pallas kernels, shards(): pl.pallas_call(residual_kernel, out_shape=jax.ShapeDtypeStruct((rows, wid...  7.74 us
    pallas_call x1, Pallas kernels, shards(): pl.pallas_call(pages_kernel, out_shape=(jax.ShapeDtypeStruct(near_shape,...  6.1 us
    slice x1, local copies, waits for them, and re-layouts, shards(): top = w_output[:w_output.shape[0] // 4]  1.67 us
  transfers between devices with their start and end apart: 22, of which 7 were waited for; matrix products, arithmetic and copies ran while one was open for 2% of the time, Pallas kernels for 52%

profile of v5, /device:TPU:0, one launch (start us, length us, event | category | flops | bytes accessed | tf_op | source)
XLA Modules:
  0.0 82.0 jit_solution(9619203721882869249)
XLA Ops:
  0.0 0.5 collective-permute-start.2
  0.5 1.7 %slice.3 = bf16[64,2048]{1,0:T(8,128)(2,1)} slice(bf16[256,2048]{1,0:T(8,128)(2,1)} %refs_0_.1), slice={[0:64], [0:2048]} | slice | bytes 524288 | tf_op jit(solution)/shard_map/slice | solution.py:472
  2.1 2.5 %collective-permute-start = (bf16[64,2048]{1,0:T(8,128)(2,1)}, bf16[64,2048]{1,0:T(8,128)(2,1)}, u32[]{:S(2)}, u32[]{:S(2)}) collective-permute-start(bf16[64,2048]{1,0:T(8,128)(2,1)} %slice.3), channel_id=1, source_target_pairs={{0,8},{4,12},{8,0},{12,4},{16,24},{20,28},{24,16},{28,20},{1,9},{5... | collective-permute-start | bytes 786440 | tf_op jit(solution)/shard_map/ppermute | solution.py:462
  4.6 1.5 %collective-permute-start.1 = (bf16[64,2048]{1,0:T(8,128)(2,1)}, bf16[64,2048]{1,0:T(8,128)(2,1)}, u32[]{:S(2)}, u32[]{:S(2)}) collective-permute-start(bf16[64,2048]{1,0:T(8,128)(2,1)} %slice.3), channel_id=1, source_target_pairs={{0,16},{4,20},{8,24},{12,28},{16,0},{20,4},{24,8},{28,12},{1,17},{... | collective-permute-start | bytes 786440 | tf_op jit(solution)/shard_map/ppermute | solution.py:462
  6.1 6.1 %pages.1 = (bf16[16,64,1024]{2,1,0:T(8,128)(2,1)}, bf16[8,64,512]{2,1,0:T(8,128)(2,1)}, bf16[8,64,512]{2,1,0:T(8,128)(2,1)}, bf16[128,2048]{1,0:T(8,128)(2,1)}, bf16[64,2048]{1,0:T(8,128)(2,1)}) custom-call(s32[32]{0:T(128)} %slot_of.6, s32[16,32]{1,0:T(8,128)} %bitcast.8, bf16[64,64,1024]{2,1,0:T(8,128)(2,1)} %pool.5, bf16[256,2048]{1,0:T(8,128)(2,1)} %refs_0_.1), custom_call_target="tpu_custom_call" | custom-call | flops 1 | bytes 1 | tf_op jit(solution)/shard_map/pages/pallas_call | solution.py:486
  12.2 1.1 %collective-permute-done.1.refs_4_ = bf16[64,2048]{1,0:T(8,128)(2,1)} collective-permute-done((bf16[64,2048]{1,0:T(8,128)(2,1)}, bf16[64,2048]{1,0:T(8,128)(2,1)}, u32[]{:S(2)}, u32[]{:S(2)}) %collective-permute-start.1) | collective-permute-done | bytes 262176 | tf_op jit(solution)/shard_map/ppermute | solution.py:462
  13.4 1.6 %collective-permute-start.5 = (bf16[8,64,512]{2,1,0:T(8,128)(2,1)}, bf16[8,64,512]{2,1,0:T(8,128)(2,1)}, u32[]{:S(2)}, u32[]{:S(2)}) collective-permute-start(bf16[8,64,512]{2,1,0:T(8,128)(2,1)} %get-tuple-element.43), channel_id=1, source_target_pairs={{0,28},{4,8},{8,4},{12,16},{16,12},{20,24},{24,20},{28,0},{1,29},{... | collective-permute-start | bytes 1572872 | tf_op jit(solution)/shard_map/ppermute | solution.py:462
  15.0 1.0 %collective-permute-start.4 = (bf16[8,64,512]{2,1,0:T(8,128)(2,1)}, bf16[8,64,512]{2,1,0:T(8,128)(2,1)}, u32[]{:S(2)}, u32[]{:S(2)}) collective-permute-start(bf16[8,64,512]{2,1,0:T(8,128)(2,1)} %get-tuple-element.41), channel_id=1, source_target_pairs={{0,28},{4,8},{8,4},{12,16},{16,12},{20,24},{24,20},{28,0},{1,29},{... | collective-permute-start | bytes 1572872 | tf_op jit(solution)/shard_map/ppermute | solution.py:462
  16.0 1.5 %collective-permute-start.6 = (bf16[64,2048]{1,0:T(8,128)(2,1)}, bf16[64,2048]{1,0:T(8,128)(2,1)}, u32[]{:S(2)}, u32[]{:S(2)}) collective-permute-start(bf16[64,2048]{1,0:T(8,128)(2,1)} %collective-permute-done.refs_2_), channel_id=1, source_target_pairs={{0,16},{4,20},{8,24},{12,28},{16,0},{20,4},{24,8},{28,12},{1,17},{... | collective-permute-start | bytes 786440 | tf_op jit(solution)/shard_map/ppermute | solution.py:462
  17.5 12.9 %qkv.1 = (bf16[8,512,256]{2,1,0:T(8,128)(2,1)}, bf16[2,512,256]{2,1,0:T(8,128)(2,1)}, bf16[2,512,256]{2,1,0:T(8,128)(2,1)}) custom-call(s32[32]{0:T(128)} %slot_of.6, s32[32]{0:T(128)} %cached_len.5, f32[1,2048]{1,0:T(1,128)} %bitcast.11, f32[1,256]{1,0:T(1,128)} %bitcast.15, f32[1,256]{1,0:T(1,128)} %bitcast.16, bf16[512,2048]{1,0:T(8,128)(2,1)} %tokens_in.2, ...), custom_call_target="tpu_custom_call" | custom-call | flops 1 | bytes 1 | tf_op jit(solution)/shard_map/qkv/pallas_call | solution.py:518
  30.5 0.6 collective-permute-start.9
  31.1 1.6 %collective-permute-start.8 = (bf16[8,64,512]{2,1,0:T(8,128)(2,1)}, bf16[8,64,512]{2,1,0:T(8,128)(2,1)}, u32[]{:S(2)}, u32[]{:S(2)}) collective-permute-start(bf16[8,64,512]{2,1,0:T(8,128)(2,1)} %collective-permute-done.5.far_own), channel_id=1, source_target_pairs={{0,1},{1,0},{2,3},{3,2},{4,5},{5,4},{6,7},{7,6},{8,9},{9,8},{10,11... | collective-permute-start | bytes 1572872 | tf_op jit(solution)/shard_map/ppermute | solution.py:462
  32.6 7.7 %residual.1.residual_in = f32[512,2048]{1,0:T(8,128)} custom-call(f32[1,2048]{1,0:T(1,128)} %bitcast.12, bf16[64,2048]{1,0:T(8,128)(2,1)} %bitcast.7, bf16[64,2048]{1,0:T(8,128)(2,1)} %right.1, f32[1,2048]{1,0:T(1,128)} %bitcast.13, bf16[512,2048]{1,0:T(8,128)(2,1)} %tokens_in.2), custom_call_target="tpu_custom_call" | custom-call | flops 1 | bytes 1 | tf_op jit(solution)/shard_map/residual/pallas_call | solution.py:548
  40.4 0.1 collective-permute-start.12
  40.5 0.5 collective-permute-start.7
  41.0 0.7 collective-permute-done.9.rest_1_.refs_8_
  41.7 1.4 %collective-permute-start.16 = (bf16[128,2048]{1,0:T(8,128)(2,1)}, bf16[128,2048]{1,0:T(8,128)(2,1)}, u32[]{:S(2)}, u32[]{:S(2)}) collective-permute-start(bf16[128,2048]{1,0:T(8,128)(2,1)} %get-tuple-element.57), channel_id=1, source_target_pairs={{0,16},{4,20},{8,24},{12,28},{16,0},{20,4},{24,8},{28,12},{1,17},{... | collective-permute-start | bytes 1572872 | tf_op jit(solution)/shard_map/ppermute | solution.py:462
  43.0 2.1 %collective-permute-done.8.far_other = bf16[8,64,512]{2,1,0:T(8,128)(2,1)} collective-permute-done((bf16[8,64,512]{2,1,0:T(8,128)(2,1)}, bf16[8,64,512]{2,1,0:T(8,128)(2,1)}, u32[]{:S(2)}, u32[]{:S(2)}) %collective-permute-start.8) | collective-permute-done | bytes 524320 | tf_op jit(solution)/shard_map/ppermute | solution.py:462
  45.1 8.0 %attention.2 = (bf16[8,512,256]{2,1,0:T(8,128)(2,1)}, bf16[128,2048]{1,0:T(8,128)(2,1)}) custom-call(s32[32]{0:T(128)} %slot_of.6, s32[32]{0:T(128)} %cached_len.5, s32[16,32]{1,0:T(8,128)} %bitcast.9, bf16[8,512,256]{2,1,0:T(8,128)(2,1)} %get-tuple-element.34.query_in, bf16[2,512,256]{2,1,0:T(8,128)(2,1)} %get-tuple-element.35.key_in, ...), custom_call_target="tpu_custom_call" | custom-call | flops 1 | bytes 1 | tf_op jit(solution)/shard_map/attention/pallas_call | solution.py:589
  53.1 0.7 collective-permute-start.20
  53.8 1.6 %collective-permute-start.18 = (bf16[128,2048]{1,0:T(8,128)(2,1)}, bf16[128,2048]{1,0:T(8,128)(2,1)}, u32[]{:S(2)}, u32[]{:S(2)}) collective-permute-start(bf16[128,2048]{1,0:T(8,128)(2,1)} %collective-permute-done.12.refs_6_), channel_id=1, source_target_pairs={{0,16},{4,20},{8,24},{12,28},{16,0},{20,4},{24,8},{28,12},{1,17},{... | collective-permute-start | bytes 1572872 | tf_op jit(solution)/shard_map/ppermute | solution.py:462
  55.4 0.0 collective-permute-done.7.far_other
  55.5 0.1 collective-permute-start.11
  55.6 0.1 collective-permute-done.16.refs_12_
  55.7 0.2 collective-permute-start.14
  56.0 8.0 %attention.3.attended = bf16[8,512,256]{2,1,0:T(8,128)(2,1)} custom-call(s32[32]{0:T(128)} %slot_of.6, s32[32]{0:T(128)} %cached_len.5, s32[16,32]{1,0:T(8,128)} %bitcast.10, bf16[8,512,256]{2,1,0:T(8,128)(2,1)} %get-tuple-element.34.query_in, bf16[2,512,256]{2,1,0:T(8,128)(2,1)} %get-tuple-element.35.key_in, ...), custom_call_target="tpu_custom_call", output_to_operand_aliasing={{}: (10, {})} | custom-call | flops 1 | bytes 1 | tf_op jit(solution)/shard_map/attention/pallas_call | solution.py:589
  64.0 0.3 collective-permute-start.17
  64.3 1.7 %collective-permute-done.20.refs_16_ = bf16[128,2048]{1,0:T(8,128)(2,1)} collective-permute-done((bf16[128,2048]{1,0:T(8,128)(2,1)}, bf16[128,2048]{1,0:T(8,128)(2,1)}, u32[]{:S(2)}, u32[]{:S(2)}) %collective-permute-start.20) | collective-permute-done | bytes 524320 | tf_op jit(solution)/shard_map/ppermute | solution.py:462
  66.0 2.5 %collective-permute-done.18.refs_14_ = bf16[128,2048]{1,0:T(8,128)(2,1)} collective-permute-done((bf16[128,2048]{1,0:T(8,128)(2,1)}, bf16[128,2048]{1,0:T(8,128)(2,1)}, u32[]{:S(2)}, u32[]{:S(2)}) %collective-permute-start.18) | collective-permute-done | bytes 524320 | tf_op jit(solution)/shard_map/ppermute | solution.py:462
  68.5 0.5 collective-permute-start.15
  69.0 2.1 %collective-permute-done.15.refs_11_ = bf16[64,2048]{1,0:T(8,128)(2,1)} collective-permute-done((bf16[64,2048]{1,0:T(8,128)(2,1)}, bf16[64,2048]{1,0:T(8,128)(2,1)}, u32[]{:S(2)}, u32[]{:S(2)}) %collective-permute-start.15) | collective-permute-done | bytes 262176 | tf_op jit(solution)/shard_map/ppermute | solution.py:462
  71.1 10.7 %project.1 = bf16[512,2048]{1,0:T(8,128)(2,1)} custom-call(f32[1,2048]{1,0:T(1,128)} %bitcast.14, bf16[8,512,256]{2,1,0:T(8,128)(2,1)} %attention.3.attended, f32[512,2048]{1,0:T(8,128)} %residual.1.residual_in, bf16[256,2048]{1,0:T(8,128)(2,1)} %refs_0_.1, bf16[256,2048]{1,0:T(8,128)(2,1)} %collective-permute-done.2.refs_1_, ...), custom_call_target="tpu_custom_call" | custom-call | flops 1 | bytes 1 | tf_op jit(solution)/shard_map/project/pallas_call | solution.py:657
  (19 shorter events, 0.1 us)
Async XLA Ops:
  0.0 13.4 %collective-permute-start.2 = (bf16[256,2048]{1,0:T(8,128)(2,1)}, bf16[256,2048]{1,0:T(8,128)(2,1)}, u32[]{:S(2)}, u32[]{:S(2)}) collective-permute-start(bf16[256,2048]{1,0:T(8,128)(2,1)} %refs_0_.1), channel_id=1, source_target_pairs={{0,4},{4,0},{8,12},{12,8},{16,20},{20,16},{24,28},{28,24},{1,5},{5... | collective-permute-start | bytes 3145736 | tf_op jit(solution)/shard_map/ppermute | solution.py:462
  2.1 10.1 %collective-permute-start = (bf16[64,2048]{1,0:T(8,128)(2,1)}, bf16[64,2048]{1,0:T(8,128)(2,1)}, u32[]{:S(2)}, u32[]{:S(2)}) collective-permute-start(bf16[64,2048]{1,0:T(8,128)(2,1)} %slice.3), channel_id=1, source_target_pairs={{0,8},{4,12},{8,0},{12,4},{16,24},{20,28},{24,16},{28,20},{1,9},{5... | collective-permute-start | bytes 786440 | tf_op jit(solution)/shard_map/ppermute | solution.py:462
  4.6 8.8 %collective-permute-start.1 = (bf16[64,2048]{1,0:T(8,128)(2,1)}, bf16[64,2048]{1,0:T(8,128)(2,1)}, u32[]{:S(2)}, u32[]{:S(2)}) collective-permute-start(bf16[64,2048]{1,0:T(8,128)(2,1)} %slice.3), channel_id=1, source_target_pairs={{0,16},{4,20},{8,24},{12,28},{16,0},{20,4},{24,8},{28,12},{1,17},{... | collective-permute-start | bytes 786440 | tf_op jit(solution)/shard_map/ppermute | solution.py:462
  13.4 19.3 %collective-permute-start.3 = (bf16[16,64,1024]{2,1,0:T(8,128)(2,1)}, bf16[16,64,1024]{2,1,0:T(8,128)(2,1)}, u32[]{:S(2)}, u32[]{:S(2)}) collective-permute-start(bf16[16,64,1024]{2,1,0:T(8,128)(2,1)} %get-tuple-element.39), channel_id=1, source_target_pairs={{0,4},{4,0},{8,12},{12,8},{16,20},{20,16},{24,28},{28,24},{1,5},{5... | collective-permute-start | bytes 6291464 | tf_op jit(solution)/shard_map/ppermute | solution.py:462
  13.4 17.7 %collective-permute-start.5 = (bf16[8,64,512]{2,1,0:T(8,128)(2,1)}, bf16[8,64,512]{2,1,0:T(8,128)(2,1)}, u32[]{:S(2)}, u32[]{:S(2)}) collective-permute-start(bf16[8,64,512]{2,1,0:T(8,128)(2,1)} %get-tuple-element.43), channel_id=1, source_target_pairs={{0,28},{4,8},{8,4},{12,16},{16,12},{20,24},{24,20},{28,0},{1,29},{... | collective-permute-start | bytes 1572872 | tf_op jit(solution)/shard_map/ppermute | solution.py:462
  15.0 25.4 %collective-permute-start.4 = (bf16[8,64,512]{2,1,0:T(8,128)(2,1)}, bf16[8,64,512]{2,1,0:T(8,128)(2,1)}, u32[]{:S(2)}, u32[]{:S(2)}) collective-permute-start(bf16[8,64,512]{2,1,0:T(8,128)(2,1)} %get-tuple-element.41), channel_id=1, source_target_pairs={{0,28},{4,8},{8,4},{12,16},{16,12},{20,24},{24,20},{28,0},{1,29},{... | collective-permute-start | bytes 1572872 | tf_op jit(solution)/shard_map/ppermute | solution.py:462
  16.0 16.6 %collective-permute-start.6 = (bf16[64,2048]{1,0:T(8,128)(2,1)}, bf16[64,2048]{1,0:T(8,128)(2,1)}, u32[]{:S(2)}, u32[]{:S(2)}) collective-permute-start(bf16[64,2048]{1,0:T(8,128)(2,1)} %collective-permute-done.refs_2_), channel_id=1, source_target_pairs={{0,16},{4,20},{8,24},{12,28},{16,0},{20,4},{24,8},{28,12},{1,17},{... | collective-permute-start | bytes 786440 | tf_op jit(solution)/shard_map/ppermute | solution.py:462
  30.5 11.2 %collective-permute-start.9 = (bf16[64,2048]{1,0:T(8,128)(2,1)}, bf16[64,2048]{1,0:T(8,128)(2,1)}, u32[]{:S(2)}, u32[]{:S(2)}) collective-permute-start(bf16[64,2048]{1,0:T(8,128)(2,1)} %get-tuple-element.49.rest_0_), channel_id=1, source_target_pairs={{0,16},{4,20},{8,24},{12,28},{16,0},{20,4},{24,8},{28,12},{1,17},{... | collective-permute-start | bytes 786440 | tf_op jit(solution)/shard_map/ppermute | solution.py:462
  31.1 14.1 %collective-permute-start.8 = (bf16[8,64,512]{2,1,0:T(8,128)(2,1)}, bf16[8,64,512]{2,1,0:T(8,128)(2,1)}, u32[]{:S(2)}, u32[]{:S(2)}) collective-permute-start(bf16[8,64,512]{2,1,0:T(8,128)(2,1)} %collective-permute-done.5.far_own), channel_id=1, source_target_pairs={{0,1},{1,0},{2,3},{3,2},{4,5},{5,4},{6,7},{7,6},{8,9},{9,8},{10,11... | collective-permute-start | bytes 1572872 | tf_op jit(solution)/shard_map/ppermute | solution.py:462
  40.4 13.4 %collective-permute-start.12 = (bf16[128,2048]{1,0:T(8,128)(2,1)}, bf16[128,2048]{1,0:T(8,128)(2,1)}, u32[]{:S(2)}, u32[]{:S(2)}) collective-permute-start(bf16[128,2048]{1,0:T(8,128)(2,1)} %get-tuple-element.57), channel_id=1, source_target_pairs={{0,8},{4,12},{8,0},{12,4},{16,24},{20,28},{24,16},{28,20},{1,9},{5... | collective-permute-start | bytes 1572872 | tf_op jit(solution)/shard_map/ppermute | solution.py:462
  40.5 15.0 %collective-permute-start.7 = (bf16[8,64,512]{2,1,0:T(8,128)(2,1)}, bf16[8,64,512]{2,1,0:T(8,128)(2,1)}, u32[]{:S(2)}, u32[]{:S(2)}) collective-permute-start(bf16[8,64,512]{2,1,0:T(8,128)(2,1)} %collective-permute-done.4.far_own), channel_id=1, source_target_pairs={{0,1},{1,0},{2,3},{3,2},{4,5},{5,4},{6,7},{7,6},{8,9},{9,8},{10,11... | collective-permute-start | bytes 1572872 | tf_op jit(solution)/shard_map/ppermute | solution.py:462
  41.7 14.1 %collective-permute-start.16 = (bf16[128,2048]{1,0:T(8,128)(2,1)}, bf16[128,2048]{1,0:T(8,128)(2,1)}, u32[]{:S(2)}, u32[]{:S(2)}) collective-permute-start(bf16[128,2048]{1,0:T(8,128)(2,1)} %get-tuple-element.57), channel_id=1, source_target_pairs={{0,16},{4,20},{8,24},{12,28},{16,0},{20,4},{24,8},{28,12},{1,17},{... | collective-permute-start | bytes 1572872 | tf_op jit(solution)/shard_map/ppermute | solution.py:462
  43.0 10.8 %collective-permute-start.10 = (bf16[64,2048]{1,0:T(8,128)(2,1)}, bf16[64,2048]{1,0:T(8,128)(2,1)}, u32[]{:S(2)}, u32[]{:S(2)}) collective-permute-start(bf16[64,2048]{1,0:T(8,128)(2,1)} %collective-permute-done.refs_2_), channel_id=1, source_target_pairs={{0,4},{4,0},{8,12},{12,8},{16,20},{20,16},{24,28},{28,24},{1,5},{5... | collective-permute-start | bytes 786440 | tf_op jit(solution)/shard_map/ppermute | solution.py:462
  53.1 12.9 %collective-permute-start.20 = (bf16[128,2048]{1,0:T(8,128)(2,1)}, bf16[128,2048]{1,0:T(8,128)(2,1)}, u32[]{:S(2)}, u32[]{:S(2)}) collective-permute-start(bf16[128,2048]{1,0:T(8,128)(2,1)} %get-tuple-element.61), channel_id=1, source_target_pairs={{0,8},{4,12},{8,0},{12,4},{16,24},{20,28},{24,16},{28,20},{1,9},{5... | collective-permute-start | bytes 1572872 | tf_op jit(solution)/shard_map/ppermute | solution.py:462
  53.8 12.2 %collective-permute-start.13 = (bf16[128,2048]{1,0:T(8,128)(2,1)}, bf16[128,2048]{1,0:T(8,128)(2,1)}, u32[]{:S(2)}, u32[]{:S(2)}) collective-permute-start(bf16[128,2048]{1,0:T(8,128)(2,1)} %collective-permute-done.12.refs_6_), channel_id=1, source_target_pairs={{0,4},{4,0},{8,12},{12,8},{16,20},{20,16},{24,28},{28,24},{1,5},{5... | collective-permute-start | bytes 1572872 | tf_op jit(solution)/shard_map/ppermute | solution.py:462
  53.8 14.7 %collective-permute-start.18 = (bf16[128,2048]{1,0:T(8,128)(2,1)}, bf16[128,2048]{1,0:T(8,128)(2,1)}, u32[]{:S(2)}, u32[]{:S(2)}) collective-permute-start(bf16[128,2048]{1,0:T(8,128)(2,1)} %collective-permute-done.12.refs_6_), channel_id=1, source_target_pairs={{0,16},{4,20},{8,24},{12,28},{16,0},{20,4},{24,8},{28,12},{1,17},{... | collective-permute-start | bytes 1572872 | tf_op jit(solution)/shard_map/ppermute | solution.py:462
  55.5 8.5 %collective-permute-start.11 = (bf16[64,2048]{1,0:T(8,128)(2,1)}, bf16[64,2048]{1,0:T(8,128)(2,1)}, u32[]{:S(2)}, u32[]{:S(2)}) collective-permute-start(bf16[64,2048]{1,0:T(8,128)(2,1)} %collective-permute-done.1.refs_4_), channel_id=1, source_target_pairs={{0,4},{4,0},{8,12},{12,8},{16,20},{20,16},{24,28},{28,24},{1,5},{5... | collective-permute-start | bytes 786440 | tf_op jit(solution)/shard_map/ppermute | solution.py:462
  55.7 8.6 %collective-permute-start.14 = (bf16[64,2048]{1,0:T(8,128)(2,1)}, bf16[64,2048]{1,0:T(8,128)(2,1)}, u32[]{:S(2)}, u32[]{:S(2)}) collective-permute-start(bf16[64,2048]{1,0:T(8,128)(2,1)} %collective-permute-done.9.rest_1_.refs_8_), channel_id=1, source_target_pairs={{0,4},{4,0},{8,12},{12,8},{16,20},{20,16},{24,28},{28,24},{1,5},{5... | collective-permute-start | bytes 786440 | tf_op jit(solution)/shard_map/ppermute | solution.py:462
  64.0 7.1 %collective-permute-start.17 = (bf16[128,2048]{1,0:T(8,128)(2,1)}, bf16[128,2048]{1,0:T(8,128)(2,1)}, u32[]{:S(2)}, u32[]{:S(2)}) collective-permute-start(bf16[128,2048]{1,0:T(8,128)(2,1)} %collective-permute-done.16.refs_12_), channel_id=1, source_target_pairs={{0,4},{4,0},{8,12},{12,8},{16,20},{20,16},{24,28},{28,24},{1,5},{5... | collective-permute-start | bytes 1572872 | tf_op jit(solution)/shard_map/ppermute | solution.py:462
  66.0 5.1 %collective-permute-start.21 = (bf16[128,2048]{1,0:T(8,128)(2,1)}, bf16[128,2048]{1,0:T(8,128)(2,1)}, u32[]{:S(2)}, u32[]{:S(2)}) collective-permute-start(bf16[128,2048]{1,0:T(8,128)(2,1)} %collective-permute-done.20.refs_16_), channel_id=1, source_target_pairs={{0,4},{4,0},{8,12},{12,8},{16,20},{20,16},{24,28},{28,24},{1,5},{5... | collective-permute-start | bytes 1572872 | tf_op jit(solution)/shard_map/ppermute | solution.py:462
  68.5 2.6 %collective-permute-start.19 = (bf16[128,2048]{1,0:T(8,128)(2,1)}, bf16[128,2048]{1,0:T(8,128)(2,1)}, u32[]{:S(2)}, u32[]{:S(2)}) collective-permute-start(bf16[128,2048]{1,0:T(8,128)(2,1)} %collective-permute-done.18.refs_14_), channel_id=1, source_target_pairs={{0,4},{4,0},{8,12},{12,8},{16,20},{20,16},{24,28},{28,24},{1,5},{5... | collective-permute-start | bytes 1572872 | tf_op jit(solution)/shard_map/ppermute | solution.py:462
  68.5 2.6 %collective-permute-start.15 = (bf16[64,2048]{1,0:T(8,128)(2,1)}, bf16[64,2048]{1,0:T(8,128)(2,1)}, u32[]{:S(2)}, u32[]{:S(2)}) collective-permute-start(bf16[64,2048]{1,0:T(8,128)(2,1)} %collective-permute-done.6.refs_10_), channel_id=1, source_target_pairs={{0,4},{4,0},{8,12},{12,8},{16,20},{20,16},{24,28},{28,24},{1,5},{5... | collective-permute-start | bytes 786440 | tf_op jit(solution)/shard_map/ppermute | solution.py:462
